TPU v7x, 32 devices: a whole 2x2x4 slice. The times are simulated.
32 devices in a mesh: clip: 4 (over y, core), seq: 8 (over z, x).
Axes of the slice: x: 2, y: 2, z: 4, core: 2. Of those that a mesh axis runs over, the one named last changes fastest.
Arguments:
- tokens: bfloat16 [4, 1024, 1536], P('clip', 'seq'), may hold values from -6 to 6
- caption: bfloat16 [4, 256, 4096], P('clip', 'seq'), may hold values from -6 to 6
- lengths: int32 [4], P('clip'), may hold values from 128 to 256, as said below
- timesteps: int32 [4], P('clip'), may hold values from 0 to 999
- positions: int32 [3, 4, 1024], P(None, 'clip', 'seq'), may hold values from 0 to 63
- w_time: bfloat16 [256, 1024], P(('clip', 'seq')), may hold values from -0.375 to 0.375
- w_pool: bfloat16 [4096, 1024], P(('clip', 'seq')), may hold values from -0.09375 to 0.09375
- w_ada: bfloat16 [1024, 6144], P(('clip', 'seq')), may hold values from -0.09375 to 0.09375
- b_ada: float32 [6144], replicated, may hold values from -2 to 2
- norm1_gain: float32 [1536], replicated, may hold values from 0.25 to 1.75
- w_qkv: bfloat16 [1536, 4608], P(('clip', 'seq')), may hold values from -0.15625 to 0.15625
- w_key_text: bfloat16 [4096, 1536], P(('clip', 'seq')), may hold values from -0.09375 to 0.09375
- w_value_text: bfloat16 [4096, 1536], P(('clip', 'seq')), may hold values from -0.09375 to 0.09375
- cross_gate: float32 [24], replicated, may hold values from 0.2 to 0.8
- w_out: bfloat16 [1536, 1536], P(('clip', 'seq')), may hold values from -1.25 to 1.25
- norm2_gain: float32 [1536], replicated, may hold values from 0.25 to 1.75
- w_gate: bfloat16 [1536, 4096], P(('clip', 'seq')), may hold values from -0.15625 to 0.15625
- w_up: bfloat16 [1536, 4096], P(('clip', 'seq')), may hold values from -0.15625 to 0.15625
- w_down: bfloat16 [4096, 1536], P(('clip', 'seq')), may hold values from -0.09375 to 0.09375
- cotangent: bfloat16 [4, 1024, 1536], P('clip', 'seq'), may hold values from -6 to 6
Outputs:
- mixed_out: bfloat16 [4, 1024, 1536], P('clip', 'seq')
- grad_tokens: float32 [4, 1024, 1536], P('clip', 'seq')
- grad_caption: float32 [4, 256, 4096], P('clip', 'seq')
- grad_w_time: float32 [256, 1024], P(('clip', 'seq'))
- grad_w_pool: float32 [4096, 1024], P(('clip', 'seq'))
- grad_w_ada: float32 [1024, 6144], P(('clip', 'seq'))
- grad_b_ada: float32 [6144], replicated
- grad_norm1_gain: float32 [1536], replicated
- grad_w_qkv: float32 [1536, 4608], P(('clip', 'seq'))
- grad_w_key_text: float32 [4096, 1536], P(('clip', 'seq'))
- grad_w_value_text: float32 [4096, 1536], P(('clip', 'seq'))
- grad_cross_gate: float32 [24], replicated
- grad_w_out: float32 [1536, 1536], P(('clip', 'seq'))
- grad_norm2_gain: float32 [1536], replicated
- grad_w_gate: float32 [1536, 4096], P(('clip', 'seq'))
- grad_w_up: float32 [1536, 4096], P(('clip', 'seq'))
- grad_w_down: float32 [4096, 1536], P(('clip', 'seq'))
Inputs may be any that keep to these rules, and one draw needn't show every extreme that they name: caption slots below lengths[c] hold the caption of clip c; in every draw some clip has all 256 slots.
All inputs are finite; a program needn't handle non-finite values.
Results may differ from a plain program's by a relative error of at most 0.018.
Values may be sent and summed in bfloat16 or wider, within the bound.
No kernel may reach another device: no remote copies, remote signals or barrier semaphores. Data moves between devices by JAX's collectives and lax.ppermute only.
A program may use at most 448 MiB of HBM per device.

v0:
```python
import math

import jax
import jax.numpy as jnp
from jax import lax
from jax.sharding import PartitionSpec as P

epsilon = 1e-05
head_eps = 1e-06
highest = lax.Precision.HIGHEST
big_negative = -1e30


def rope_tables(posint, half_dim):
    pair_ids = jnp.arange(half_dim)
    first_cut = half_dim // 4
    second_cut = first_cut + (half_dim - first_cut) // 2
    group_of = (pair_ids >= first_cut).astype(jnp.int32) + (pair_ids >= second_cut).astype(
        jnp.int32
    )
    starts = jnp.where(group_of == 0, 0, jnp.where(group_of == 1, first_cut, second_cut))
    counts = jnp.where(
        group_of == 0,
        first_cut,
        jnp.where(group_of == 1, second_cut - first_cut, half_dim - second_cut),
    )
    frequency = jnp.exp(
        -math.log(10000.0) * (pair_ids - starts).astype(jnp.float32) / counts.astype(jnp.float32)
    )
    onehot = (group_of[:, None] == jnp.arange(3)[None, :]).astype(jnp.float32)
    coords = jnp.dot(onehot, posint.astype(jnp.float32), precision=highest)
    angles = coords.T * frequency[None, :]
    return (jnp.cos(angles), jnp.sin(angles))


def rotate(vector, cos_tab, sin_tab):
    half_dim = cos_tab.shape[-1]
    front = vector[..., :half_dim]
    behind = vector[..., half_dim:]
    cos_b = cos_tab[:, None, :]
    sin_b = sin_tab[:, None, :]
    return jnp.concatenate([front * cos_b - behind * sin_b, front * sin_b + behind * cos_b], -1)


def rotate_back(gradient, cos_tab, sin_tab):
    half_dim = cos_tab.shape[-1]
    front = gradient[..., :half_dim]
    behind = gradient[..., half_dim:]
    cos_b = cos_tab[:, None, :]
    sin_b = sin_tab[:, None, :]
    return jnp.concatenate([front * cos_b + behind * sin_b, behind * cos_b - front * sin_b], -1)


def head_norm(vector, eps_value):
    inverse = lax.rsqrt(jnp.mean(vector * vector, -1, keepdims=True) + eps_value)
    return (vector * inverse, inverse)


def norm_back(normed, inverse, gradient):
    return inverse * (gradient - normed * jnp.mean(gradient * normed, -1, keepdims=True))


def timestep_embed(time_step, embed_width):
    half_dim = embed_width // 2
    frequency = jnp.exp(-math.log(10000.0) * jnp.arange(half_dim, dtype=jnp.float32) / half_dim)
    angles = time_step.astype(jnp.float32) * frequency
    return jnp.concatenate([jnp.cos(angles), jnp.sin(angles)])


def body(
    tokens,
    caption,
    lengths,
    timesteps,
    positions,
    w_time,
    w_pool,
    w_ada,
    b_ada,
    norm1_gain,
    w_qkv,
    w_key_text,
    w_value_text,
    cross_gate,
    w_out,
    norm2_gain,
    w_gate,
    w_up,
    w_down,
    cotangent,
):
    head_count = cross_gate.shape[0]
    width = tokens.shape[2]
    head_dim = width // head_count
    tok_rows = tokens.shape[1]
    seq_devices = lax.axis_size("seq")
    seq_len = tok_rows * seq_devices
    attn_scale = 1.0 / math.sqrt(head_dim)
    group_size = 1
    while group_size * tok_rows < 512 and seq_devices % (group_size * 2) == 0:
        group_size = group_size * 2
    key_block = group_size * tok_rows
    time_w, pool_w, ada_w, qkv_w, key_w, value_w, out_w = (
        lax.all_gather(w_time, ("clip", "seq"), axis=0, tiled=True),
        lax.all_gather(w_pool, ("clip", "seq"), axis=0, tiled=True),
        lax.all_gather(w_ada, ("clip", "seq"), axis=0, tiled=True),
        lax.all_gather(w_qkv, ("clip", "seq"), axis=0, tiled=True),
        lax.all_gather(w_key_text, ("clip", "seq"), axis=0, tiled=True),
        lax.all_gather(w_value_text, ("clip", "seq"), axis=0, tiled=True),
        lax.all_gather(w_out, ("clip", "seq"), axis=0, tiled=True),
    )
    gate_w, up_w, down_w = (
        lax.all_gather(w_gate, ("clip", "seq"), axis=0, tiled=True),
        lax.all_gather(w_up, ("clip", "seq"), axis=0, tiled=True),
        lax.all_gather(w_down, ("clip", "seq"), axis=0, tiled=True),
    )
    full_caption = lax.all_gather(caption[0], "seq", axis=0, tiled=True)
    cap_len = full_caption.shape[0]
    cap_rows = caption.shape[1]
    length_f = lengths[0].astype(jnp.float32)
    cap_mask = (jnp.arange(cap_len) < lengths[0]).astype(jnp.float32)
    pooled = jnp.sum(full_caption.astype(jnp.float32) * cap_mask[:, None], 0) / length_f
    time_embed = timestep_embed(timesteps[0], time_w.shape[0])
    time_embed_b = time_embed.astype(jnp.bfloat16)
    pooled_b = pooled.astype(jnp.bfloat16)
    condition = jnp.dot(time_embed_b[None], time_w, preferred_element_type=jnp.float32) + jnp.dot(
        pooled_b[None], pool_w, preferred_element_type=jnp.float32
    )
    cond_b = jax.nn.silu(condition).astype(jnp.bfloat16)
    modulation = jnp.dot(cond_b, ada_w, preferred_element_type=jnp.float32) + b_ada[None]
    scale_attn, gate_attn, scale_ffn, gate_ffn = jnp.split(modulation[0], 4)
    tanh_attn = jnp.tanh(gate_attn)
    tanh_ffn = jnp.tanh(gate_ffn)
    tokens_f = tokens[0].astype(jnp.float32)
    normed1, inverse1 = head_norm(tokens_f, epsilon)
    mix_in = (normed1 * norm1_gain * (1.0 + scale_attn)).astype(jnp.bfloat16)
    qkv_all = jnp.dot(mix_in, qkv_w, preferred_element_type=jnp.float32)
    queries_n, inverse_q = head_norm(
        qkv_all[:, :width].reshape(tok_rows, head_count, head_dim), head_eps
    )
    keys_n, inverse_k = head_norm(
        qkv_all[:, width : 2 * width].reshape(tok_rows, head_count, head_dim), head_eps
    )
    values_b = qkv_all[:, 2 * width :].reshape(tok_rows, head_count, head_dim).astype(jnp.bfloat16)
    cos_tab, sin_tab = rope_tables(positions[:, 0, :], head_dim // 2)
    queries_b = rotate(queries_n, cos_tab, sin_tab).astype(jnp.bfloat16)
    keys_b = rotate(keys_n, cos_tab, sin_tab).astype(jnp.bfloat16)

    def block_step(run_state, block_pair):
        run_max, run_sum, run_acc = run_state
        keys_blk, values_blk = block_pair
        scores = (
            jnp.einsum("qhd,khd->hqk", queries_b, keys_blk, preferred_element_type=jnp.float32)
            * attn_scale
        )
        new_max = jnp.maximum(run_max, jnp.max(scores, -1))
        factor = jnp.exp(run_max - new_max)
        soft_probs = jnp.exp(scores - new_max[:, :, None])
        new_sum = run_sum * factor + jnp.sum(soft_probs, -1)
        update = jnp.einsum(
            "hqk,khd->qhd",
            soft_probs.astype(jnp.bfloat16),
            values_blk,
            preferred_element_type=jnp.float32,
        )
        return ((new_max, new_sum, run_acc * factor.T[:, :, None] + update), None)

    start_state = (
        jnp.full((head_count, tok_rows), big_negative, jnp.float32),
        jnp.zeros((head_count, tok_rows), jnp.float32),
        jnp.zeros((tok_rows, head_count, head_dim), jnp.float32),
    )
    keys_part = lax.all_gather(keys_b, "seq", axis=0, tiled=True)
    values_part = lax.all_gather(values_b, "seq", axis=0, tiled=True)
    part_rows = keys_part.shape[0]
    block_rows = math.gcd(part_rows, key_block)
    stacked = (
        keys_part.reshape(part_rows // block_rows, block_rows, head_count, head_dim),
        values_part.reshape(part_rows // block_rows, block_rows, head_count, head_dim),
    )
    final, leftover = lax.scan(block_step, start_state, stacked)
    run_max, run_sum, run_acc = final
    self_out = run_acc / run_sum.T[:, :, None]
    log_sum = run_max + jnp.log(run_sum)
    text_keys_raw = jnp.dot(full_caption, key_w, preferred_element_type=jnp.float32).reshape(
        cap_len, head_count, head_dim
    )
    text_keys_n, inverse_t = head_norm(text_keys_raw, head_eps)
    keys_text_b = text_keys_n.astype(jnp.bfloat16)
    values_text_b = (
        jnp.dot(full_caption, value_w, preferred_element_type=jnp.float32)
        .reshape(cap_len, head_count, head_dim)
        .astype(jnp.bfloat16)
    )
    cross_scores = (
        jnp.einsum("qhd,khd->hqk", queries_b, keys_text_b, preferred_element_type=jnp.float32)
        * attn_scale
    )
    cross_scores = jnp.where(cap_mask[None, None, :] > 0, cross_scores, big_negative)
    cross_probs = jax.nn.softmax(cross_scores, axis=-1)
    cross_probs_b = cross_probs.astype(jnp.bfloat16)
    cross_out = jnp.einsum(
        "hqk,khd->qhd", cross_probs_b, values_text_b, preferred_element_type=jnp.float32
    )
    gate_t = jnp.tanh(cross_gate)
    mixed_b = (
        (self_out + gate_t[None, :, None] * cross_out).reshape(tok_rows, width).astype(jnp.bfloat16)
    )
    attn_out = jnp.dot(mixed_b, out_w, preferred_element_type=jnp.float32)
    resid = tokens_f + tanh_attn * attn_out
    normed2, inverse2 = head_norm(resid, epsilon)
    ffn_in = (normed2 * norm2_gain * (1.0 + scale_ffn)).astype(jnp.bfloat16)
    gate_pre = jnp.dot(ffn_in, gate_w, preferred_element_type=jnp.float32)
    up_pre = jnp.dot(ffn_in, up_w, preferred_element_type=jnp.float32)
    sigmoid_g = jax.nn.sigmoid(gate_pre)
    silu_g = gate_pre * sigmoid_g
    hidden_b = (silu_g * up_pre).astype(jnp.bfloat16)
    ffn_out = jnp.dot(hidden_b, down_w, preferred_element_type=jnp.float32)
    mixed_out = (resid + tanh_ffn * ffn_out).astype(jnp.bfloat16)
    d_out = cotangent[0].astype(jnp.float32)
    d_ffn_b = (tanh_ffn * d_out).astype(jnp.bfloat16)
    grad_gate_ffn = jnp.sum(d_out * ffn_out, 0) * (1.0 - tanh_ffn * tanh_ffn)
    grad_w_down = jnp.einsum("tf,td->fd", hidden_b, d_ffn_b, preferred_element_type=jnp.float32)
    d_hidden = jnp.einsum("td,fd->tf", d_ffn_b, down_w, preferred_element_type=jnp.float32)
    silu_slope = sigmoid_g * (1.0 + gate_pre * (1.0 - sigmoid_g))
    d_gate_b = (d_hidden * up_pre * silu_slope).astype(jnp.bfloat16)
    d_up_b = (d_hidden * silu_g).astype(jnp.bfloat16)
    grad_w_gate = jnp.einsum("td,tf->df", ffn_in, d_gate_b, preferred_element_type=jnp.float32)
    grad_w_up = jnp.einsum("td,tf->df", ffn_in, d_up_b, preferred_element_type=jnp.float32)
    sum_gate, sum_up, sum_down = (
        lax.psum_scatter(grad_w_gate, ("clip", "seq"), scatter_dimension=0, tiled=True),
        lax.psum_scatter(grad_w_up, ("clip", "seq"), scatter_dimension=0, tiled=True),
        lax.psum_scatter(grad_w_down, ("clip", "seq"), scatter_dimension=0, tiled=True),
    )
    d_ffn_in = jnp.einsum(
        "tf,df->td", d_gate_b, gate_w, preferred_element_type=jnp.float32
    ) + jnp.einsum("tf,df->td", d_up_b, up_w, preferred_element_type=jnp.float32)
    grad_norm2 = jnp.sum(d_ffn_in * normed2 * (1.0 + scale_ffn), 0)
    grad_scale_ffn = jnp.sum(d_ffn_in * normed2 * norm2_gain, 0)
    d_resid = d_out + norm_back(normed2, inverse2, d_ffn_in * norm2_gain * (1.0 + scale_ffn))
    d_attn_b = (tanh_attn * d_resid).astype(jnp.bfloat16)
    grad_gate_attn = jnp.sum(d_resid * attn_out, 0) * (1.0 - tanh_attn * tanh_attn)
    grad_w_out = jnp.einsum("td,te->de", mixed_b, d_attn_b, preferred_element_type=jnp.float32)
    d_mixed = jnp.einsum("te,de->td", d_attn_b, out_w, preferred_element_type=jnp.float32).reshape(
        tok_rows, head_count, head_dim
    )
    grad_cross_gate = jnp.sum(d_mixed * cross_out, axis=(0, 2)) * (1.0 - gate_t * gate_t)
    d_self_b = d_mixed.astype(jnp.bfloat16)
    d_cross_b = (gate_t[None, :, None] * d_mixed).astype(jnp.bfloat16)
    d_cross_probs = jnp.einsum(
        "qhd,khd->hqk", d_cross_b, values_text_b, preferred_element_type=jnp.float32
    )
    d_cross_scores = (
        cross_probs * (d_cross_probs - jnp.sum(cross_probs * d_cross_probs, -1, keepdims=True))
    ).astype(jnp.bfloat16)
    d_queries_cross = (
        jnp.einsum("hqk,khd->qhd", d_cross_scores, keys_text_b, preferred_element_type=jnp.float32)
        * attn_scale
    )
    d_text_keys_n = (
        jnp.einsum("hqk,qhd->khd", d_cross_scores, queries_b, preferred_element_type=jnp.float32)
        * attn_scale
    )
    d_text_values = jnp.einsum(
        "hqk,qhd->khd", cross_probs_b, d_cross_b, preferred_element_type=jnp.float32
    )
    d_text_keys = norm_back(text_keys_n, inverse_t, d_text_keys_n)
    text_grads = jnp.concatenate(
        [d_text_keys.reshape(cap_len, width), d_text_values.reshape(cap_len, width)], -1
    )
    row_dots = jnp.sum(d_self_b.astype(jnp.float32) * self_out, -1).T

    def key_terms(keys_blk, values_blk):
        scores = (
            jnp.einsum("qhd,khd->hqk", queries_b, keys_blk, preferred_element_type=jnp.float32)
            * attn_scale
        )
        soft_probs = jnp.exp(scores - log_sum[:, :, None])
        d_probs = jnp.einsum(
            "qhd,khd->hqk", d_self_b, values_blk, preferred_element_type=jnp.float32
        )
        d_scores_b = (soft_probs * (d_probs - row_dots[:, :, None])).astype(jnp.bfloat16)
        dq_part = (
            jnp.einsum("hqk,khd->qhd", d_scores_b, keys_blk, preferred_element_type=jnp.float32)
            * attn_scale
        )
        dk_part = (
            jnp.einsum("hqk,qhd->khd", d_scores_b, queries_b, preferred_element_type=jnp.float32)
            * attn_scale
        )
        dv_part = jnp.einsum(
            "hqk,qhd->khd",
            soft_probs.astype(jnp.bfloat16),
            d_self_b,
            preferred_element_type=jnp.float32,
        )
        return (dq_part, dk_part, dv_part)

    zero_rows = jnp.zeros((tok_rows, head_count, head_dim), jnp.float32)
    all_keys, all_values = (
        lax.all_gather(keys_b, "seq", axis=0, tiled=True),
        lax.all_gather(values_b, "seq", axis=0, tiled=True),
    )
    block_count = seq_len // key_block

    def back_step(dq_run, block_pair):
        dq_part, dk_part, dv_part = key_terms(block_pair[0], block_pair[1])
        return (dq_run + dq_part, (dk_part, dv_part))

    dq_self, key_stacks = lax.scan(
        back_step,
        zero_rows,
        (
            all_keys.reshape(block_count, key_block, head_count, head_dim),
            all_values.reshape(block_count, key_block, head_count, head_dim),
        ),
    )
    d_keys_local, d_values_local = (
        lax.psum_scatter(
            key_stacks[0].reshape(seq_len, width).astype(jnp.bfloat16),
            "seq",
            scatter_dimension=0,
            tiled=True,
        ).astype(jnp.float32),
        lax.psum_scatter(
            key_stacks[1].reshape(seq_len, width).astype(jnp.bfloat16),
            "seq",
            scatter_dimension=0,
            tiled=True,
        ).astype(jnp.float32),
    )
    d_keys_local = d_keys_local.reshape(tok_rows, head_count, head_dim)
    d_values_local = d_values_local.reshape(tok_rows, head_count, head_dim)
    d_queries = rotate_back(dq_self + d_queries_cross, cos_tab, sin_tab)
    d_queries_raw = norm_back(queries_n, inverse_q, d_queries)
    d_keys_raw = norm_back(keys_n, inverse_k, rotate_back(d_keys_local, cos_tab, sin_tab))
    d_qkv_b = jnp.concatenate(
        [
            d_queries_raw.reshape(tok_rows, width),
            d_keys_raw.reshape(tok_rows, width),
            d_values_local.reshape(tok_rows, width),
        ],
        -1,
    ).astype(jnp.bfloat16)
    grad_w_qkv = jnp.einsum("td,te->de", mix_in, d_qkv_b, preferred_element_type=jnp.float32)
    d_mix_in = jnp.einsum("te,de->td", d_qkv_b, qkv_w, preferred_element_type=jnp.float32)
    grad_norm1 = jnp.sum(d_mix_in * normed1 * (1.0 + scale_attn), 0)
    grad_scale_attn = jnp.sum(d_mix_in * normed1 * norm1_gain, 0)
    d_tokens = d_resid + norm_back(normed1, inverse1, d_mix_in * norm1_gain * (1.0 + scale_attn))
    d_modulation = jnp.concatenate(
        [grad_scale_attn, grad_gate_attn, grad_scale_ffn, grad_gate_ffn]
    )[None]
    grad_w_ada = jnp.einsum(
        "ic,ie->ce", cond_b.astype(jnp.float32), d_modulation, precision=highest
    )
    d_cond_act = jnp.einsum(
        "ie,ce->ic", d_modulation, ada_w, precision=highest, preferred_element_type=jnp.float32
    )
    cond_sigmoid = jax.nn.sigmoid(condition)
    d_condition = d_cond_act * cond_sigmoid * (1.0 + condition * (1.0 - cond_sigmoid))
    grad_w_time = time_embed_b.astype(jnp.float32)[:, None] * d_condition
    grad_w_pool = pooled_b.astype(jnp.float32)[:, None] * d_condition
    d_pooled = jnp.einsum(
        "ic,pc->ip", d_condition, pool_w, precision=highest, preferred_element_type=jnp.float32
    )
    pool_rows = jnp.broadcast_to(d_pooled, (seq_devices, d_pooled.shape[1]))
    text_sum, pool_sum = (
        lax.psum_scatter(
            text_grads.astype(jnp.bfloat16), "seq", scatter_dimension=0, tiled=True
        ).astype(jnp.float32),
        lax.psum_scatter(
            pool_rows.astype(jnp.bfloat16), "seq", scatter_dimension=0, tiled=True
        ).astype(jnp.float32),
    )
    d_text_keys_b = text_sum[:, :width].astype(jnp.bfloat16)
    d_text_values_b = text_sum[:, width:].astype(jnp.bfloat16)
    local_mask = (lax.axis_index("seq") * cap_rows + jnp.arange(cap_rows) < lengths[0]).astype(
        jnp.float32
    )
    grad_w_key_text = jnp.einsum(
        "cp,cd->pd", caption[0], d_text_keys_b, preferred_element_type=jnp.float32
    )
    grad_w_value_text = jnp.einsum(
        "cp,cd->pd", caption[0], d_text_values_b, preferred_element_type=jnp.float32
    )
    d_caption = (
        jnp.einsum("cd,pd->cp", d_text_keys_b, key_w, preferred_element_type=jnp.float32)
        + jnp.einsum("cd,pd->cp", d_text_values_b, value_w, preferred_element_type=jnp.float32)
        + local_mask[:, None] * pool_sum / length_f
    )
    sum_time, sum_pool, sum_ada, sum_qkv, sum_key_text, sum_value_text, sum_out = (
        lax.psum_scatter(grad_w_time, ("clip", "seq"), scatter_dimension=0, tiled=True),
        lax.psum_scatter(grad_w_pool, ("clip", "seq"), scatter_dimension=0, tiled=True),
        lax.psum_scatter(grad_w_ada, ("clip", "seq"), scatter_dimension=0, tiled=True),
        lax.psum_scatter(grad_w_qkv, ("clip", "seq"), scatter_dimension=0, tiled=True),
        lax.psum_scatter(grad_w_key_text, ("clip", "seq"), scatter_dimension=0, tiled=True),
        lax.psum_scatter(grad_w_value_text, ("clip", "seq"), scatter_dimension=0, tiled=True),
        lax.psum_scatter(grad_w_out, ("clip", "seq"), scatter_dimension=0, tiled=True),
    )
    sum_norm1, sum_norm2, sum_bias, sum_cross = lax.psum(
        (grad_norm1, grad_norm2, d_modulation[0], grad_cross_gate), ("clip", "seq")
    )
    return (
        mixed_out[None],
        d_tokens[None],
        d_caption[None],
        sum_time,
        sum_pool,
        sum_ada,
        sum_bias,
        sum_norm1,
        sum_qkv,
        sum_key_text,
        sum_value_text,
        sum_cross,
        sum_out,
        sum_norm2,
        sum_gate,
        sum_up,
        sum_down,
    )


def solution(mesh):
    placed = (
        P("clip", "seq", None),
        P("clip", "seq", None),
        P("clip"),
        P("clip"),
        P(None, "clip", "seq"),
        P(("clip", "seq"), None),
        P(("clip", "seq"), None),
        P(("clip", "seq"), None),
        P(),
        P(),
        P(("clip", "seq"), None),
        P(("clip", "seq"), None),
        P(("clip", "seq"), None),
        P(),
        P(("clip", "seq"), None),
        P(),
        P(("clip", "seq"), None),
        P(("clip", "seq"), None),
        P(("clip", "seq"), None),
        P("clip", "seq", None),
    )
    return jax.shard_map(
        body,
        mesh=mesh,
        in_specs=placed,
        out_specs=(
            P("clip", "seq", None),
            P("clip", "seq", None),
            P("clip", "seq", None),
            P(("clip", "seq"), None),
            P(("clip", "seq"), None),
            P(("clip", "seq"), None),
            P(),
            P(),
            P(("clip", "seq"), None),
            P(("clip", "seq"), None),
            P(("clip", "seq"), None),
            P(),
            P(("clip", "seq"), None),
            P(),
            P(("clip", "seq"), None),
            P(("clip", "seq"), None),
            P(("clip", "seq"), None),
        ),
        check_vma=False,
    )
```

profile of v0, /device:TPU:0, one launch (start us, length us, event | category | flops | bytes accessed | tf_op | source)
XLA Modules:
  0.0 3833.2 jit_solution(6508571385783438446)
XLA Ops:
  15.3 75.2 %all_gather.41 = bf16[256,1024]{1,0:T(8,128)(2,1)S(1)} all-gather(bf16[8,1024]{1,0:T(8,128)(2,1)} %param.29), channel_id=1, replica_groups=mesh['clip'=4,'seq'=8] {'clip','seq'}, dimensions={0}, use_global_device_ids=true | all-gather | bytes 540672 | tf_op jit(solution)/shard_map/all_gather | solution.py:104
  93.5 51.7 %all-gather.14.cloned.1.call-done = bf16[4096,1024]{1,0:T(8,128)(2,1)} async-done(((bf16[128,1024]{1,0:T(8,128)(2,1)}), bf16[4096,1024]{1,0:T(8,128)(2,1)}) %all-gather.14.cloned.1.call-update) | async-done | bytes 8388624 | tf_op jit(solution)/shard_map/all_gather | solution.py:105
  150.4 92.4 %all-gather.16.cloned.1.call-done = bf16[1024,6144]{1,0:T(8,128)(2,1)} async-done(((bf16[32,6144]{1,0:T(8,128)(2,1)}), bf16[1024,6144]{1,0:T(8,128)(2,1)}) %all-gather.16.cloned.1.call-update) | async-done | bytes 12582928 | tf_op jit(solution)/shard_map/all_gather | solution.py:106
  249.9 97.3 %all-gather.18.cloned.1.call-done = bf16[1536,4608]{1,0:T(8,128)(2,1)} async-done(((bf16[48,4608]{1,0:T(8,128)(2,1)}), bf16[1536,4608]{1,0:T(8,128)(2,1)}) %all-gather.18.cloned.1.call-update) | async-done | bytes 14155792 | tf_op jit(solution)/shard_map/all_gather | solution.py:107
  367.2 76.9 %all-gather.24.cloned.1.call-done = bf16[4096,1536]{1,0:T(8,128)(2,1)} async-done(((bf16[128,1536]{1,0:T(8,128)(2,1)}), bf16[4096,1536]{1,0:T(8,128)(2,1)}) %all-gather.24.cloned.1.call-update) | async-done | bytes 12582928 | tf_op jit(solution)/shard_map/all_gather | solution.py:109
  444.2 8.6 convolution_convert_fusion
  453.9 87.3 %all-gather.26.cloned.1.call-done = bf16[4096,1536]{1,0:T(8,128)(2,1)} async-done(((bf16[128,1536]{1,0:T(8,128)(2,1)}), bf16[4096,1536]{1,0:T(8,128)(2,1)}) %all-gather.26.cloned.1.call-update) | async-done | bytes 12582928 | tf_op jit(solution)/shard_map/all_gather | solution.py:108
  541.3 7.9 fusion.59
  553.5 51.8 %all-gather.20.cloned.1.call-done = bf16[1024,24,64]{0,2,1:T(8,128)(2,1)} async-done(((bf16[128,24,64]{0,2,1:T(8,128)(2,1)}), bf16[1024,24,64]{0,2,1:T(8,128)(2,1)}) %all-gather.20.cloned.1.call-update) | async-done | bytes 3145744 | tf_op jit(solution)/shard_map/all_gather | solution.py:173
  607.6 61.6 %all-gather.22.cloned.1.call-done = bf16[1024,24,64]{0,2,1:T(8,128)(2,1)} async-done(((bf16[128,24,64]{0,2,1:T(8,128)(2,1)}), bf16[1024,24,64]{0,2,1:T(8,128)(2,1)}) %all-gather.22.cloned.1.call-update) | async-done | bytes 3145744 | tf_op jit(solution)/shard_map/all_gather | solution.py:174
  673.1 27.7 while.30
  705.0 29.1 all-gather.28.cloned.1.call-done
  740.1 91.6 %all-gather.30.cloned.1.call-done = bf16[1536,4096]{1,0:T(8,128)(2,1)} async-done(((bf16[48,4096]{1,0:T(8,128)(2,1)}), bf16[1536,4096]{1,0:T(8,128)(2,1)}) %all-gather.30.cloned.1.call-update) | async-done | bytes 12582928 | tf_op jit(solution)/shard_map/all_gather | solution.py:113
  839.6 89.4 %all-gather.32.cloned.1.call-done = bf16[1536,4096]{1,0:T(8,128)(2,1)} async-done(((bf16[48,4096]{1,0:T(8,128)(2,1)}), bf16[1536,4096]{1,0:T(8,128)(2,1)}) %all-gather.32.cloned.1.call-update) | async-done | bytes 12582928 | tf_op jit(solution)/shard_map/all_gather | solution.py:114
  936.8 89.3 %all-gather.34.cloned.1.call-done = bf16[4096,1536]{1,0:T(8,128)(2,1)} async-done(((bf16[128,1536]{1,0:T(8,128)(2,1)}), bf16[4096,1536]{1,0:T(8,128)(2,1)}) %all-gather.34.cloned.1.call-update) | async-done | bytes 12582928 | tf_op jit(solution)/shard_map/all_gather | solution.py:115
  1026.1 10.2 multiply_convert_fusion.2
  1036.4 10.0 fusion.136
  1046.5 10.1 multiply_reduce_fusion.3
  1057.2 8.2 fusion.84
  1068.8 33.8 while.31
  1110.4 9.6 reshape.312
  1127.9 9.2 reshape.311
  1158.8 33.9 reduce-scatter.40.cloned.1.call-done
  1213.2 56.5 %reduce-scatter.18.cloned.1.call-done = bf16[128,1536]{1,0:T(8,128)(2,1)} async-done(((bf16[1024,1536]{1,0:T(8,128)(2,1)}), bf16[128,1536]{1,0:T(8,128)(2,1)}) %reduce-scatter.18.cloned.1.call-update) | async-done | bytes 393232 | tf_op jit(solution)/shard_map/reduce_scatter | solution.py:325
  1269.8 10.8 multiply_reduce_fusion.5
  1280.6 12.7 fusion.137
  1293.4 9.0 fusion.138
  1303.1 34.0 reduce-scatter.42.cloned.1.call-done
  1337.1 11.0 convolution_bitcast_fusion.1
  1349.1 10.1 convolution_bitcast_fusion
  1367.5 10.2 fusion.139
  1378.9 10.1 fusion.140
  1390.2 10.5 fusion.90
  1408.9 11.9 broadcast_multiply_fusion
  1422.2 14.5 fusion.87
  1438.0 9.7 fusion.101
  1447.7 40.6 %all-reduce.1 = (f32[6144]{0:T(1024)}, f32[1536]{0:T(1024)}, f32[24]{0:T(128)}, f32[1536]{0:T(1024)}) all-reduce(f32[6144]{0:T(1024)S(1)} %pad_maximum_fusion.8, f32[1536]{0:T(1024)S(1)} %get-tuple-element.278, f32[24]{0:T(128)S(1)} %subtract_multiply_fusion, f32[1536]{0:T(1024)S(1)} %copy-done.90), channel_id=1, replica_groups=mesh['clip'=4,'seq'=8] {'clip','seq'}, use_global_device_ids=true, to_apply=%region_32.33 | all-reduce | flops 9240 | bytes 73920 | tf_op jit(solution)/shard_map/psum | solution.py:400
  1492.1 9.3 fusion.57
  1501.5 157.9 %reduce-scatter.28.cloned.1.call-done = f32[128,1536]{0,1:T(8,128)} async-done(((f32[4096,1536]{0,1:T(8,128)}), f32[128,1536]{0,1:T(8,128)}) %reduce-scatter.28.cloned.1.call-update) | async-done | bytes 786448 | tf_op jit(solution)/shard_map/reduce_scatter | solution.py:396
  1661.7 247.4 %reduce-scatter.30.cloned.1.call-done = f32[128,1536]{0,1:T(8,128)} async-done(((f32[4096,1536]{0,1:T(8,128)}), f32[128,1536]{0,1:T(8,128)}) %reduce-scatter.30.cloned.1.call-update) | async-done | bytes 786448 | tf_op jit(solution)/shard_map/reduce_scatter | solution.py:397
  1911.4 135.2 %reduce-scatter.20.cloned.1.call-done = f32[8,1024]{1,0:T(8,128)} async-done(((f32[256,1024]{1,0:T(8,128)}), f32[8,1024]{1,0:T(8,128)}) %reduce-scatter.20.cloned.1.call-update) | async-done | bytes 32784 | tf_op jit(solution)/shard_map/reduce_scatter | solution.py:392
  2046.7 138.3 %reduce-scatter.32.cloned.1.call-done = f32[48,1536]{1,0:T(8,128)} async-done(((f32[1536,1536]{1,0:T(8,128)}), f32[48,1536]{1,0:T(8,128)}) %reduce-scatter.32.cloned.1.call-update) | async-done | bytes 294928 | tf_op jit(solution)/shard_map/reduce_scatter | solution.py:398
  2185.0 252.6 %reduce-scatter.34.cloned.1.call-done = f32[48,4096]{1,0:T(8,128)} async-done(((f32[1536,4096]{1,0:T(8,128)}), f32[48,4096]{1,0:T(8,128)}) %reduce-scatter.34.cloned.1.call-update) | async-done | bytes 786448 | tf_op jit(solution)/shard_map/reduce_scatter | solution.py:231
  2437.5 252.0 %reduce-scatter.36.cloned.1.call-done = f32[48,4096]{1,0:T(8,128)} async-done(((f32[1536,4096]{1,0:T(8,128)}), f32[48,4096]{1,0:T(8,128)}) %reduce-scatter.36.cloned.1.call-update) | async-done | bytes 786448 | tf_op jit(solution)/shard_map/reduce_scatter | solution.py:232
  2689.5 253.2 %reduce-scatter.38.cloned.1.call-done = f32[128,1536]{1,0:T(8,128)} async-done(((f32[4096,1536]{1,0:T(8,128)}), f32[128,1536]{1,0:T(8,128)}) %reduce-scatter.38.cloned.1.call-update) | async-done | bytes 786448 | tf_op jit(solution)/shard_map/reduce_scatter | solution.py:233
  2942.7 360.5 %reduce-scatter.22.cloned.1.call-done = f32[128,1024]{1,0:T(8,128)} async-done(((f32[4096,1024]{1,0:T(8,128)}), f32[128,1024]{1,0:T(8,128)}) %reduce-scatter.22.cloned.1.call-update) | async-done | bytes 524304 | tf_op jit(solution)/shard_map/reduce_scatter | solution.py:393
  3303.1 251.7 %reduce-scatter.24.cloned.1.call-done = f32[32,6144]{1,0:T(8,128)} async-done(((f32[1024,6144]{1,0:T(8,128)}), f32[32,6144]{1,0:T(8,128)}) %reduce-scatter.24.cloned.1.call-update) | async-done | bytes 786448 | tf_op jit(solution)/shard_map/reduce_scatter | solution.py:394
  3554.8 271.4 %reduce-scatter.26.cloned.1.call-done = f32[48,4608]{1,0:T(8,128)} async-done(((f32[1536,4608]{1,0:T(8,128)}), f32[48,4608]{1,0:T(8,128)}) %reduce-scatter.26.cloned.1.call-update) | async-done | bytes 884752 | tf_op jit(solution)/shard_map/reduce_scatter | solution.py:395
  (431 shorter events, 233.5 us)
Async XLA Ops:
  7.2 83.5 %all-gather.36.cloned.1.call-start = ((), (), s32[]{:S(2)}) async-start(), calls=%async_computation.35 | async-start | bytes 2359296 | tf_op jit(solution)/shard_map/all_gather | solution.py:117
  7.9 137.3 %all-gather.14.cloned.1.call-start = ((), (), s32[]{:S(2)}) async-start(), calls=%async_computation.13 | async-start | bytes 8650752 | tf_op jit(solution)/shard_map/all_gather | solution.py:105
  8.7 234.2 %all-gather.16.cloned.1.call-start = ((), (), s32[]{:S(2)}) async-start(), calls=%async_computation.14 | async-start | bytes 12976128 | tf_op jit(solution)/shard_map/all_gather | solution.py:106
  9.4 337.8 %all-gather.18.cloned.1.call-start = ((), (), s32[]{:S(2)}) async-start(), calls=%async_computation.15 | async-start | bytes 14598144 | tf_op jit(solution)/shard_map/all_gather | solution.py:107
  10.0 434.2 %all-gather.24.cloned.1.call-start = ((), (), s32[]{:S(2)}) async-start(), calls=%async_computation.18 | async-start | bytes 12976128 | tf_op jit(solution)/shard_map/all_gather | solution.py:109
  10.6 530.7 %all-gather.26.cloned.1.call-start = ((), (), s32[]{:S(2)}) async-start(), calls=%async_computation.19 | async-start | bytes 12976128 | tf_op jit(solution)/shard_map/all_gather | solution.py:108
  11.1 594.1 %all-gather.20.cloned.1.call-start = ((), (), s32[]{:S(2)}) async-start(), calls=%async_computation.16 | async-start | bytes 3538944 | tf_op jit(solution)/shard_map/all_gather | solution.py:173
  15.0 332.2 %copy-start.96 = (f32[128]{0:T(128)}, f32[128]{0:T(128)S(1)}, u32[]{:S(2)}) copy-start(f32[128]{0:T(128)S(1)} %add_rsqrt_fusion.4) | copy-start | bytes 1540
  15.3 346.5 %copy-start.80 = (f32[128,32]{0,1:T(8,128)}, f32[128,32]{0,1:T(8,128)S(1)}, u32[]{:S(2)}) copy-start(f32[128,32]{0,1:T(8,128)S(1)} %get-tuple-element.369) | copy-start | bytes 49156
  15.3 346.5 %copy-start.81 = (f32[128,32]{0,1:T(8,128)}, f32[128,32]{0,1:T(8,128)S(1)}, u32[]{:S(2)}) copy-start(f32[128,32]{0,1:T(8,128)S(1)} %get-tuple-element.370) | copy-start | bytes 49156
  90.7 59.1 %copy-start.83 = (f32[1,1024]{1,0:T(1,128)}, f32[1,1024]{1,0:T(1,128)S(1)}, u32[]{:S(2)}) copy-start(f32[1,1024]{1,0:T(1,128)S(1)} %fusion.131) | copy-start | bytes 12292
  149.8 99.4 %copy-start.85 = (f32[1,1024]{1,0:T(1,128)}, f32[1,1024]{1,0:T(1,128)S(1)}, u32[]{:S(2)}) copy-start(f32[1,1024]{1,0:T(1,128)S(1)} %fusion.132) | copy-start | bytes 12292
  150.4 98.8 %copy-start.95 = (f32[6144]{0:T(1024)S(1)}, f32[6144]{0:T(1024)}, u32[]{:S(2)}) copy-start(f32[6144]{0:T(1024)} %param.32) | copy-start | bytes 73732
  150.4 196.8 %copy-start.24 = (bf16[1,128,1536]{2,1,0:T(8,128)(2,1)S(1)}, bf16[1,128,1536]{2,1,0:T(8,128)(2,1)}, u32[]{:S(2)}) copy-start(bf16[1,128,1536]{2,1,0:T(8,128)(2,1)} %param.24) | copy-start | bytes 1179652
  150.4 196.8 %copy-start.66 = (f32[1536]{0:T(1024)S(1)}, f32[1536]{0:T(1024)}, u32[]{:S(2)}) copy-start(f32[1536]{0:T(1024)} %param.33) | copy-start | bytes 18436
  249.9 104.4 %copy-start.64 = (f32[1536]{0:T(1024)}, f32[1536]{0:T(1024)S(1)}, u32[]{:S(2)}) copy-start(f32[1536]{0:T(1024)S(1)} %get-tuple-element.285) | copy-start | bytes 18436
  362.0 187.5 %copy-start.32 = (bf16[128,24,32]{0,2,1:T(8,128)(2,1)}, bf16[128,24,32]{0,2,1:T(8,128)(2,1)S(1)}, u32[]{:S(2)}) copy-start(bf16[128,24,32]{0,2,1:T(8,128)(2,1)S(1)} %get-tuple-element.367) | copy-start | bytes 589828
  362.0 187.4 %copy-start.34 = (bf16[128,24,32]{0,2,1:T(8,128)(2,1)}, bf16[128,24,32]{0,2,1:T(8,128)(2,1)S(1)}, u32[]{:S(2)}) copy-start(bf16[128,24,32]{0,2,1:T(8,128)(2,1)S(1)} %get-tuple-element.368) | copy-start | bytes 589828
  362.9 306.2 %all-gather.22.cloned.1.call-start = ((), (), s32[]{:S(2)}) async-start(), calls=%async_computation.17 | async-start | bytes 3538944 | tf_op jit(solution)/shard_map/all_gather | solution.py:174
  364.0 370.1 %all-gather.28.cloned.1.call-start = ((), (), s32[]{:S(2)}) async-start(), calls=%async_computation.20 | async-start | bytes 4866048 | tf_op jit(solution)/shard_map/all_gather | solution.py:110
  364.7 467.0 %all-gather.30.cloned.1.call-start = ((), (), s32[]{:S(2)}) async-start(), calls=%async_computation.21 | async-start | bytes 12976128 | tf_op jit(solution)/shard_map/all_gather | solution.py:113
  365.3 563.7 %all-gather.32.cloned.1.call-start = ((), (), s32[]{:S(2)}) async-start(), calls=%async_computation.22 | async-start | bytes 12976128 | tf_op jit(solution)/shard_map/all_gather | solution.py:114
  366.0 660.0 %all-gather.34.cloned.1.call-start = ((), (), s32[]{:S(2)}) async-start(), calls=%async_computation.23 | async-start | bytes 12976128 | tf_op jit(solution)/shard_map/all_gather | solution.py:115
  366.6 826.1 %reduce-scatter.40.cloned.1.call-start = ((), (), s32[]{:S(2)}) async-start(), calls=%async_computation.36 | async-start | bytes 3538944
  367.2 333.6 %copy-start.105 = (f32[24]{0:T(128)}, f32[24]{0:T(128)S(1)}, u32[]{:S(2)}) copy-start(f32[24]{0:T(128)S(1)} %tanh.14) | copy-start | bytes 292
  367.2 174.1 %copy-start.49 = (bf16[1,256,4096]{2,1,0:T(8,128)(2,1)S(1)}, bf16[1,256,4096]{2,1,0:T(8,128)(2,1)}, u32[]{:S(2)}) copy-start(bf16[1,256,4096]{2,1,0:T(8,128)(2,1)} %all-gather.36.cloned.1.call-done) | copy-start | bytes 6291460
  1036.3 20.8 copy-start.26
  1046.5 18.9 slice-start
  1120.0 149.8 %reduce-scatter.18.cloned.1.call-start = ((), (), s32[]{:S(2)}) async-start(), calls=%async_computation.24 | async-start | bytes 3538944 | tf_op jit(solution)/shard_map/reduce_scatter | solution.py:325
  1137.2 199.9 %reduce-scatter.42.cloned.1.call-start = ((), (), s32[]{:S(2)}) async-start(), calls=%async_computation.37 | async-start | bytes 1769472
  1157.3 38.5 %copy-start.21 = (f32[128,1536]{0,1:T(8,128)S(1)}, f32[128,1536]{0,1:T(8,128)}, u32[]{:S(2)}) copy-start(f32[128,1536]{0,1:T(8,128)} %copy.81) | copy-start | bytes 2359300
  1157.4 333.3 %all-reduce.4.cloned.1.call-start = ((), (), s32[]{:S(2)}) async-start(), calls=%async_computation.38 | async-start | bytes 131072
  1209.5 60.3 %copy-start.25 = (bf16[1,128,1536]{2,1,0:T(8,128)(2,1)S(1)}, bf16[1,128,1536]{2,1,0:T(8,128)(2,1)}, u32[]{:S(2)}) copy-start(bf16[1,128,1536]{2,1,0:T(8,128)(2,1)} %param.24) | copy-start | bytes 1179652
  1209.5 60.3 %copy-start.65 = (f32[1536]{0:T(1024)S(1)}, f32[1536]{0:T(1024)}, u32[]{:S(2)}) copy-start(f32[1536]{0:T(1024)} %copy-done.64) | copy-start | bytes 18436
  1209.5 60.3 %copy-start.67 = (f32[1536]{0:T(1024)S(1)}, f32[1536]{0:T(1024)}, u32[]{:S(2)}) copy-start(f32[1536]{0:T(1024)} %param.33) | copy-start | bytes 18436
  1280.6 12.8 copy-start.84
  1280.6 12.8 copy-start.86
  1293.4 43.7 %copy-start.48 = (bf16[1,32,4096]{2,1,0:T(8,128)(2,1)S(1)}, bf16[1,32,4096]{2,1,0:T(8,128)(2,1)}, u32[]{:S(2)}) copy-start(bf16[1,32,4096]{2,1,0:T(8,128)(2,1)} %param.25) | copy-start | bytes 786436
  1303.1 356.4 %reduce-scatter.28.cloned.1.call-start = ((), (), s32[]{:S(2)}) async-start(), calls=%async_computation.29 | async-start | bytes 25952256 | tf_op jit(solution)/shard_map/reduce_scatter | solution.py:396
  1348.2 561.0 %reduce-scatter.30.cloned.1.call-start = ((), (), s32[]{:S(2)}) async-start(), calls=%async_computation.30 | async-start | bytes 25952256 | tf_op jit(solution)/shard_map/reduce_scatter | solution.py:397
  1359.2 687.4 %reduce-scatter.20.cloned.1.call-start = ((), (), s32[]{:S(2)}) async-start(), calls=%async_computation.25 | async-start | bytes 1081344 | tf_op jit(solution)/shard_map/reduce_scatter | solution.py:392
  1361.0 824.0 %reduce-scatter.32.cloned.1.call-start = ((), (), s32[]{:S(2)}) async-start(), calls=%async_computation.31 | async-start | bytes 9732096 | tf_op jit(solution)/shard_map/reduce_scatter | solution.py:398
  1366.1 1071.4 %reduce-scatter.34.cloned.1.call-start = ((), (), s32[]{:S(2)}) async-start(), calls=%async_computation.32 | async-start | bytes 25952256 | tf_op jit(solution)/shard_map/reduce_scatter | solution.py:231
  1377.7 1311.9 %reduce-scatter.36.cloned.1.call-start = ((), (), s32[]{:S(2)}) async-start(), calls=%async_computation.33 | async-start | bytes 25952256 | tf_op jit(solution)/shard_map/reduce_scatter | solution.py:232
  1388.9 1553.7 %reduce-scatter.38.cloned.1.call-start = ((), (), s32[]{:S(2)}) async-start(), calls=%async_computation.34 | async-start | bytes 25952256 | tf_op jit(solution)/shard_map/reduce_scatter | solution.py:233
  1400.7 1902.4 %reduce-scatter.22.cloned.1.call-start = ((), (), s32[]{:S(2)}) async-start(), calls=%async_computation.26 | async-start | bytes 17301504 | tf_op jit(solution)/shard_map/reduce_scatter | solution.py:393
  1408.3 2146.6 %reduce-scatter.24.cloned.1.call-start = ((), (), s32[]{:S(2)}) async-start(), calls=%async_computation.27 | async-start | bytes 25952256 | tf_op jit(solution)/shard_map/reduce_scatter | solution.py:394
  1420.8 2405.4 %reduce-scatter.26.cloned.1.call-start = ((), (), s32[]{:S(2)}) async-start(), calls=%async_computation.28 | async-start | bytes 29196288 | tf_op jit(solution)/shard_map/reduce_scatter | solution.py:395
  (102 other events, 410.7 us)
Sparse Core Ops, SparseCore 0:
  10.1 54.8 all-gather.35
  68.0 77.2 all-gather.13
  148.2 94.5 all-gather.15
  245.7 101.4 all-gather.17
  350.0 94.1 all-gather.23
  447.0 94.2 all-gather.25
  543.9 61.2 all-gather.19
  607.8 61.2 all-gather.21
  672.1 61.8 all-gather.27
  736.9 94.8 all-gather.29
  834.7 94.2 all-gather.31
  931.8 94.2 all-gather.33
  1120.1 72.6 reduce-scatter.39
  1196.2 73.5 reduce-scatter.17
  1273.0 64.0 reduce-scatter.41
  1340.8 67.3 all-reduce.3
  1415.6 243.7 reduce-scatter.27
  1665.7 243.3 reduce-scatter.29
  1912.0 134.5 reduce-scatter.19
  2053.0 131.9 reduce-scatter.31
  2193.1 244.3 reduce-scatter.33
  2444.5 244.9 reduce-scatter.35
  2697.7 244.9 reduce-scatter.37
  2945.4 357.6 reduce-scatter.21
  3310.1 244.6 reduce-scatter.23
  3562.8 263.3 reduce-scatter.25
where the time goes:
time: 3840 us; the launch traced here: 3830 us
  waiting for transfers between devices  3270 us (85%)
  matrix products  263 us (7%)
  blocking collectives  116 us (3%)
  local copies, waits for them, and re-layouts  101 us (3%)
  other arithmetic  64.2 us (2%)
    reduce_scatter x1, waiting for transfers between devices, body(): lax.psum_scatter(grad_w_pool, ('clip', 'seq'), scatter_dimension=0, tiled...  360 us
    reduce_scatter x1, waiting for transfers between devices, body(): lax.psum_scatter(grad_w_qkv, ('clip', 'seq'), scatter_dimension=0, tiled=...  271 us
    reduce_scatter x1, waiting for transfers between devices, body(): lax.psum_scatter(grad_w_down, ('clip', 'seq'), scatter_dimension=0, tiled...  253 us
    reduce_scatter x1, waiting for transfers between devices, body(): lax.psum_scatter(grad_w_gate, ('clip', 'seq'), scatter_dimension=0, tiled...  253 us
    reduce_scatter x1, waiting for transfers between devices, body(): lax.psum_scatter(grad_w_up, ('clip', 'seq'), scatter_dimension=0, tiled=T...  252 us
    reduce_scatter x1, waiting for transfers between devices, body(): lax.psum_scatter(grad_w_ada, ('clip', 'seq'), scatter_dimension=0, tiled=...  252 us
    reduce_scatter x1, waiting for transfers between devices, body(): lax.psum_scatter(grad_w_value_text, ('clip', 'seq'), scatter_dimension=0,...  247 us
    reduce_scatter x1, waiting for transfers between devices, body(): lax.psum_scatter(grad_w_key_text, ('clip', 'seq'), scatter_dimension=0, t...  158 us
  transfers between devices with their start and end apart: 26, of which 24 were waited for; matrix products, arithmetic and copies ran while one was open for 8% of the time, Pallas kernels for 0%

commit v1 on v0

v1 whole, which is shorter than its diff:
```python
import math

import jax
import jax.numpy as jnp
from jax import lax
from jax.sharding import Mesh
from jax.sharding import PartitionSpec as P

epsilon = 1e-05
head_eps = 1e-06
big_negative = -1e30
f32 = jnp.float32
bf16 = jnp.bfloat16


def rope_tables(posint, half_dim):
    pair_ids = jnp.arange(half_dim)
    first_cut = half_dim // 4
    second_cut = first_cut + (half_dim - first_cut) // 2
    group_of = (pair_ids >= first_cut).astype(jnp.int32) + (pair_ids >= second_cut).astype(
        jnp.int32
    )
    starts = jnp.where(group_of == 0, 0, jnp.where(group_of == 1, first_cut, second_cut))
    counts = jnp.where(
        group_of == 0,
        first_cut,
        jnp.where(group_of == 1, second_cut - first_cut, half_dim - second_cut),
    )
    frequency = jnp.exp(
        -math.log(10000.0) * (pair_ids - starts).astype(f32) / counts.astype(f32)
    )
    spots = posint.astype(f32)[:, :, None]
    coords = jnp.where(group_of == 0, spots[0], jnp.where(group_of == 1, spots[1], spots[2]))
    angles = coords * frequency[None, :]
    return (jnp.cos(angles), jnp.sin(angles))


def rotate(vector, cos_tab, sin_tab):
    half_dim = cos_tab.shape[-1]
    front = vector[..., :half_dim]
    behind = vector[..., half_dim:]
    return jnp.concatenate(
        [front * cos_tab - behind * sin_tab, front * sin_tab + behind * cos_tab], -1
    )


def rms_norm(vector, eps_value):
    inverse = lax.rsqrt(jnp.mean(vector * vector, -1, keepdims=True) + eps_value)
    return (vector * inverse, inverse)


def norm_back(normed, inverse, gradient):
    return inverse * (gradient - normed * jnp.mean(gradient * normed, -1, keepdims=True))


def timestep_embed(time_step, embed_width):
    half_dim = embed_width // 2
    frequency = jnp.exp(-math.log(10000.0) * jnp.arange(half_dim, dtype=f32) / half_dim)
    angles = time_step.astype(f32)[..., None] * frequency
    return jnp.concatenate([jnp.cos(angles), jnp.sin(angles)], -1)


def dot(a, b):
    return jnp.dot(a, b, preferred_element_type=f32)


def dot_tn(a, b):
    return lax.dot_general(a, b, (((0,), (0,)), ((), ())), preferred_element_type=f32)


def dot_nt(a, b):
    return lax.dot_general(a, b, (((1,), (1,)), ((), ())), preferred_element_type=f32)


def ein(spec, a, b):
    return jnp.einsum(spec, a, b, preferred_element_type=f32)


def make_body(clips, outer, inner):
    shards = clips * outer
    team = "inner"
    spread = ("clip", "outer") if outer > 1 else "clip"
    whole_clip = ("outer", "inner") if outer > 1 else "inner"

    def gather_team(x):
        return lax.all_gather(x, team, axis=0, tiled=True)

    def scatter_team(x):
        return lax.psum_scatter(x, team, scatter_dimension=0, tiled=True)

    def swap_team(x):
        return lax.all_to_all(x, team, split_axis=0, concat_axis=0, tiled=True)

    def gather_spread(x):
        return lax.all_gather(x, spread, axis=0, tiled=True)

    def scatter_spread(x):
        return lax.psum_scatter(x, spread, scatter_dimension=0, tiled=True)

    def by_columns(w):
        rows, columns = w.shape
        blocks = w.reshape(rows, shards, inner, columns // (shards * inner))
        return blocks.transpose(2, 0, 1, 3).reshape(inner, rows, columns // inner)

    def back_columns(w):
        _, rows, columns = w.shape
        blocks = w.reshape(inner, rows, shards, columns // shards)
        return blocks.transpose(1, 2, 0, 3).reshape(rows, inner * columns)

    def body(
        tokens,
        caption,
        lengths,
        timesteps,
        positions,
        w_time,
        w_pool,
        w_ada,
        b_ada,
        norm1_gain,
        w_qkv,
        w_key_text,
        w_value_text,
        cross_gate,
        w_out,
        norm2_gain,
        w_gate,
        w_up,
        w_down,
        cotangent,
    ):
        head_count = cross_gate.shape[0]
        width = tokens.shape[2]
        head_dim = width // head_count
        heads = head_count // inner
        own = heads * head_dim
        tok_rows = tokens.shape[1]
        team_rows = tok_rows * inner
        cap_rows = caption.shape[1]
        cond_width = w_pool.shape[1]
        mod_width = b_ada.shape[0]
        mod_own = mod_width // inner
        attn_scale = 1.0 / math.sqrt(head_dim)
        member = lax.axis_index(team)
        shard = lax.axis_index(spread)
        length_f = lengths[0].astype(f32)

        cap_part = swap_team(by_columns(caption[0])).reshape(inner * cap_rows, -1)
        cap_own = cap_part
        if outer > 1:
            cap_part = lax.all_gather(cap_part, "outer", axis=0, tiled=True)
        cap_len = cap_part.shape[0]
        pool_s = gather_spread(w_pool)
        time_s = gather_spread(w_time)
        rows = w_ada.shape[0]
        ada_blocks = w_ada.reshape(rows, inner, mod_own).transpose(1, 0, 2)
        ada_s = gather_spread(swap_team(ada_blocks).reshape(inner * rows, mod_own))
        rows = w_qkv.shape[0]
        qkv_blocks = w_qkv.reshape(rows, 3, inner, own).transpose(2, 0, 1, 3)
        qkv_blocks = qkv_blocks.reshape(inner, rows, 3 * own)
        qkv_s = gather_spread(swap_team(qkv_blocks).reshape(inner * rows, 3 * own))
        tokens_all = gather_team(tokens[0])
        spots = lax.all_gather(positions[:, 0, :], team, axis=1, tiled=True)
        text_s = gather_spread(jnp.concatenate([w_key_text, w_value_text], -1))
        to_heads = [
            (r, (r % shards) * inner + r // shards) for r in range(shards * inner)
        ]
        from_heads = [(b, a) for a, b in to_heads]
        every = ("clip", "outer", "inner")
        out_s = gather_spread(lax.ppermute(w_out, every, to_heads))
        ffn_blocks = jnp.concatenate([by_columns(w_gate), by_columns(w_up)], -1)
        ffn_s = gather_spread(swap_team(ffn_blocks).reshape(inner * rows, -1))
        down_s = gather_spread(w_down)
        ff_own = down_s.shape[0]
        cot_all = gather_team(cotangent[0])

        cap_mask = (jnp.arange(cap_len) < lengths[0]).astype(f32)
        pooled = jnp.sum(cap_part.astype(f32) * cap_mask[:, None], 0) / length_f
        pooled_b = pooled.astype(bf16)
        time_rows = w_time.shape[0]
        embed_width = time_rows * shards * inner
        time_embed = timestep_embed(timesteps[0], embed_width).astype(bf16)
        time_own = lax.dynamic_index_in_dim(
            time_embed.reshape(shards, inner, time_rows), member, 1, keepdims=False
        ).reshape(1, -1)
        condition = lax.psum(dot(pooled_b[None], pool_s) + dot(time_own, time_s), team)
        cond_b = jax.nn.silu(condition).astype(bf16)
        bias_own = lax.dynamic_slice_in_dim(b_ada, member * mod_own, mod_own)
        modulation = gather_team(dot(cond_b, ada_s)[0] + bias_own)
        scale_attn, gate_attn, scale_ffn, gate_ffn = jnp.split(modulation, 4)
        tanh_attn = jnp.tanh(gate_attn)
        tanh_ffn = jnp.tanh(gate_ffn)
        packed = jnp.concatenate(
            [
                modulation,
                condition[0],
                pooled,
                jnp.full((128,), timesteps[0].astype(f32)),
            ]
        )
        clip_facts = lax.all_gather(packed.reshape(-1, 128), "clip", axis=0).reshape(clips, -1)

        normed_all, _ = rms_norm(tokens_all.astype(f32), epsilon)
        gain1 = norm1_gain * (1.0 + scale_attn)
        mix_in = (normed_all * gain1).astype(bf16)
        qkv_own = dot(mix_in, qkv_s).reshape(team_rows, 3, heads, head_dim).transpose(1, 2, 0, 3)
        cos_tab, sin_tab = rope_tables(spots, head_dim // 2)
        queries_n, inverse_q = rms_norm(qkv_own[0], head_eps)
        keys_n, inverse_k = rms_norm(qkv_own[1], head_eps)
        queries_b = rotate(queries_n, cos_tab, sin_tab).astype(bf16)
        keys_b = rotate(keys_n, cos_tab, sin_tab).astype(bf16)
        values_b = qkv_own[2].astype(bf16)
        if outer > 1:
            keys_b = lax.all_gather(keys_b, "outer", axis=1, tiled=True)
            values_b = lax.all_gather(values_b, "outer", axis=1, tiled=True)
        scores = ein("hqd,hkd->hqk", queries_b, keys_b) * attn_scale
        top = jnp.max(scores, -1, keepdims=True)
        raised = jnp.exp(scores - top)
        total = jnp.sum(raised, -1, keepdims=True)
        self_out = ein("hqk,hkd->hqd", raised.astype(bf16), values_b) / total
        log_sum = top + jnp.log(total)

        text_part = dot(cap_part, text_s).astype(bf16)
        text_part = text_part.reshape(cap_len, 2, inner, own).transpose(2, 0, 1, 3)
        text_own = scatter_team(text_part.reshape(inner * cap_len, 2 * own)).astype(f32)
        text_own = text_own.reshape(cap_len, 2, heads, head_dim).transpose(1, 2, 0, 3)
        text_keys_n, inverse_t = rms_norm(text_own[0], head_eps)
        keys_text_b = text_keys_n.astype(bf16)
        values_text_b = text_own[1].astype(bf16)
        cross_scores = ein("hqd,hkd->hqk", queries_b, keys_text_b) * attn_scale
        cross_scores = jnp.where(cap_mask > 0, cross_scores, big_negative)
        cross_probs = jax.nn.softmax(cross_scores, axis=-1)
        cross_probs_b = cross_probs.astype(bf16)
        cross_out = ein("hqk,hkd->hqd", cross_probs_b, values_text_b)
        gate_own = jnp.tanh(lax.dynamic_slice_in_dim(cross_gate, member * heads, heads))
        gate_t = gate_own[:, None, None]
        mixed = self_out + gate_t * cross_out
        mixed_b = mixed.transpose(1, 0, 2).reshape(team_rows, own).astype(bf16)
        attn_out = scatter_team(dot(mixed_b, out_s).astype(bf16)).astype(f32)

        tokens_f = tokens[0].astype(f32)
        normed1, inverse1 = rms_norm(tokens_f, epsilon)
        resid = tokens_f + tanh_attn * attn_out
        normed2, inverse2 = rms_norm(resid, epsilon)
        gain2 = norm2_gain * (1.0 + scale_ffn)
        ffn_in = gather_team((normed2 * gain2).astype(bf16))
        gate_up = dot(ffn_in, ffn_s)
        gate_pre, up_pre = gate_up[:, :ff_own], gate_up[:, ff_own:]
        sigmoid_g = jax.nn.sigmoid(gate_pre)
        silu_g = gate_pre * sigmoid_g
        hidden_b = (silu_g * up_pre).astype(bf16)
        d_ffn_b = (tanh_ffn * cot_all.astype(f32)).astype(bf16)
        d_hidden = dot_nt(d_ffn_b, down_s)
        silu_slope = sigmoid_g * (1.0 + gate_pre * (1.0 - sigmoid_g))
        d_gate_up = jnp.concatenate(
            [
                (d_hidden * up_pre * silu_slope).astype(bf16),
                (d_hidden * silu_g).astype(bf16),
            ],
            -1,
        )
        d_ffn_in = scatter_team(dot_nt(d_gate_up, ffn_s).astype(bf16)).astype(f32)
        ffn_out = scatter_team(dot(hidden_b, down_s).astype(bf16)).astype(f32)
        mixed_out = (resid + tanh_ffn * ffn_out).astype(bf16)
        d_out = cotangent[0].astype(f32)
        sum_gate_ffn = jnp.sum(d_out * ffn_out, 0)
        sum_down = scatter_spread(dot_tn(hidden_b, d_ffn_b).astype(bf16)).astype(f32)
        sum_ffn = scatter_spread(dot_tn(ffn_in, d_gate_up).astype(bf16))
        sum_ffn = swap_team(sum_ffn.reshape(inner, rows, 2 * ff_own))
        sum_gate = back_columns(sum_ffn[:, :, :ff_own]).astype(f32)
        sum_up = back_columns(sum_ffn[:, :, ff_own:]).astype(f32)

        sum_norm2 = jnp.sum(d_ffn_in * normed2, 0)
        d_resid = d_out + norm_back(normed2, inverse2, d_ffn_in * gain2)
        sum_gate_attn = jnp.sum(d_resid * attn_out, 0)
        d_attn_b = gather_team((tanh_attn * d_resid).astype(bf16))
        grad_out = dot_tn(mixed_b, d_attn_b).astype(bf16)
        sum_out = lax.ppermute(scatter_spread(grad_out), every, from_heads).astype(f32)
        d_mixed = dot_nt(d_attn_b, out_s).reshape(team_rows, heads, head_dim).transpose(1, 0, 2)
        grad_cross = jnp.sum(d_mixed * cross_out, axis=(1, 2)) * (1.0 - gate_own * gate_own)
        d_self_b = d_mixed.astype(bf16)
        d_cross_b = (gate_t * d_mixed).astype(bf16)

        d_cross_probs = ein("hqd,hkd->hqk", d_cross_b, values_text_b)
        d_cross_scores = (
            cross_probs
            * (d_cross_probs - jnp.sum(cross_probs * d_cross_probs, -1, keepdims=True))
        ).astype(bf16)
        d_queries = ein("hqk,hkd->hqd", d_cross_scores, keys_text_b)
        d_text_keys_n = ein("hqk,hqd->hkd", d_cross_scores, queries_b) * attn_scale
        d_text_values = ein("hqk,hqd->hkd", cross_probs_b, d_cross_b)
        if outer > 1:
            d_text_keys_n = lax.psum(d_text_keys_n, "outer")
            d_text_values = lax.psum(d_text_values, "outer")
        d_text_keys = norm_back(text_keys_n, inverse_t, d_text_keys_n)
        text_grads = jnp.stack([d_text_keys, d_text_values]).transpose(2, 0, 1, 3)
        text_grads = text_grads.reshape(cap_len, 2 * own).astype(bf16)
        if outer > 1:
            text_grads = lax.dynamic_slice_in_dim(
                text_grads, lax.axis_index("outer") * inner * cap_rows, inner * cap_rows
            )
        text_rows = text_grads.shape[0]
        text_grads = gather_team(text_grads).reshape(inner, text_rows, 2, own)
        text_grads = text_grads.transpose(1, 2, 0, 3).reshape(text_rows, 2 * width)
        sum_text = scatter_spread(dot_tn(cap_own, text_grads).astype(bf16)).astype(f32)
        d_cap = dot_nt(text_grads, text_s).astype(bf16).reshape(inner, cap_rows, -1)
        d_cap = back_columns(swap_team(d_cap)).astype(f32)

        row_dots = jnp.sum(d_self_b.astype(f32) * self_out, -1, keepdims=True)
        soft_probs = jnp.exp(scores - log_sum)
        d_probs = ein("hqd,hkd->hqk", d_self_b, values_b)
        d_scores_b = (soft_probs * (d_probs - row_dots)).astype(bf16)
        d_queries = (d_queries + ein("hqk,hkd->hqd", d_scores_b, keys_b)) * attn_scale
        d_keys = ein("hqk,hqd->hkd", d_scores_b, queries_b) * attn_scale
        d_values = ein("hqk,hqd->hkd", soft_probs.astype(bf16), d_self_b)
        if outer > 1:
            d_keys = lax.psum_scatter(d_keys, "outer", scatter_dimension=1, tiled=True)
            d_values = lax.psum_scatter(d_values, "outer", scatter_dimension=1, tiled=True)
        d_queries_raw = norm_back(queries_n, inverse_q, rotate(d_queries, cos_tab, -sin_tab))
        d_keys_raw = norm_back(keys_n, inverse_k, rotate(d_keys, cos_tab, -sin_tab))
        d_qkv = jnp.stack([d_queries_raw, d_keys_raw, d_values]).astype(bf16)
        d_qkv = d_qkv.transpose(2, 0, 1, 3).reshape(team_rows, 3 * own)
        d_mix_in = scatter_team(dot_nt(d_qkv, qkv_s).astype(bf16)).astype(f32)
        sum_qkv = scatter_spread(dot_tn(mix_in, d_qkv).astype(bf16))
        sum_qkv = swap_team(sum_qkv.reshape(inner, rows, 3 * own)).reshape(inner, rows, 3, own)
        sum_qkv = sum_qkv.transpose(1, 2, 0, 3).reshape(rows, 3 * width).astype(f32)

        sum_norm1 = jnp.sum(d_mix_in * normed1, 0)
        d_tokens = d_resid + norm_back(normed1, inverse1, d_mix_in * gain1)

        cross_slots = jnp.zeros((128,), f32)
        cross_slots = lax.dynamic_update_slice_in_dim(cross_slots, grad_cross, member * heads, 0)
        sums = jnp.concatenate(
            [sum_norm1, sum_gate_attn, sum_norm2, sum_gate_ffn, cross_slots]
        ).reshape(-1, 128)
        sums = lax.psum(sums, whole_clip)
        sums = lax.all_gather(sums, "clip", axis=0).reshape(clips, -1)
        mods = clip_facts[:, :mod_width].reshape(clips, 4, width)
        at = mod_width
        cond_all = clip_facts[:, at : at + cond_width]
        at += cond_width
        pool_all = clip_facts[:, at : at + pooled.shape[0]]
        steps_all = clip_facts[:, at + pooled.shape[0]]
        token_sums = sums[:, :mod_width].reshape(clips, 4, width)
        grad_norm1 = jnp.sum(token_sums[:, 0] * (1.0 + mods[:, 0]), 0)
        grad_norm2 = jnp.sum(token_sums[:, 2] * (1.0 + mods[:, 2]), 0)
        tanh1, tanh3 = jnp.tanh(mods[:, 1]), jnp.tanh(mods[:, 3])
        d_modulation = jnp.concatenate(
            [
                token_sums[:, 0] * norm1_gain,
                token_sums[:, 1] * (1.0 - tanh1 * tanh1),
                token_sums[:, 2] * norm2_gain,
                token_sums[:, 3] * (1.0 - tanh3 * tanh3),
            ],
            -1,
        )
        grad_bias = jnp.sum(d_modulation, 0)
        grad_cross_gate = jnp.sum(sums[:, mod_width : mod_width + head_count], 0)
        row = shard * inner + member
        ada_rows = w_ada.shape[0]
        cond_rows = lax.dynamic_slice_in_dim(
            jax.nn.silu(cond_all).astype(bf16).astype(f32), row * ada_rows, ada_rows, 1
        )
        sum_ada = jnp.sum(cond_rows[:, :, None] * d_modulation[:, None, :], 0)
        d_mod_clip = lax.dynamic_index_in_dim(d_modulation, lax.axis_index("clip"), 0)
        d_mod_own = lax.dynamic_slice_in_dim(d_mod_clip, member * mod_own, mod_own, 1)
        d_cond_act = lax.psum(dot_nt(d_mod_own.astype(bf16), ada_s), team)
        sigmoid_c = jax.nn.sigmoid(condition)
        d_condition = d_cond_act * sigmoid_c * (1.0 + condition * (1.0 - sigmoid_c))
        d_cond_all = lax.all_gather(d_condition[0], "clip", axis=0)
        d_pooled = gather_team(dot_nt(d_condition.astype(bf16), pool_s)[0])
        d_pooled = d_pooled.reshape(inner, shards, -1).transpose(1, 0, 2).reshape(1, -1)
        seq_row = lax.axis_index(whole_clip)
        local_mask = (seq_row * cap_rows + jnp.arange(cap_rows) < lengths[0]).astype(f32)
        d_caption = d_cap + local_mask[:, None] * d_pooled / length_f
        embed_all = timestep_embed(steps_all, embed_width).astype(bf16).astype(f32)
        embed_rows = lax.dynamic_slice_in_dim(embed_all, row * time_rows, time_rows, 1)
        sum_time = jnp.sum(embed_rows[:, :, None] * d_cond_all[:, None, :], 0)
        pool_rows = lax.dynamic_slice_in_dim(
            pool_all.astype(bf16).astype(f32), shard * w_pool.shape[0], w_pool.shape[0], 1
        )
        sum_pool = jnp.sum(pool_rows[:, :, None] * d_cond_all[:, None, :], 0)
        return (
            mixed_out[None],
            d_tokens[None],
            d_caption[None],
            sum_time,
            sum_pool,
            sum_ada,
            grad_bias,
            grad_norm1,
            sum_qkv,
            sum_text[:, :width],
            sum_text[:, width:],
            grad_cross_gate,
            sum_out,
            grad_norm2,
            sum_gate,
            sum_up,
            sum_down,
        )

    return body


def solution(mesh):
    clips, members = mesh.shape["clip"], mesh.shape["seq"]

    def run(*args):
        inner = math.gcd(args[13].shape[0], members)
        outer = members // inner
        fine = Mesh(mesh.devices.reshape(clips, outer, inner), ("clip", "outer", "inner"))
        seq = ("outer", "inner")
        every = P(("clip", "outer", "inner"), None)
        by_token = P("clip", seq, None)
        return jax.shard_map(
            make_body(clips, outer, inner),
            mesh=fine,
            in_specs=(
                by_token,
                by_token,
                P("clip"),
                P("clip"),
                P(None, "clip", seq),
                every,
                every,
                every,
                P(),
                P(),
                every,
                every,
                every,
                P(),
                every,
                P(),
                every,
                every,
                every,
                by_token,
            ),
            out_specs=(
                by_token,
                by_token,
                by_token,
                every,
                every,
                every,
                P(),
                P(),
                every,
                every,
                every,
                P(),
                every,
                P(),
                every,
                every,
                every,
            ),
            check_vma=False,
        )(*args)

    return run
```

time: 3840 us -> 1150 us (0.30)
  waiting for transfers between devices: 3270 us -> 639 us
  matrix products: 263 us -> 108 us
  blocking collectives: 116 us -> 247 us
  local copies, waits for them, and re-layouts: 101 us -> 54.3 us
    reduce_scatter x11 -> x9, waiting for transfers between devices: 2380 us -> 361 us  [the longest x5 314 us: scatter_team(): return lax.psum_scatter(x, team, scatter_dimension=0, tiled=True)]
    all_gather x12 -> x11, waiting for transfers between devices: 818 us -> 268 us  [the longest x5 213 us: gather_team(): return lax.all_gather(x, team, axis=0, tiled=True)]
    dot_general x47 -> x31, matrix products: 263 us -> 104 us  [the longest x11 29.3 us: ein(): return jnp.einsum(spec, a, b, preferred_element_type=f32)]
    unnamed x29 -> x22, waiting for transfers between devices: 74.3 us -> 3.21 us
    all_to_all x0 -> x2, blocking collectives: none -> 60.2 us  [swap_team(): return lax.all_to_all(x, team, split_axis=0, concat_axis=0, tiled=True)]
    all_gather x1 -> x8, blocking collectives: 75.2 us -> 112 us  [the longest x2 56.8 us: gather_team(): return lax.all_gather(x, team, axis=0, tiled=True)]
  transfers between devices with their start and end apart: 26 -> 28, of which waited for: 24 -> 16; matrix products, arithmetic and copies ran while one was open for 8% -> 14% of each run, Pallas kernels for 0% -> 0%
where the time goes in v1:
time: 1150 us; the launch traced here: 1140 us
  waiting for transfers between devices  639 us (56%)
  blocking collectives  247 us (21%)
  matrix products  108 us (9%)
  local copies, waits for them, and re-layouts  54.3 us (5%)
  other arithmetic  47.3 us (4%)
  starting transfers between devices  26.7 us (2%)
  between operations  17.6 us (2%)
    reduce_scatter x5, waiting for transfers between devices, scatter_team(): return lax.psum_scatter(x, team, scatter_dimension=0, tiled=True)  314 us
    all_gather x5, waiting for transfers between devices, gather_team(): return lax.all_gather(x, team, axis=0, tiled=True)  213 us
    all_to_all x2, blocking collectives, swap_team(): return lax.all_to_all(x, team, split_axis=0, concat_axis=0, tiled=True)  60.2 us
    all_gather x2, blocking collectives, gather_team(): return lax.all_gather(x, team, axis=0, tiled=True)  56.8 us
    all_gather x6, waiting for transfers between devices, gather_spread(): return lax.all_gather(x, spread, axis=0, tiled=True)  54.9 us
    reduce_scatter x4, waiting for transfers between devices, scatter_spread(): return lax.psum_scatter(x, spread, scatter_dimension=0, tiled=True)  47.4 us
    unnamed x225, local copies, waits for them, and re-layouts  38.1 us
    psum x1, blocking collectives, body(): sums = lax.psum(sums, whole_clip)  35.9 us
  transfers between devices with their start and end apart: 28, of which 16 were waited for; matrix products, arithmetic and copies ran while one was open for 14% of the time, Pallas kernels for 0%

profile of v1, /device:TPU:0, one launch (start us, length us, event | category | flops | bytes accessed | tf_op | source)
XLA Modules:
  0.0 1139.2 jit_solution(5549040213062144296)
XLA Ops:
  9.1 19.2 %all_to_all.35 = bf16[8,32,768]{2,1,0:T(8,128)(2,1)} all-to-all(bf16[8,32,768]{2,1,0:T(8,128)(2,1)S(1)} %copy.235), channel_id=1, replica_groups=mesh['clip'=4,'seq'=8] {'seq'}, dimensions={0} | all-to-all | bytes 786432 | tf_op jit(solution)/shard_map/all_to_all | solution.py:92
  32.2 3.5 all-to-all-start.2
  38.1 23.0 %all-gather.1 = s32[3,1,1024]{2,1,0:T(1,128)S(1)} all-gather(s32[3,1,128]{2,1,0:T(1,128)S(1)} %copy-done.83), channel_id=3, replica_groups=mesh['clip'=4,'seq'=8] {'seq'}, dimensions={2}, use_global_device_ids=true | all-gather | bytes 13824 | tf_op jit(solution)/shard_map/all_gather | solution.py:163
  61.2 6.2 all-to-all-start
  68.8 5.6 all_gather.61
  77.0 10.0 all_gather.68
  89.4 21.5 %psum.21 = f32[1,1024]{1,0:T(1,128)S(1)} all-reduce(f32[1,1024]{1,0:T(1,128)S(1)} %bitcast.415), channel_id=1, replica_groups=mesh['clip'=4,'seq'=8] {'seq'}, use_global_device_ids=true, to_apply=%region_1.2 | all-reduce | flops 1024 | bytes 8192 | tf_op jit(solution)/shard_map/psum | solution.py:186
  113.5 30.7 %all-gather.3 = f32[8,1,768]{2,1,0:T(1,128)S(1)} all-gather(f32[1,1,768]{2,1,0:T(1,128)S(1)} %reshape.702), channel_id=1, replica_groups=mesh['clip'=4,'seq'=8] {'seq'}, dimensions={0}, use_global_device_ids=true | all-gather | bytes 27648 | tf_op jit(solution)/shard_map/all_gather | solution.py:86
  153.3 18.7 %all-gather.22.cloned.1.call-done = bf16[1536,576]{1,0:T(8,128)(2,1)} async-done(((bf16[384,576]{1,0:T(8,128)(2,1)}), bf16[1536,576]{1,0:T(8,128)(2,1)}) %all-gather.22.cloned.1.call-update) | async-done | bytes 1769488 | tf_op jit(solution)/shard_map/all_gather | solution.py:95
  172.0 4.7 fusion.36
  180.5 4.5 copy-done
  187.3 53.7 %reduce-scatter.15.cloned.1.call-done = bf16[256,384]{0,1:T(8,128)(2,1)} async-done(((bf16[2048,384]{0,1:T(8,128)(2,1)}), bf16[256,384]{0,1:T(8,128)(2,1)}) %reduce-scatter.15.cloned.1.call-update) | async-done | bytes 196624 | tf_op jit(solution)/shard_map/reduce_scatter | solution.py:89
  242.5 4.4 fusion.151
  249.4 8.0 fusion.57
  262.4 41.0 %all_to_all.36 = bf16[8,48,1024]{2,1,0:T(8,128)(2,1)} all-to-all(bf16[8,48,1024]{2,1,0:T(8,128)(2,1)S(1)} %pad_maximum_fusion.5), channel_id=1, replica_groups=mesh['clip'=4,'seq'=8] {'seq'}, dimensions={0} | all-to-all | bytes 1572864 | tf_op jit(solution)/shard_map/all_to_all | solution.py:92
  303.5 45.7 %reduce-scatter.17.cloned.1.call-done = bf16[128,1536]{1,0:T(8,128)(2,1)} async-done(((bf16[1024,1536]{1,0:T(8,128)(2,1)}), bf16[128,1536]{1,0:T(8,128)(2,1)}) %reduce-scatter.17.cloned.1.call-update) | async-done | bytes 393232 | tf_op jit(solution)/shard_map/reduce_scatter | solution.py:89
  353.8 24.7 %all-gather.28.cloned.1.call-done = bf16[1536,1024]{1,0:T(8,128)(2,1)} async-done(((bf16[384,1024]{1,0:T(8,128)(2,1)}), bf16[1536,1024]{1,0:T(8,128)(2,1)}) %all-gather.28.cloned.1.call-update) | async-done | bytes 3145744 | tf_op jit(solution)/shard_map/all_gather | solution.py:95
  378.5 63.5 %all-gather.26.cloned.1.call-done = bf16[1024,1536]{1,0:T(8,128)(2,1)} async-done(((bf16[128,1536]{1,0:T(8,128)(2,1)}), bf16[1024,1536]{1,0:T(8,128)(2,1)}) %all-gather.26.cloned.1.call-update) | async-done | bytes 3145744 | tf_op jit(solution)/shard_map/all_gather | solution.py:86
  441.9 8.2 fusion.158
  450.2 11.6 %all-gather.30.cloned.1.call-done = bf16[512,1536]{1,0:T(8,128)(2,1)} async-done(((bf16[128,1536]{1,0:T(8,128)(2,1)}), bf16[512,1536]{1,0:T(8,128)(2,1)}) %all-gather.30.cloned.1.call-update) | async-done | bytes 1572880 | tf_op jit(solution)/shard_map/all_gather | solution.py:95
  461.7 62.9 %all-gather.38.cloned.1.call-done = bf16[1,1024,1536]{2,1,0:T(8,128)(2,1)} async-done(((bf16[1,128,1536]{2,1,0:T(8,128)(2,1)}), bf16[1,1024,1536]{2,1,0:T(8,128)(2,1)}) %all-gather.38.cloned.1.call-update) | async-done | bytes 3145744 | tf_op jit(solution)/shard_map/all_gather | solution.py:86
  524.7 7.3 multiply_convert_fusion.3
  533.2 5.0 convolution_convert_fusion.6
  539.6 4.7 convolution_convert_fusion.4
  544.6 66.7 %reduce-scatter.21.cloned.1.call-done = bf16[128,1536]{1,0:T(8,128)(2,1)} async-done(((bf16[1024,1536]{1,0:T(8,128)(2,1)}), bf16[128,1536]{1,0:T(8,128)(2,1)}) %reduce-scatter.21.cloned.1.call-update) | async-done | bytes 393232 | tf_op jit(solution)/shard_map/reduce_scatter | solution.py:89
  612.7 76.4 %reduce-scatter.19.cloned.1.call-done = bf16[128,1536]{1,0:T(8,128)(2,1)} async-done(((bf16[1024,1536]{1,0:T(8,128)(2,1)}), bf16[128,1536]{1,0:T(8,128)(2,1)}) %reduce-scatter.19.cloned.1.call-update) | async-done | bytes 393232 | tf_op jit(solution)/shard_map/reduce_scatter | solution.py:89
  692.5 7.7 convolution_convert_fusion.5
  700.9 51.2 %all-gather.32.cloned.1.call-done = bf16[1024,1536]{1,0:T(8,128)(2,1)} async-done(((bf16[128,1536]{1,0:T(8,128)(2,1)}), bf16[1024,1536]{1,0:T(8,128)(2,1)}) %all-gather.32.cloned.1.call-update) | async-done | bytes 3145744 | tf_op jit(solution)/shard_map/all_gather | solution.py:86
  763.8 6.5 multiply_convert_fusion
  779.5 4.0 convolution_convert_fusion.7
  785.9 5.4 convolution_convert_fusion.8
  791.3 3.5 convolution_convert_fusion.9
  795.2 5.7 convolution_convert_fusion.2
  800.9 4.2 all-to-all-start.6
  806.4 5.4 all_gather.77
  812.5 35.0 %all-gather.34.cloned.1.call-done = bf16[2048,384]{0,1:T(8,128)(2,1)} async-done(((bf16[256,384]{0,1:T(8,128)(2,1)}), bf16[2048,384]{0,1:T(8,128)(2,1)}) %all-gather.34.cloned.1.call-update) | async-done | bytes 1572880 | tf_op jit(solution)/shard_map/all_gather | solution.py:86
  856.7 3.7 convolution_convert_fusion.10
  865.4 7.2 all-to-all-done.4
  872.6 6.2 reduce-scatter.31.cloned.1.call-done
  878.8 5.4 all-to-all-start.5
  885.6 23.9 %reduce-scatter.29.cloned.1.call-done = bf16[128,1536]{1,0:T(8,128)(2,1)} async-done(((bf16[512,1536]{1,0:T(8,128)(2,1)}), bf16[128,1536]{1,0:T(8,128)(2,1)}) %reduce-scatter.29.cloned.1.call-update) | async-done | bytes 393232 | tf_op jit(solution)/shard_map/reduce_scatter | solution.py:98
  917.5 17.2 %reduce-scatter.25.cloned.1.call-done = bf16[48,1536]{1,0:T(8,128)(2,1)} async-done(((bf16[192,1536]{1,0:T(8,128)(2,1)}), bf16[48,1536]{1,0:T(8,128)(2,1)}) %reduce-scatter.25.cloned.1.call-update) | async-done | bytes 147472 | tf_op jit(solution)/shard_map/reduce_scatter | solution.py:98
  944.0 71.1 %reduce-scatter.23.cloned.1.call-done = bf16[128,1536]{1,0:T(8,128)(2,1)} async-done(((bf16[1024,1536]{1,0:T(8,128)(2,1)}), bf16[128,1536]{1,0:T(8,128)(2,1)}) %reduce-scatter.23.cloned.1.call-update) | async-done | bytes 393232 | tf_op jit(solution)/shard_map/reduce_scatter | solution.py:89
  1023.5 35.9 %psum.22 = f32[1,49,128]{2,1,0:T(8,128)S(1)} all-reduce(f32[1,49,128]{2,1,0:T(8,128)} %bitcast.409), channel_id=1, replica_groups=mesh['clip'=4,'seq'=8] {'seq'}, use_global_device_ids=true, to_apply=%region_29.30 | all-reduce | flops 6272 | bytes 50176 | tf_op jit(solution)/shard_map/psum | solution.py:336
  1059.4 5.7 all_gather.76
  1068.6 17.3 %psum.23 = f32[1,1024]{1,0:T(1,128)S(1)} all-reduce(f32[1,1024]{1,0:T(1,128)S(1)} %fusion.118), channel_id=1, replica_groups=mesh['clip'=4,'seq'=8] {'seq'}, use_global_device_ids=true, to_apply=%region_30.31 | all-reduce | flops 1024 | bytes 8192 | tf_op jit(solution)/shard_map/psum | solution.py:367
  1085.9 5.2 all-gather.5
  1091.5 26.0 %all-gather.4 = f32[8,1,512]{2,1,0:T(1,128)S(1)} all-gather(f32[1,1,512]{2,1,0:T(1,128)S(1)} %convolution_bitcast_fusion), channel_id=1, replica_groups=mesh['clip'=4,'seq'=8] {'seq'}, dimensions={0}, use_global_device_ids=true | all-gather | bytes 18432 | tf_op jit(solution)/shard_map/all_gather | solution.py:86
  (411 shorter events, 136.8 us)
Async XLA Ops:
  7.2 80.7 %all-gather.18.cloned.1.call-start = ((), (), s32[]{:S(2)}) async-start(), calls=%async_computation.17 | async-start | bytes 1310720 | tf_op jit(solution)/shard_map/all_gather | solution.py:95
  8.0 103.0 %all-gather.20.cloned.1.call-start = ((), (), s32[]{:S(2)}) async-start(), calls=%async_computation.18 | async-start | bytes 1966080 | tf_op jit(solution)/shard_map/all_gather | solution.py:95
  28.4 116.5 %all-gather.24.cloned.1.call-start = ((), (), s32[]{:S(2)}) async-start(), calls=%async_computation.20 | async-start | bytes 3932160 | tf_op jit(solution)/shard_map/all_gather | solution.py:95
  29.5 121.3 %all-gather.36.cloned.1.call-start = ((), (), s32[]{:S(2)}) async-start(), calls=%async_computation.34 | async-start | bytes 3538944 | tf_op jit(solution)/shard_map/all_gather | solution.py:86
  32.2 29.0 %all-to-all-start.2 = ((bf16[8,48,576]{2,1,0:T(8,128)(2,1)}), bf16[8,48,576]{2,1,0:T(8,128)(2,1)S(1)}, u32[]{:S(2)}, u32[]{:S(2)}) async-start(bf16[8,48,576]{2,1,0:T(8,128)(2,1)} %reshape.651), calls=%async_computation.2 | async-start | bytes 983040 | tf_op jit(solution)/shard_map/all_to_all | solution.py:92
  35.7 41.3 %collective-permute-start = (bf16[48,1536]{1,0:T(8,128)(2,1)S(1)}, bf16[48,1536]{1,0:T(8,128)(2,1)S(1)}, u32[]{:S(2)}, u32[]{:S(2)}) collective-permute-start(bf16[48,1536]{1,0:T(8,128)(2,1)S(1)} %copy-done.93), channel_id=1, source_target_pairs={{0,0},{1,8},{2,16},{3,24},{4,1},{5,9},{6,17},{7,25},{8,2},{9,10},{... | collective-permute-start | bytes 442376 | tf_op jit(solution)/shard_map/ppermute | solution.py:170
  37.2 107.6 %copy-start.70 = (f32[1536]{0:T(1024)S(1)}, f32[1536]{0:T(1024)}, u32[]{:S(2)}) copy-start(f32[1536]{0:T(1024)} %param.29) | copy-start | bytes 18436
  61.2 25.8 %all-to-all-start = ((bf16[8,32,512]{2,1,0:T(8,128)(2,1)}), bf16[8,32,512]{2,1,0:T(8,128)(2,1)S(1)}, u32[]{:S(2)}, u32[]{:S(2)}) async-start(bf16[8,32,512]{2,1,0:T(8,128)(2,1)} %reshape.645), calls=%async_computation | async-start | bytes 524288 | tf_op jit(solution)/shard_map/all_to_all | solution.py:92
  67.4 104.6 %all-gather.22.cloned.1.call-start = ((), (), s32[]{:S(2)}) async-start(), calls=%async_computation.19 | async-start | bytes 2457600 | tf_op jit(solution)/shard_map/all_gather | solution.py:95
  68.0 172.9 %reduce-scatter.15.cloned.1.call-start = ((), (), s32[]{:S(2)}) async-start(), calls=%async_computation.21 | async-start | bytes 1769472 | tf_op jit(solution)/shard_map/reduce_scatter | solution.py:89
  87.0 170.4 %copy-start.22 = (bf16[192,1536]{1,0:T(8,128)(2,1)}, bf16[192,1536]{1,0:T(8,128)(2,1)S(1)}, u32[]{:S(2)}) copy-start(bf16[192,1536]{1,0:T(8,128)(2,1)S(1)} %all_gather.68) | copy-start | bytes 1769476
  87.0 60.9 %copy-start.24 = (bf16[8,32,512]{2,1,0:T(8,128)(2,1)}, bf16[8,32,512]{2,1,0:T(8,128)(2,1)S(1)}, u32[]{:S(2)}) copy-start(bf16[8,32,512]{2,1,0:T(8,128)(2,1)S(1)} %all-to-all-done) | copy-start | bytes 786436
  150.5 198.7 %reduce-scatter.17.cloned.1.call-start = ((), (), s32[]{:S(2)}) async-start(), calls=%async_computation.22 | async-start | bytes 3538944 | tf_op jit(solution)/shard_map/reduce_scatter | solution.py:89
  176.7 72.6 %copy-start.2 = (f32[1024,576]{0,1:T(8,128)}, f32[1024,576]{0,1:T(8,128)S(1)}, u32[]{:S(2)}) copy-start(f32[1024,576]{0,1:T(8,128)S(1)} %fusion.36) | copy-start | bytes 7077892
  178.3 64.3 %copy-start.28 = (bf16[3,1024,32]{1,2,0:T(8,128)(2,1)}, bf16[3,1024,32]{1,2,0:T(8,128)(2,1)S(1)}, u32[]{:S(2)}) copy-start(bf16[3,1024,32]{1,2,0:T(8,128)(2,1)S(1)} %get-tuple-element.187) | copy-start | bytes 589828
  187.2 62.1 %copy-start.49 = (f32[3,1024]{1,0:T(4,128)}, f32[3,1024]{1,0:T(4,128)S(1)}, u32[]{:S(2)}) copy-start(f32[3,1024]{1,0:T(4,128)S(1)} %fusion.1) | copy-start | bytes 36868
  260.5 118.0 %all-gather.28.cloned.1.call-start = ((), (), s32[]{:S(2)}) async-start(), calls=%async_computation.24 | async-start | bytes 3932160 | tf_op jit(solution)/shard_map/all_gather | solution.py:95
  261.9 87.3 %copy-start.1 = (bf16[1,128,1536]{2,1,0:T(8,128)(2,1)S(1)}, bf16[1,128,1536]{2,1,0:T(8,128)(2,1)}, u32[]{:S(2)}) copy-start(bf16[1,128,1536]{2,1,0:T(8,128)(2,1)} %param.20) | copy-start | bytes 1179652
  262.4 91.4 %copy-start.72 = (f32[2,768]{1,0:T(2,128)S(1)}, f32[2,768]{1,0:T(2,128)}, u32[]{:S(2)}) copy-start(f32[2,768]{1,0:T(2,128)} %get-tuple-element.165) | copy-start | bytes 18436
  303.4 138.5 %all-gather.26.cloned.1.call-start = ((), (), s32[]{:S(2)}) async-start(), calls=%async_computation.23 | async-start | bytes 3538944 | tf_op jit(solution)/shard_map/all_gather | solution.py:86
  350.4 338.6 %copy-start.78 = (f32[128]{0:T(128)}, f32[128]{0:T(128)S(1)}, u32[]{:S(2)}) copy-start(f32[128]{0:T(128)S(1)} %add_rsqrt_fusion.5) | copy-start | bytes 1540
  352.4 109.4 %all-gather.30.cloned.1.call-start = ((), (), s32[]{:S(2)}) async-start(), calls=%async_computation.25 | async-start | bytes 1966080 | tf_op jit(solution)/shard_map/all_gather | solution.py:95
  353.0 171.7 %all-gather.38.cloned.1.call-start = ((), (), s32[]{:S(2)}) async-start(), calls=%async_computation.35 | async-start | bytes 3538944 | tf_op jit(solution)/shard_map/all_gather | solution.py:86
  353.7 257.6 %reduce-scatter.21.cloned.1.call-start = ((), (), s32[]{:S(2)}) async-start(), calls=%async_computation.27 | async-start | bytes 3538944 | tf_op jit(solution)/shard_map/reduce_scatter | solution.py:89
  353.8 335.2 %copy-start.68 = (f32[1536]{0:T(1024)}, f32[1536]{0:T(1024)S(1)}, u32[]{:S(2)}) copy-start(f32[1536]{0:T(1024)S(1)} %reshape.716) | copy-start | bytes 18436
  538.3 150.8 %reduce-scatter.19.cloned.1.call-start = ((), (), s32[]{:S(2)}) async-start(), calls=%async_computation.26 | async-start | bytes 3538944 | tf_op jit(solution)/shard_map/reduce_scatter | solution.py:89
  544.4 67.0 %copy-start.6 = (bf16[128,1536]{1,0:T(8,128)(2,1)S(1)}, bf16[128,1536]{1,0:T(8,128)(2,1)}, u32[]{:S(2)}) copy-start(bf16[128,1536]{1,0:T(8,128)(2,1)} %reduce-scatter.17.cloned.1.call-done) | copy-start | bytes 1179652
  544.4 144.7 %copy-start.16 = (bf16[1,128,1536]{2,1,0:T(8,128)(2,1)S(1)}, bf16[1,128,1536]{2,1,0:T(8,128)(2,1)}, u32[]{:S(2)}) copy-start(bf16[1,128,1536]{2,1,0:T(8,128)(2,1)} %param.39) | copy-start | bytes 1179652
  544.4 148.1 %copy-start.96 = (bf16[1024,512]{0,1:T(8,128)(2,1)S(1)}, bf16[1024,512]{0,1:T(8,128)(2,1)}, u32[]{:S(2)}) copy-start(bf16[1024,512]{0,1:T(8,128)(2,1)} %copy-done.95) | copy-start | bytes 3145732
  544.4 148.1 %copy-start.98 = (bf16[1024,512]{0,1:T(8,128)(2,1)S(1)}, bf16[1024,512]{0,1:T(8,128)(2,1)}, u32[]{:S(2)}) copy-start(bf16[1024,512]{0,1:T(8,128)(2,1)} %copy-done.97) | copy-start | bytes 3145732
  544.4 207.8 %all-gather.32.cloned.1.call-start = ((), (), s32[]{:S(2)}) async-start(), calls=%async_computation.28 | async-start | bytes 3538944 | tf_op jit(solution)/shard_map/all_gather | solution.py:86
  612.7 87.5 %copy-start.81 = (f32[128]{0:T(128)}, f32[128]{0:T(128)S(1)}, u32[]{:S(2)}) copy-start(f32[128]{0:T(128)S(1)} %broadcast_multiply_fusion.4) | copy-start | bytes 1540
  692.4 108.5 %reduce-scatter.27.cloned.1.call-start = ((), (), s32[]{:S(2)}) async-start(), calls=%async_computation.32 | async-start | bytes 3932160 | tf_op jit(solution)/shard_map/reduce_scatter | solution.py:98
  700.2 147.2 %all-gather.34.cloned.1.call-start = ((), (), s32[]{:S(2)}) async-start(), calls=%async_computation.30 | async-start | bytes 1769472 | tf_op jit(solution)/shard_map/all_gather | solution.py:86
  763.5 115.3 %reduce-scatter.31.cloned.1.call-start = ((), (), s32[]{:S(2)}) async-start(), calls=%async_computation.36 | async-start | bytes 2457600 | tf_op jit(solution)/shard_map/reduce_scatter | solution.py:98
  785.8 123.7 %reduce-scatter.29.cloned.1.call-start = ((), (), s32[]{:S(2)}) async-start(), calls=%async_computation.33 | async-start | bytes 1966080 | tf_op jit(solution)/shard_map/reduce_scatter | solution.py:98
  791.3 143.4 %reduce-scatter.25.cloned.1.call-start = ((), (), s32[]{:S(2)}) async-start(), calls=%async_computation.31 | async-start | bytes 737280 | tf_op jit(solution)/shard_map/reduce_scatter | solution.py:98
  794.9 220.3 %reduce-scatter.23.cloned.1.call-start = ((), (), s32[]{:S(2)}) async-start(), calls=%async_computation.29 | async-start | bytes 3538944 | tf_op jit(solution)/shard_map/reduce_scatter | solution.py:89
  800.9 59.6 %all-to-all-start.6 = ((bf16[8,48,1024]{2,1,0:T(8,128)(2,1)}), bf16[8,48,1024]{2,1,0:T(8,128)(2,1)}, u32[]{:S(2)}, u32[]{:S(2)}) async-start(bf16[8,48,1024]{2,1,0:T(8,128)(2,1)} %bitcast.375), calls=%async_computation.13 | async-start | bytes 1572864 | tf_op jit(solution)/shard_map/all_to_all | solution.py:92
  805.1 322.9 %reduce-scatter.33.cloned.1.call-start = ((), (), s32[]{:S(2)}) async-start(), calls=%async_computation.37 | async-start | bytes 3932160
  860.5 12.1 %all-to-all-start.4 = ((bf16[8,32,512]{2,1,0:T(8,128)(2,1)}), bf16[8,32,512]{2,1,0:T(8,128)(2,1)S(1)}, u32[]{:S(2)}, u32[]{:S(2)}) async-start(bf16[8,32,512]{2,1,0:T(8,128)(2,1)} %bitcast.60), calls=%async_computation.9 | async-start | bytes 524288 | tf_op jit(solution)/shard_map/all_to_all | solution.py:92
  878.8 59.7 %all-to-all-start.5 = ((bf16[8,48,576]{2,1,0:T(8,128)(2,1)}), bf16[8,48,576]{2,1,0:T(8,128)(2,1)S(1)}, u32[]{:S(2)}, u32[]{:S(2)}) async-start(bf16[8,48,576]{2,1,0:T(8,128)(2,1)} %bitcast.380), calls=%async_computation.10 | async-start | bytes 983040 | tf_op jit(solution)/shard_map/all_to_all | solution.py:92
  934.7 1.7 collective-permute-start.1
  940.5 127.6 %copy-start.12 = (bf16[1024,768]{1,0:T(8,128)(2,1)S(1)}, bf16[1024,768]{1,0:T(8,128)(2,1)}, u32[]{:S(2)}) copy-start(bf16[1024,768]{1,0:T(8,128)(2,1)} %all-gather.20.cloned.1.call-done) | copy-start | bytes 4718596
  944.0 141.8 %copy-start.63 = (f32[1,1024]{1,0:T(1,128)S(1)}, f32[1,1024]{1,0:T(1,128)}, u32[]{:S(2)}) copy-start(f32[1,1024]{1,0:T(1,128)} %copy-done.61) | copy-start | bytes 12292
  944.0 147.1 %copy-start.15 = (bf16[512,1024]{1,0:T(8,128)(2,1)S(1)}, bf16[512,1024]{1,0:T(8,128)(2,1)}, u32[]{:S(2)}) copy-start(bf16[512,1024]{1,0:T(8,128)(2,1)} %all-gather.18.cloned.1.call-done) | copy-start | bytes 3145732
  944.0 180.3 %copy-start.7 = (bf16[128,1536]{1,0:T(8,128)(2,1)S(1)}, bf16[128,1536]{1,0:T(8,128)(2,1)}, u32[]{:S(2)}) copy-start(bf16[128,1536]{1,0:T(8,128)(2,1)} %reduce-scatter.17.cloned.1.call-done) | copy-start | bytes 1179652
  944.0 180.3 %copy-start.66 = (f32[1536]{0:T(1024)S(1)}, f32[1536]{0:T(1024)}, u32[]{:S(2)}) copy-start(f32[1536]{0:T(1024)} %copy-done.64) | copy-start | bytes 18436
  (82 other events, 963.3 us)
Sparse Core Ops, SparseCore 0:
  9.6 19.4 all-gather.17
  30.6 19.6 all-gather.19
  52.5 34.4 all-gather.23
  89.0 60.3 all-gather.35
  151.4 20.5 all-gather.21
  175.3 65.5 reduce-scatter.14
  260.6 88.5 reduce-scatter.16
  350.8 27.5 all-gather.27
  381.5 60.4 all-gather.25
  443.4 18.2 all-gather.29
  464.2 60.4 all-gather.37
  538.4 72.9 reduce-scatter.20
  615.3 73.6 reduce-scatter.18
  692.5 59.6 all-gather.31
  754.7 36.6 reduce-scatter.26
  793.9 53.5 all-gather.33
  849.9 28.8 reduce-scatter.30
  881.4 28.1 reduce-scatter.28
  912.6 22.0 reduce-scatter.24
  938.1 76.9 reduce-scatter.22
  1017.7 37.1 reduce-scatter.32

commit v2 on v1

--- a/solution.py
+++ b/solution.py
@@ -76,26 +76,109 @@
     return jnp.einsum(spec, a, b, preferred_element_type=f32)
 
 
-def make_body(clips, outer, inner):
+def make_body(clips, outer, ring, pair):
+    inner = ring * pair
     shards = clips * outer
-    team = "inner"
+    team = ("ring", "pair")
     spread = ("clip", "outer") if outer > 1 else "clip"
-    whole_clip = ("outer", "inner") if outer > 1 else "inner"
-
-    def gather_team(x):
-        return lax.all_gather(x, team, axis=0, tiled=True)
-
-    def scatter_team(x):
-        return lax.psum_scatter(x, team, scatter_dimension=0, tiled=True)
+    spread_ffn = ("clip", "outer", "pair")
+    every = ("clip", "outer", "ring", "pair")
+    forward = [(z, (z + 1) % ring) for z in range(ring)]
+    crossed = [(x, (x + 1) % pair) for x in range(pair)]
+    slots = [(k, e) for k in range(ring) for e in range(pair)]
 
     def swap_team(x):
         return lax.all_to_all(x, team, split_axis=0, concat_axis=0, tiled=True)
 
-    def gather_spread(x):
-        return lax.all_gather(x, spread, axis=0, tiled=True)
-
-    def scatter_spread(x):
-        return lax.psum_scatter(x, spread, scatter_dimension=0, tiled=True)
+    def gather_spread(x, axes=spread):
+        return lax.all_gather(x, axes, axis=0, tiled=True)
+
+    def scatter_spread(x, axes=spread):
+        return lax.psum_scatter(x, axes, scatter_dimension=0, tiled=True)
+
+    def ring_gather(x):
+        parts, now = [], x
+        for k in range(ring):
+            parts.append(now)
+            other = now
+            for _ in range(1, pair):
+                other = lax.ppermute(other, "pair", crossed)
+                parts.append(other)
+            if k + 1 < ring:
+                now = lax.ppermute(now, "ring", forward)
+        return parts
+
+    def ring_scatter(block_of):
+        passed = None
+        for step in range(1, ring + 1):
+            k = step % ring
+            total = block_of(k, 0).astype(f32)
+            if pair > 1:
+                total = total + lax.ppermute(block_of(k, 1), "pair", crossed).astype(f32)
+            if passed is not None:
+                total = total + passed.astype(f32)
+            if step < ring:
+                passed = lax.ppermute(total.astype(bf16), "ring", forward)
+        return total
+
+    def row_blocks(x):
+        rows = x.shape[0] // inner
+        return lambda k, e: x[(k * pair + e) * rows : (k * pair + e + 1) * rows]
+
+    def line_gather(x):
+        parts = [x]
+        for _ in range(1, ring):
+            parts.append(lax.ppermute(parts[-1], "ring", forward))
+        return jnp.concatenate(parts, 0)
+
+    def line_scatter(x):
+        rows = x.shape[0] // ring
+        passed = None
+        for step in range(1, ring + 1):
+            k = step % ring
+            total = x[k * rows : (k + 1) * rows].astype(f32)
+            if passed is not None:
+                total = total + passed.astype(f32)
+            if step < ring:
+                passed = lax.ppermute(total.astype(bf16), "ring", forward)
+        return total
+
+    def direct(x, k, e):
+        if k == 0 and e == 0:
+            return x
+        moves = [
+            (z * pair + y, (z + k) % ring * pair + (y + e) % pair)
+            for z in range(ring)
+            for y in range(pair)
+        ]
+        return lax.ppermute(x, team, moves)
+
+    def small_gather(x):
+        return [direct(x, k, e) for k, e in slots]
+
+    def small_sum(x):
+        parts = small_gather(x)
+        total = parts[0]
+        for part in parts[1:]:
+            total = total + part
+        return total
+
+    def in_order(parts):
+        z, y = lax.axis_index("ring"), lax.axis_index("pair")
+        whole = jnp.zeros((inner,) + parts[0].shape, parts[0].dtype)
+        for (k, e), part in zip(slots, parts):
+            spot = lax.rem(z + ring - k, ring) * pair + lax.rem(y + pair - e, pair)
+            whole = lax.dynamic_update_index_in_dim(whole, part, spot, 0)
+        return whole
+
+    def slot_blocks(x):
+        z, y = lax.axis_index("ring"), lax.axis_index("pair")
+
+        def block_of(k, e):
+            spot = lax.rem(z + ring - k, ring) * pair + lax.rem(y + pair - e, pair)
+            return lax.dynamic_index_in_dim(x, spot, 0, keepdims=False)
+
+        return block_of
 
     def by_columns(w):
         rows, columns = w.shape
@@ -106,6 +189,16 @@
         _, rows, columns = w.shape
         blocks = w.reshape(inner, rows, shards, columns // shards)
         return blocks.transpose(1, 2, 0, 3).reshape(rows, inner * columns)
+
+    def line_columns(w):
+        rows, columns = w.shape
+        blocks = w.reshape(rows, shards, ring, columns // (shards * ring))
+        return blocks.transpose(2, 0, 1, 3).reshape(ring, rows, columns // ring)
+
+    def back_line_columns(w):
+        _, rows, columns = w.shape
+        blocks = w.reshape(ring, rows, shards, columns // shards)
+        return blocks.transpose(1, 2, 0, 3).reshape(rows, ring * columns)
 
     def body(
         tokens,
@@ -159,20 +252,22 @@
         qkv_blocks = w_qkv.reshape(rows, 3, inner, own).transpose(2, 0, 1, 3)
         qkv_blocks = qkv_blocks.reshape(inner, rows, 3 * own)
         qkv_s = gather_spread(swap_team(qkv_blocks).reshape(inner * rows, 3 * own))
-        tokens_all = gather_team(tokens[0])
-        spots = lax.all_gather(positions[:, 0, :], team, axis=1, tiled=True)
+        tokens_all = jnp.concatenate(ring_gather(tokens[0]), 0)
+        spots = jnp.concatenate(small_gather(positions[:, 0, :].astype(f32)), 1)
         text_s = gather_spread(jnp.concatenate([w_key_text, w_value_text], -1))
         to_heads = [
             (r, (r % shards) * inner + r // shards) for r in range(shards * inner)
         ]
         from_heads = [(b, a) for a, b in to_heads]
-        every = ("clip", "outer", "inner")
         out_s = gather_spread(lax.ppermute(w_out, every, to_heads))
-        ffn_blocks = jnp.concatenate([by_columns(w_gate), by_columns(w_up)], -1)
-        ffn_s = gather_spread(swap_team(ffn_blocks).reshape(inner * rows, -1))
-        down_s = gather_spread(w_down)
+        ffn_blocks = jnp.concatenate([line_columns(w_gate), line_columns(w_up)], -1)
+        ffn_blocks = lax.all_to_all(ffn_blocks, "ring", split_axis=0, concat_axis=0, tiled=True)
+        ffn_s = gather_spread(ffn_blocks.reshape(ring * rows, -1), spread_ffn)
+        ffn_s = ffn_s.reshape(shards, pair, ring, rows, -1).transpose(0, 2, 1, 3, 4)
+        ffn_s = ffn_s.reshape(width, -1)
+        down_s = gather_spread(w_down, spread_ffn)
         ff_own = down_s.shape[0]
-        cot_all = gather_team(cotangent[0])
+        cot_all = line_gather(cotangent[0])
 
         cap_mask = (jnp.arange(cap_len) < lengths[0]).astype(f32)
         pooled = jnp.sum(cap_part.astype(f32) * cap_mask[:, None], 0) / length_f
@@ -183,10 +278,10 @@
         time_own = lax.dynamic_index_in_dim(
             time_embed.reshape(shards, inner, time_rows), member, 1, keepdims=False
         ).reshape(1, -1)
-        condition = lax.psum(dot(pooled_b[None], pool_s) + dot(time_own, time_s), team)
+        condition = small_sum(dot(pooled_b[None], pool_s) + dot(time_own, time_s))
         cond_b = jax.nn.silu(condition).astype(bf16)
         bias_own = lax.dynamic_slice_in_dim(b_ada, member * mod_own, mod_own)
-        modulation = gather_team(dot(cond_b, ada_s)[0] + bias_own)
+        modulation = in_order(small_gather(dot(cond_b, ada_s)[0] + bias_own)).reshape(-1)
         scale_attn, gate_attn, scale_ffn, gate_ffn = jnp.split(modulation, 4)
         tanh_attn = jnp.tanh(gate_attn)
         tanh_ffn = jnp.tanh(gate_ffn)
@@ -222,7 +317,7 @@
 
         text_part = dot(cap_part, text_s).astype(bf16)
         text_part = text_part.reshape(cap_len, 2, inner, own).transpose(2, 0, 1, 3)
-        text_own = scatter_team(text_part.reshape(inner * cap_len, 2 * own)).astype(f32)
+        text_own = ring_scatter(slot_blocks(text_part.reshape(inner, cap_len, 2 * own)))
         text_own = text_own.reshape(cap_len, 2, heads, head_dim).transpose(1, 2, 0, 3)
         text_keys_n, inverse_t = rms_norm(text_own[0], head_eps)
         keys_text_b = text_keys_n.astype(bf16)
@@ -236,14 +331,14 @@
         gate_t = gate_own[:, None, None]
         mixed = self_out + gate_t * cross_out
         mixed_b = mixed.transpose(1, 0, 2).reshape(team_rows, own).astype(bf16)
-        attn_out = scatter_team(dot(mixed_b, out_s).astype(bf16)).astype(f32)
+        attn_out = ring_scatter(row_blocks(dot(mixed_b, out_s).astype(bf16)))
 
         tokens_f = tokens[0].astype(f32)
         normed1, inverse1 = rms_norm(tokens_f, epsilon)
         resid = tokens_f + tanh_attn * attn_out
         normed2, inverse2 = rms_norm(resid, epsilon)
         gain2 = norm2_gain * (1.0 + scale_ffn)
-        ffn_in = gather_team((normed2 * gain2).astype(bf16))
+        ffn_in = line_gather((normed2 * gain2).astype(bf16))
         gate_up = dot(ffn_in, ffn_s)
         gate_pre, up_pre = gate_up[:, :ff_own], gate_up[:, ff_own:]
         sigmoid_g = jax.nn.sigmoid(gate_pre)
@@ -259,21 +354,25 @@
             ],
             -1,
         )
-        d_ffn_in = scatter_team(dot_nt(d_gate_up, ffn_s).astype(bf16)).astype(f32)
-        ffn_out = scatter_team(dot(hidden_b, down_s).astype(bf16)).astype(f32)
+        d_ffn_in = line_scatter(dot_nt(d_gate_up, ffn_s).astype(bf16))
+        ffn_out = line_scatter(dot(hidden_b, down_s).astype(bf16))
         mixed_out = (resid + tanh_ffn * ffn_out).astype(bf16)
         d_out = cotangent[0].astype(f32)
         sum_gate_ffn = jnp.sum(d_out * ffn_out, 0)
-        sum_down = scatter_spread(dot_tn(hidden_b, d_ffn_b).astype(bf16)).astype(f32)
-        sum_ffn = scatter_spread(dot_tn(ffn_in, d_gate_up).astype(bf16))
-        sum_ffn = swap_team(sum_ffn.reshape(inner, rows, 2 * ff_own))
-        sum_gate = back_columns(sum_ffn[:, :, :ff_own]).astype(f32)
-        sum_up = back_columns(sum_ffn[:, :, ff_own:]).astype(f32)
+        grad_down = dot_tn(hidden_b, d_ffn_b).astype(bf16)
+        sum_down = scatter_spread(grad_down, spread_ffn).astype(f32)
+        grad_ffn = dot_tn(ffn_in, d_gate_up).astype(bf16)
+        grad_ffn = grad_ffn.reshape(shards, ring, pair, rows, -1).transpose(0, 2, 1, 3, 4)
+        sum_ffn = scatter_spread(grad_ffn.reshape(width, -1), spread_ffn)
+        sum_ffn = sum_ffn.reshape(ring, rows, 2 * ff_own)
+        sum_ffn = lax.all_to_all(sum_ffn, "ring", split_axis=0, concat_axis=0, tiled=True)
+        sum_gate = back_line_columns(sum_ffn[:, :, :ff_own]).astype(f32)
+        sum_up = back_line_columns(sum_ffn[:, :, ff_own:]).astype(f32)
 
         sum_norm2 = jnp.sum(d_ffn_in * normed2, 0)
         d_resid = d_out + norm_back(normed2, inverse2, d_ffn_in * gain2)
         sum_gate_attn = jnp.sum(d_resid * attn_out, 0)
-        d_attn_b = gather_team((tanh_attn * d_resid).astype(bf16))
+        d_attn_b = jnp.concatenate(ring_gather((tanh_attn * d_resid).astype(bf16)), 0)
         grad_out = dot_tn(mixed_b, d_attn_b).astype(bf16)
         sum_out = lax.ppermute(scatter_spread(grad_out), every, from_heads).astype(f32)
         d_mixed = dot_nt(d_attn_b, out_s).reshape(team_rows, heads, head_dim).transpose(1, 0, 2)
@@ -300,7 +399,7 @@
                 text_grads, lax.axis_index("outer") * inner * cap_rows, inner * cap_rows
             )
         text_rows = text_grads.shape[0]
-        text_grads = gather_team(text_grads).reshape(inner, text_rows, 2, own)
+        text_grads = in_order(ring_gather(text_grads)).reshape(inner, text_rows, 2, own)
         text_grads = text_grads.transpose(1, 2, 0, 3).reshape(text_rows, 2 * width)
         sum_text = scatter_spread(dot_tn(cap_own, text_grads).astype(bf16)).astype(f32)
         d_cap = dot_nt(text_grads, text_s).astype(bf16).reshape(inner, cap_rows, -1)
@@ -320,7 +419,7 @@
         d_keys_raw = norm_back(keys_n, inverse_k, rotate(d_keys, cos_tab, -sin_tab))
         d_qkv = jnp.stack([d_queries_raw, d_keys_raw, d_values]).astype(bf16)
         d_qkv = d_qkv.transpose(2, 0, 1, 3).reshape(team_rows, 3 * own)
-        d_mix_in = scatter_team(dot_nt(d_qkv, qkv_s).astype(bf16)).astype(f32)
+        d_mix_in = ring_scatter(row_blocks(dot_nt(d_qkv, qkv_s).astype(bf16)))
         sum_qkv = scatter_spread(dot_tn(mix_in, d_qkv).astype(bf16))
         sum_qkv = swap_team(sum_qkv.reshape(inner, rows, 3 * own)).reshape(inner, rows, 3, own)
         sum_qkv = sum_qkv.transpose(1, 2, 0, 3).reshape(rows, 3 * width).astype(f32)
@@ -330,11 +429,15 @@
 
         cross_slots = jnp.zeros((128,), f32)
         cross_slots = lax.dynamic_update_slice_in_dim(cross_slots, grad_cross, member * heads, 0)
-        sums = jnp.concatenate(
-            [sum_norm1, sum_gate_attn, sum_norm2, sum_gate_ffn, cross_slots]
-        ).reshape(-1, 128)
-        sums = lax.psum(sums, whole_clip)
-        sums = lax.all_gather(sums, "clip", axis=0).reshape(clips, -1)
+        early = jnp.concatenate([sum_gate_attn, sum_norm2, sum_gate_ffn, cross_slots])
+        early = small_sum(early.reshape(-1, 128))
+        late = small_sum(sum_norm1.reshape(-1, 128))
+        if outer > 1:
+            early = lax.psum(early, "outer")
+            late = lax.psum(late, "outer")
+        early = lax.all_gather(early, "clip", axis=0).reshape(clips, -1)
+        late = lax.all_gather(late, "clip", axis=0).reshape(clips, -1)
+        sums = jnp.concatenate([late, early], -1)
         mods = clip_facts[:, :mod_width].reshape(clips, 4, width)
         at = mod_width
         cond_all = clip_facts[:, at : at + cond_width]
@@ -364,13 +467,13 @@
         sum_ada = jnp.sum(cond_rows[:, :, None] * d_modulation[:, None, :], 0)
         d_mod_clip = lax.dynamic_index_in_dim(d_modulation, lax.axis_index("clip"), 0)
         d_mod_own = lax.dynamic_slice_in_dim(d_mod_clip, member * mod_own, mod_own, 1)
-        d_cond_act = lax.psum(dot_nt(d_mod_own.astype(bf16), ada_s), team)
+        d_cond_act = small_sum(dot_nt(d_mod_own.astype(bf16), ada_s))
         sigmoid_c = jax.nn.sigmoid(condition)
         d_condition = d_cond_act * sigmoid_c * (1.0 + condition * (1.0 - sigmoid_c))
         d_cond_all = lax.all_gather(d_condition[0], "clip", axis=0)
-        d_pooled = gather_team(dot_nt(d_condition.astype(bf16), pool_s)[0])
+        d_pooled = in_order(small_gather(dot_nt(d_condition.astype(bf16), pool_s)[0]))
         d_pooled = d_pooled.reshape(inner, shards, -1).transpose(1, 0, 2).reshape(1, -1)
-        seq_row = lax.axis_index(whole_clip)
+        seq_row = lax.axis_index(("outer", "ring", "pair"))
         local_mask = (seq_row * cap_rows + jnp.arange(cap_rows) < lengths[0]).astype(f32)
         d_caption = d_cap + local_mask[:, None] * d_pooled / length_f
         embed_all = timestep_embed(steps_all, embed_width).astype(bf16).astype(f32)
@@ -408,13 +511,15 @@
 
     def run(*args):
         inner = math.gcd(args[13].shape[0], members)
-        outer = members // inner
-        fine = Mesh(mesh.devices.reshape(clips, outer, inner), ("clip", "outer", "inner"))
-        seq = ("outer", "inner")
-        every = P(("clip", "outer", "inner"), None)
+        outer, pair = members // inner, math.gcd(inner, 2)
+        ring = inner // pair
+        names = ("clip", "outer", "ring", "pair")
+        fine = Mesh(mesh.devices.reshape(clips, outer, ring, pair), names)
+        seq = names[1:]
+        every = P(names, None)
         by_token = P("clip", seq, None)
         return jax.shard_map(
-            make_body(clips, outer, inner),
+            make_body(clips, outer, ring, pair),
             mesh=fine,
             in_specs=(
                 by_token,

time: 1150 us -> 745 us (0.65)
  waiting for transfers between devices: 639 us -> 257 us
  blocking collectives: 247 us -> 77.8 us
  starting transfers between devices: 26.7 us -> 146 us
  local copies, waits for them, and re-layouts: 54.3 us -> 84.9 us
  matrix products: 108 us -> 93.6 us
    reduce_scatter x9 -> x4, waiting for transfers between devices: 361 us -> 0.03 us  [scatter_spread(): return lax.psum_scatter(x, axes, scatter_dimension=0, tiled=True)]
    all_gather x11 -> x6, waiting for transfers between devices: 268 us -> 0.07 us  [gather_spread(): return lax.all_gather(x, axes, axis=0, tiled=True)]
    ppermute x0 -> x103, waiting for transfers between devices: none -> 236 us  [the longest x9 56.5 us: ring_gather(): now = lax.ppermute(now, 'ring', forward)]
    ppermute x0 -> x103, starting transfers between devices: none -> 116 us  [the longest x49 79.3 us: direct(): return lax.ppermute(x, team, moves)]
    psum x3 -> x0, blocking collectives: 74.7 us -> none  [the longest x1 35.9 us: body(): sums = lax.psum(sums, whole_clip)]
    all_gather x6 -> x4, blocking collectives: 101 us -> 30.8 us  [the longest x2 20.4 us: gather_spread(): return lax.all_gather(x, axes, axis=0, tiled=True)]
    all_to_all x2, blocking collectives: 60.2 us -> 36.3 us  [swap_team(): return lax.all_to_all(x, team, split_axis=0, concat_axis=0, tiled=True)]
    unnamed x225 -> x294, local copies, waits for them, and re-layouts: 38.1 us -> 31.9 us
  transfers between devices with their start and end apart: 28 -> 121, of which waited for: 16 -> 44; matrix products, arithmetic and copies ran while one was open for 14% -> 26% of each run, Pallas kernels for 0% -> 0%
where the time goes in v2:
time: 745 us; the launch traced here: 735 us
  waiting for transfers between devices  257 us (34%)
  starting transfers between devices  146 us (20%)
  matrix products  93.6 us (13%)
  local copies, waits for them, and re-layouts  84.9 us (11%)
  blocking collectives  77.8 us (10%)
  other arithmetic  58 us (8%)
  between operations  17.7 us (2%)
    ppermute x49, starting transfers between devices, direct(): return lax.ppermute(x, team, moves)  79.3 us
    ppermute x9, waiting for transfers between devices, ring_gather(): now = lax.ppermute(now, 'ring', forward)  56.5 us
    ppermute x6, waiting for transfers between devices, line_scatter(): passed = lax.ppermute(total.astype(bf16), 'ring', forward)  42.2 us
    ppermute x12, waiting for transfers between devices, ring_gather(): other = lax.ppermute(other, 'pair', crossed)  36.9 us
    all_to_all x2, blocking collectives, swap_team(): return lax.all_to_all(x, team, split_axis=0, concat_axis=0, tiled=True)  36.3 us
    dot_general x11, matrix products, ein(): return jnp.einsum(spec, a, b, preferred_element_type=f32)  34.4 us
    ppermute x6, waiting for transfers between devices, line_gather(): parts.append(lax.ppermute(parts[-1], 'ring', forward))  32.9 us
    unnamed x294, local copies, waits for them, and re-layouts  31.9 us
  transfers between devices with their start and end apart: 121, of which 44 were waited for; matrix products, arithmetic and copies ran while one was open for 26% of the time, Pallas kernels for 0%

profile of v2, /device:TPU:0, one launch (start us, length us, event | category | flops | bytes accessed | tf_op | source)
XLA Modules:
  0.0 734.8 jit_solution(15817690684481246652)
XLA Ops:
  9.1 19.4 %all_to_all.35 = bf16[8,32,768]{2,1,0:T(8,128)(2,1)} all-to-all(bf16[8,32,768]{2,1,0:T(8,128)(2,1)S(1)} %copy.239), channel_id=1, replica_groups=mesh['clip'=4,'outer'=1,'ring'=4,'pair'=2] {'ring','pair'}, dimensions={0} | all-to-all | bytes 786432 | tf_op jit(solution)/shard_map/all_to_all | solution.py:91
  30.0 16.9 %all_to_all.36 = bf16[8,48,576]{2,1,0:T(8,128)(2,1)} all-to-all(bf16[8,48,576]{2,1,0:T(8,128)(2,1)S(1)} %reshape.709), channel_id=1, replica_groups=mesh['clip'=4,'outer'=1,'ring'=4,'pair'=2] {'ring','pair'}, dimensions={0} | all-to-all | bytes 884736 | tf_op jit(solution)/shard_map/all_to_all | solution.py:91
  61.8 5.6 all_gather.43
  91.8 14.8 %all_gather.47 = bf16[192,1536]{1,0:T(8,128)(2,1)} all-gather(bf16[48,1536]{1,0:T(8,128)(2,1)S(1)} %collective-permute-done.35), channel_id=1, replica_groups=mesh['clip'=4,'outer'=1,'ring'=4,'pair'=2] {'clip'}, dimensions={0}, use_global_device_ids=true | all-gather | bytes 737280 | tf_op jit(solution)/shard_map/all_gather | solution.py:94
  117.2 10.6 %all-to-all-done = bf16[8,32,512]{2,1,0:T(8,128)(2,1)} async-done(((bf16[8,32,512]{2,1,0:T(8,128)(2,1)}), bf16[8,32,512]{2,1,0:T(8,128)(2,1)}, u32[]{:S(2)}, u32[]{:S(2)}) %all-to-all-start) | async-done | bytes 262176 | tf_op jit(solution)/shard_map/all_to_all | solution.py:91
  132.4 10.7 %collective-permute-done.19 = bf16[128,1536]{1,0:T(8,128)(2,1)} collective-permute-done((bf16[128,1536]{1,0:T(8,128)(2,1)}, bf16[128,1536]{1,0:T(8,128)(2,1)}, u32[]{:S(2)}, u32[]{:S(2)}) %collective-permute-start.19) | collective-permute-done | bytes 393248 | tf_op jit(solution)/shard_map/ppermute | solution.py:108
  200.3 4.7 fusion.28
  211.4 5.4 collective-permute-done.31
  218.9 5.7 collective-permute-done.32
  227.9 4.3 collective-permute-done.33
  234.8 5.4 collective-permute-done.34
  247.5 8.0 %fusion.44 = (bf16[1024,3,64]{0,2,1:T(8,128)(2,1)S(1)}, f32[3,1024,64]{1,2,0:T(8,128)}) fusion(f32[3,1024,64]{1,2,0:T(8,128)S(1)} %fusion.48, f32[3]{0:T(128)S(1)} %copy-done.111, f32[1024,3]{0,1:T(4,128)S(1)} %bitcast.398, f32[3,1024,1024]{1,2,0:T(8,128)} %copy-done, f32[3,1024]{1,0:T(4,128)S(1)} %copy-done.71, f32[3,3,1024,64]{2,3,1,0:T(8,128)S(1)} %bitcast.327), kind=kOutput, calls=%fused_computation.86 | convolution fusion | flops 412876800 | bytes 14975488 | tf_op jit(solution)/shard_map/hqk,hkd->hqd/dot_general | solution.py:76
  259.9 8.5 %collective-permute-done.39 = bf16[128,1536]{1,0:T(8,128)(2,1)} collective-permute-done((bf16[128,1536]{1,0:T(8,128)(2,1)}, bf16[128,1536]{1,0:T(8,128)(2,1)}, u32[]{:S(2)}, u32[]{:S(2)}) %collective-permute-start.39) | collective-permute-done | bytes 393248 | tf_op jit(solution)/shard_map/ppermute | solution.py:117
  272.1 7.3 collective-permute-done.38
  285.6 4.5 collective-permute-done.41
  296.4 8.9 %collective-permute-done.42 = bf16[128,1536]{1,0:T(8,128)(2,1)} collective-permute-done((bf16[128,1536]{1,0:T(8,128)(2,1)}, bf16[128,1536]{1,0:T(8,128)(2,1)}, u32[]{:S(2)}, u32[]{:S(2)}) %collective-permute-start.42) | collective-permute-done | bytes 393248 | tf_op jit(solution)/shard_map/ppermute | solution.py:121
  308.4 13.8 %collective-permute-done.43 = bf16[128,1536]{1,0:T(8,128)(2,1)S(1)} collective-permute-done((bf16[128,1536]{1,0:T(8,128)(2,1)S(1)}, bf16[128,1536]{1,0:T(8,128)(2,1)S(1)}, u32[]{:S(2)}, u32[]{:S(2)}) %collective-permute-start.43) | collective-permute-done | bytes 393248 | tf_op jit(solution)/shard_map/ppermute | solution.py:131
  322.1 6.8 collective-permute-done.49
  328.9 4.3 collective-permute-done.44
  333.2 5.4 collective-permute-done.50
  344.4 6.7 fusion.61
  352.9 6.2 multiply_convert_fusion.4
  364.7 11.9 %collective-permute-done.52 = bf16[128,1536]{1,0:T(8,128)(2,1)S(1)} collective-permute-done((bf16[128,1536]{1,0:T(8,128)(2,1)S(1)}, bf16[128,1536]{1,0:T(8,128)(2,1)S(1)}, u32[]{:S(2)}, u32[]{:S(2)}) %collective-permute-start.52) | collective-permute-done | bytes 393248 | tf_op jit(solution)/shard_map/ppermute | solution.py:143
  376.7 4.3 collective-permute-done.46
  381.3 6.4 collective-permute-done.53
  387.8 6.9 collective-permute-done.47
  399.8 8.7 %collective-permute-done.48 = bf16[128,1536]{1,0:T(8,128)(2,1)S(1)} collective-permute-done((bf16[128,1536]{1,0:T(8,128)(2,1)S(1)}, bf16[128,1536]{1,0:T(8,128)(2,1)S(1)}, u32[]{:S(2)}, u32[]{:S(2)}) %collective-permute-start.48) | collective-permute-done | bytes 393248 | tf_op jit(solution)/shard_map/ppermute | solution.py:143
  414.4 7.3 collective-permute-done.56
  424.0 9.5 %collective-permute-done.58 = bf16[128,1536]{1,0:T(8,128)(2,1)S(1)} collective-permute-done((bf16[128,1536]{1,0:T(8,128)(2,1)S(1)}, bf16[128,1536]{1,0:T(8,128)(2,1)S(1)}, u32[]{:S(2)}, u32[]{:S(2)}) %collective-permute-start.58) | collective-permute-done | bytes 393248 | tf_op jit(solution)/shard_map/ppermute | solution.py:108
  433.7 9.5 %collective-permute-done.60 = bf16[128,1536]{1,0:T(8,128)(2,1)S(1)} collective-permute-done((bf16[128,1536]{1,0:T(8,128)(2,1)S(1)}, bf16[128,1536]{1,0:T(8,128)(2,1)S(1)}, u32[]{:S(2)}, u32[]{:S(2)}) %collective-permute-start.60) | collective-permute-done | bytes 393248 | tf_op jit(solution)/shard_map/ppermute | solution.py:108
  445.3 5.7 collective-permute-done.61
  461.7 4.3 multiply_convert_fusion
  475.4 7.3 fusion.21
  488.5 5.4 convolution_convert_fusion
  497.9 5.4 all_gather.54
  506.7 4.6 convolution_convert_fusion.5
  527.7 7.9 %collective-permute-done.72 = bf16[256,384]{0,1:T(8,128)(2,1)S(1)} collective-permute-done((bf16[256,384]{0,1:T(8,128)(2,1)S(1)}, bf16[256,384]{0,1:T(8,128)(2,1)S(1)}, u32[]{:S(2)}, u32[]{:S(2)}) %collective-permute-start.72) | collective-permute-done | bytes 196640 | tf_op jit(solution)/shard_map/ppermute | solution.py:108
  537.0 18.6 %collective-permute-done.71 = bf16[256,384]{0,1:T(8,128)(2,1)S(1)} collective-permute-done((bf16[256,384]{0,1:T(8,128)(2,1)S(1)}, bf16[256,384]{0,1:T(8,128)(2,1)S(1)}, u32[]{:S(2)}, u32[]{:S(2)}) %collective-permute-start.71) | collective-permute-done | bytes 196640 | tf_op jit(solution)/shard_map/ppermute | solution.py:105
  556.2 9.1 %collective-permute-done.74 = bf16[256,384]{0,1:T(8,128)(2,1)S(1)} collective-permute-done((bf16[256,384]{0,1:T(8,128)(2,1)S(1)}, bf16[256,384]{0,1:T(8,128)(2,1)S(1)}, u32[]{:S(2)}, u32[]{:S(2)}) %collective-permute-start.74) | collective-permute-done | bytes 196640 | tf_op jit(solution)/shard_map/ppermute | solution.py:108
  565.4 10.0 %collective-permute-done.75 = bf16[256,384]{0,1:T(8,128)(2,1)S(1)} collective-permute-done((bf16[256,384]{0,1:T(8,128)(2,1)S(1)}, bf16[256,384]{0,1:T(8,128)(2,1)S(1)}, u32[]{:S(2)}, u32[]{:S(2)}) %collective-permute-start.75) | collective-permute-done | bytes 196640 | tf_op jit(solution)/shard_map/ppermute | solution.py:105
  601.7 6.0 all-to-all-start.4
  608.7 5.3 all-gather.3
  643.1 5.2 all-gather.2
  662.5 5.1 all-to-all-start.5
  673.4 5.4 collective-permute-done.91
  687.4 5.2 all-gather.4
  699.6 4.7 all-to-all-start.6
  713.9 9.6 %all-to-all-done.6 = bf16[4,48,2048]{2,1,0:T(8,128)(2,1)S(1)} async-done(((bf16[4,48,2048]{2,1,0:T(8,128)(2,1)}), bf16[4,48,2048]{2,1,0:T(8,128)(2,1)S(1)}, u32[]{:S(2)}, u32[]{:S(2)}) %all-to-all-start.6) | async-done | bytes 786464 | tf_op jit(solution)/shard_map/all_to_all | solution.py:368
  (717 shorter events, 344.0 us)
Async XLA Ops:
  7.2 139.2 %all-gather.12.cloned.1.call-start = ((), (), s32[]{:S(2)}) async-start(), calls=%async_computation.12 | async-start | bytes 1310720 | tf_op jit(solution)/shard_map/all_gather | solution.py:94
  7.9 156.0 %all-gather.14.cloned.1.call-start = ((), (), s32[]{:S(2)}) async-start(), calls=%async_computation.13 | async-start | bytes 1966080 | tf_op jit(solution)/shard_map/all_gather | solution.py:94
  28.6 171.7 %all-gather.16.cloned.1.call-start = ((), (), s32[]{:S(2)}) async-start(), calls=%async_computation.14 | async-start | bytes 2457600 | tf_op jit(solution)/shard_map/all_gather | solution.py:94
  47.0 158.3 %all-gather.18.cloned.1.call-start = ((), (), s32[]{:S(2)}) async-start(), calls=%async_computation.15 | async-start | bytes 3932160 | tf_op jit(solution)/shard_map/all_gather | solution.py:94
  48.0 67.2 %collective-permute-start.14 = (bf16[128,1536]{1,0:T(8,128)(2,1)S(1)}, bf16[128,1536]{1,0:T(8,128)(2,1)}, u32[]{:S(2)}, u32[]{:S(2)}) collective-permute-start(bf16[128,1536]{1,0:T(8,128)(2,1)S(1)} %bitcast.348), channel_id=1, source_target_pairs={{0,1},{1,0},{2,3},{3,2},{4,5},{5,4},{6,7},{7,6},{8,9},{9,8},{10,11... | collective-permute-start | bytes 1179656 | tf_op jit(solution)/shard_map/ppermute | solution.py:105
  49.6 57.0 %collective-permute-start.15 = (bf16[128,1536]{1,0:T(8,128)(2,1)S(1)}, bf16[128,1536]{1,0:T(8,128)(2,1)}, u32[]{:S(2)}, u32[]{:S(2)}) collective-permute-start(bf16[128,1536]{1,0:T(8,128)(2,1)S(1)} %bitcast.349), channel_id=1, source_target_pairs={{0,2},{2,4},{4,6},{6,0},{1,3},{3,5},{5,7},{7,1},{8,10},{10,12},{12... | collective-permute-start | bytes 1179656 | tf_op jit(solution)/shard_map/ppermute | solution.py:108
  49.6 24.3 %collective-permute-start.21 = (f32[3,128]{1,0:T(4,128)S(1)}, f32[3,128]{1,0:T(4,128)}, u32[]{:S(2)}, u32[]{:S(2)}) collective-permute-start(f32[3,128]{1,0:T(4,128)S(1)} %bitcast.434), channel_id=1, source_target_pairs={{0,1},{1,0},{2,3},{3,2},{4,5},{5,4},{6,7},{7,6},{8,9},{9,8},{10,11... | collective-permute-start | bytes 4616 | tf_op jit(solution)/shard_map/ppermute | solution.py:154
  51.3 26.6 %collective-permute-start.22 = (f32[3,128]{1,0:T(4,128)S(1)}, f32[3,128]{1,0:T(4,128)}, u32[]{:S(2)}, u32[]{:S(2)}) collective-permute-start(f32[3,128]{1,0:T(4,128)S(1)} %bitcast.435), channel_id=1, source_target_pairs={{0,2},{1,3},{2,4},{3,5},{4,6},{5,7},{6,0},{7,1},{8,10},{9,11},{10,... | collective-permute-start | bytes 4616 | tf_op jit(solution)/shard_map/ppermute | solution.py:154
  51.9 27.5 %collective-permute-start.23 = (f32[3,128]{1,0:T(4,128)S(1)}, f32[3,128]{1,0:T(4,128)S(1)}, u32[]{:S(2)}, u32[]{:S(2)}) collective-permute-start(f32[3,128]{1,0:T(4,128)S(1)} %bitcast.436), channel_id=1, source_target_pairs={{0,3},{1,2},{2,5},{3,4},{4,7},{5,6},{6,1},{7,0},{8,11},{9,10},{10,... | collective-permute-start | bytes 4616 | tf_op jit(solution)/shard_map/ppermute | solution.py:154
  56.0 54.4 %all-to-all-start.3 = ((bf16[4,48,2048]{2,1,0:T(8,128)(2,1)}), bf16[4,48,2048]{2,1,0:T(8,128)(2,1)}, u32[]{:S(2)}, u32[]{:S(2)}) async-start(bf16[4,48,2048]{2,1,0:T(8,128)(2,1)} %pad_maximum_fusion.6), calls=%async_computation.3 | async-start | bytes 1572864 | tf_op jit(solution)/shard_map/all_to_all | solution.py:264
  106.6 23.8 %collective-permute-start.16 = (bf16[128,1536]{1,0:T(8,128)(2,1)}, bf16[128,1536]{1,0:T(8,128)(2,1)}, u32[]{:S(2)}, u32[]{:S(2)}) collective-permute-start(bf16[128,1536]{1,0:T(8,128)(2,1)} %collective-permute-done.15), channel_id=1, source_target_pairs={{0,1},{1,0},{2,3},{3,2},{4,5},{5,4},{6,7},{7,6},{8,9},{9,8},{10,11... | collective-permute-start | bytes 1179656 | tf_op jit(solution)/shard_map/ppermute | solution.py:105
  109.1 20.5 %collective-permute-start.17 = (bf16[128,1536]{1,0:T(8,128)(2,1)}, bf16[128,1536]{1,0:T(8,128)(2,1)}, u32[]{:S(2)}, u32[]{:S(2)}) collective-permute-start(bf16[128,1536]{1,0:T(8,128)(2,1)} %collective-permute-done.15), channel_id=1, source_target_pairs={{0,2},{2,4},{4,6},{6,0},{1,3},{3,5},{5,7},{7,1},{8,10},{10,12},{12... | collective-permute-start | bytes 1179656 | tf_op jit(solution)/shard_map/ppermute | solution.py:108
  110.5 17.4 %all-to-all-start = ((bf16[8,32,512]{2,1,0:T(8,128)(2,1)}), bf16[8,32,512]{2,1,0:T(8,128)(2,1)}, u32[]{:S(2)}, u32[]{:S(2)}) async-start(bf16[8,32,512]{2,1,0:T(8,128)(2,1)} %reshape.703), calls=%async_computation | async-start | bytes 524288 | tf_op jit(solution)/shard_map/all_to_all | solution.py:91
  114.5 225.5 %all-gather.20.cloned.1.call-start = ((), (), s32[]{:S(2)}) async-start(), calls=%async_computation.16 | async-start | bytes 7077888 | tf_op jit(solution)/shard_map/all_gather | solution.py:94
  115.1 237.7 %all-gather.22.cloned.1.call-start = ((), (), s32[]{:S(2)}) async-start(), calls=%async_computation.17 | async-start | bytes 3538944 | tf_op jit(solution)/shard_map/all_gather | solution.py:94
  129.5 16.9 %collective-permute-start.18 = (bf16[128,1536]{1,0:T(8,128)(2,1)}, bf16[128,1536]{1,0:T(8,128)(2,1)S(1)}, u32[]{:S(2)}, u32[]{:S(2)}) collective-permute-start(bf16[128,1536]{1,0:T(8,128)(2,1)} %collective-permute-done.17), channel_id=1, source_target_pairs={{0,1},{1,0},{2,3},{3,2},{4,5},{5,4},{6,7},{7,6},{8,9},{9,8},{10,11... | collective-permute-start | bytes 1179656 | tf_op jit(solution)/shard_map/ppermute | solution.py:105
  169.2 17.3 %collective-permute-start.9 = (f32[768]{0:T(1024)}, f32[768]{0:T(1024)}, u32[]{:S(2)}, u32[]{:S(2)}) collective-permute-start(f32[768]{0:T(1024)} %dynamic-slice_add_fusion), channel_id=1, source_target_pairs={{0,3},{1,2},{2,5},{3,4},{4,7},{5,6},{6,1},{7,0},{8,11},{9,10},{10,... | collective-permute-start | bytes 9224 | tf_op jit(solution)/shard_map/ppermute | solution.py:154
  172.2 16.4 %collective-permute-start.10 = (f32[768]{0:T(1024)}, f32[768]{0:T(1024)}, u32[]{:S(2)}, u32[]{:S(2)}) collective-permute-start(f32[768]{0:T(1024)} %dynamic-slice_add_fusion), channel_id=1, source_target_pairs={{0,4},{1,5},{2,6},{3,7},{4,0},{5,1},{6,2},{7,3},{8,12},{9,13},{10,... | collective-permute-start | bytes 9224 | tf_op jit(solution)/shard_map/ppermute | solution.py:154
  173.7 17.0 %collective-permute-start.11 = (f32[768]{0:T(1024)}, f32[768]{0:T(1024)}, u32[]{:S(2)}, u32[]{:S(2)}) collective-permute-start(f32[768]{0:T(1024)} %dynamic-slice_add_fusion), channel_id=1, source_target_pairs={{0,5},{1,4},{2,7},{3,6},{4,1},{5,0},{6,3},{7,2},{8,13},{9,12},{10,... | collective-permute-start | bytes 9224 | tf_op jit(solution)/shard_map/ppermute | solution.py:154
  175.3 17.4 %collective-permute-start.12 = (f32[768]{0:T(1024)}, f32[768]{0:T(1024)}, u32[]{:S(2)}, u32[]{:S(2)}) collective-permute-start(f32[768]{0:T(1024)} %dynamic-slice_add_fusion), channel_id=1, source_target_pairs={{0,6},{1,7},{2,0},{3,1},{4,2},{5,3},{6,4},{7,5},{8,14},{9,15},{10,... | collective-permute-start | bytes 9224 | tf_op jit(solution)/shard_map/ppermute | solution.py:154
  176.9 17.8 %collective-permute-start.13 = (f32[768]{0:T(1024)}, f32[768]{0:T(1024)}, u32[]{:S(2)}, u32[]{:S(2)}) collective-permute-start(f32[768]{0:T(1024)} %dynamic-slice_add_fusion), channel_id=1, source_target_pairs={{0,7},{1,6},{2,1},{3,0},{4,3},{5,2},{6,5},{7,4},{8,15},{9,14},{10,... | collective-permute-start | bytes 9224 | tf_op jit(solution)/shard_map/ppermute | solution.py:154
  258.9 355.8 %reduce-scatter.10.cloned.1.call-start = ((), (), s32[]{:S(2)}) async-start(), calls=%async_computation.18 | async-start | bytes 737280 | tf_op jit(solution)/shard_map/reduce_scatter | solution.py:97
  258.9 20.5 %collective-permute-start.38 = (bf16[128,1536]{1,0:T(8,128)(2,1)}, bf16[128,1536]{1,0:T(8,128)(2,1)S(1)}, u32[]{:S(2)}, u32[]{:S(2)}) collective-permute-start(bf16[128,1536]{1,0:T(8,128)(2,1)} %get-tuple-element.182), channel_id=1, source_target_pairs={{0,1},{1,0},{2,3},{3,2},{4,5},{5,4},{6,7},{7,6},{8,9},{9,8},{10,11... | collective-permute-start | bytes 1179656 | tf_op jit(solution)/shard_map/ppermute | solution.py:117
  269.5 16.1 %collective-permute-start.37 = (bf16[128,1536]{1,0:T(8,128)(2,1)}, bf16[128,1536]{1,0:T(8,128)(2,1)S(1)}, u32[]{:S(2)}, u32[]{:S(2)}) collective-permute-start(bf16[128,1536]{1,0:T(8,128)(2,1)} %get-tuple-element.183), channel_id=1, source_target_pairs={{0,1},{1,0},{2,3},{3,2},{4,5},{5,4},{6,7},{7,6},{8,9},{9,8},{10,11... | collective-permute-start | bytes 1179656 | tf_op jit(solution)/shard_map/ppermute | solution.py:117
  280.6 15.8 %collective-permute-start.36 = (bf16[128,1536]{1,0:T(8,128)(2,1)}, bf16[128,1536]{1,0:T(8,128)(2,1)}, u32[]{:S(2)}, u32[]{:S(2)}) collective-permute-start(bf16[128,1536]{1,0:T(8,128)(2,1)} %get-tuple-element.180), channel_id=1, source_target_pairs={{0,1},{1,0},{2,3},{3,2},{4,5},{5,4},{6,7},{7,6},{8,9},{9,8},{10,11... | collective-permute-start | bytes 1179656 | tf_op jit(solution)/shard_map/ppermute | solution.py:117
  308.3 20.6 %collective-permute-start.49 = (bf16[128,1536]{1,0:T(8,128)(2,1)S(1)}, bf16[128,1536]{1,0:T(8,128)(2,1)S(1)}, u32[]{:S(2)}, u32[]{:S(2)}) collective-permute-start(bf16[128,1536]{1,0:T(8,128)(2,1)S(1)} %bitcast.388), channel_id=1, source_target_pairs={{0,2},{2,4},{4,6},{6,0},{1,3},{3,5},{5,7},{7,1},{8,10},{10,12},{12... | collective-permute-start | bytes 1179656 | tf_op jit(solution)/shard_map/ppermute | solution.py:131
  364.7 16.4 %collective-permute-start.46 = (bf16[128,1536]{1,0:T(8,128)(2,1)S(1)}, bf16[128,1536]{1,0:T(8,128)(2,1)S(1)}, u32[]{:S(2)}, u32[]{:S(2)}) collective-permute-start(bf16[128,1536]{1,0:T(8,128)(2,1)S(1)} %slice.277), channel_id=1, source_target_pairs={{0,2},{2,4},{4,6},{6,0},{1,3},{3,5},{5,7},{7,1},{8,10},{10,12},{12... | collective-permute-start | bytes 1179656 | tf_op jit(solution)/shard_map/ppermute | solution.py:143
  473.1 189.4 %reduce-scatter.16.cloned.1.call-start = ((), (), s32[]{:S(2)}) async-start(), calls=%async_computation.21 | async-start | bytes 2457600 | tf_op jit(solution)/shard_map/reduce_scatter | solution.py:97
  488.4 211.2 %reduce-scatter.12.cloned.1.call-start = ((), (), s32[]{:S(2)}) async-start(), calls=%async_computation.19 | async-start | bytes 7077888 | tf_op jit(solution)/shard_map/reduce_scatter | solution.py:97
  497.2 208.1 %reduce-scatter.14.cloned.1.call-start = ((), (), s32[]{:S(2)}) async-start(), calls=%async_computation.20 | async-start | bytes 3538944 | tf_op jit(solution)/shard_map/reduce_scatter | solution.py:97
  511.4 198.6 %reduce-scatter.18.cloned.1.call-start = ((), (), s32[]{:S(2)}) async-start(), calls=%async_computation.22 | async-start | bytes 3932160
  522.6 33.1 %collective-permute-start.65 = (bf16[128,1536]{1,0:T(8,128)(2,1)S(1)}, bf16[128,1536]{1,0:T(8,128)(2,1)S(1)}, u32[]{:S(2)}, u32[]{:S(2)}) collective-permute-start(bf16[128,1536]{1,0:T(8,128)(2,1)S(1)} %get-tuple-element.177), channel_id=1, source_target_pairs={{0,1},{1,0},{2,3},{3,2},{4,5},{5,4},{6,7},{7,6},{8,9},{9,8},{10,11... | collective-permute-start | bytes 1179656 | tf_op jit(solution)/shard_map/ppermute | solution.py:117
  522.7 52.8 %collective-permute-start.64 = (bf16[128,1536]{1,0:T(8,128)(2,1)S(1)}, bf16[128,1536]{1,0:T(8,128)(2,1)S(1)}, u32[]{:S(2)}, u32[]{:S(2)}) collective-permute-start(bf16[128,1536]{1,0:T(8,128)(2,1)S(1)} %get-tuple-element.178), channel_id=1, source_target_pairs={{0,1},{1,0},{2,3},{3,2},{4,5},{5,4},{6,7},{7,6},{8,9},{9,8},{10,11... | collective-permute-start | bytes 1179656 | tf_op jit(solution)/shard_map/ppermute | solution.py:117
  524.6 63.6 %collective-permute-start.63 = (bf16[128,1536]{1,0:T(8,128)(2,1)}, bf16[128,1536]{1,0:T(8,128)(2,1)}, u32[]{:S(2)}, u32[]{:S(2)}) collective-permute-start(bf16[128,1536]{1,0:T(8,128)(2,1)} %get-tuple-element.179), channel_id=1, source_target_pairs={{0,1},{1,0},{2,3},{3,2},{4,5},{5,4},{6,7},{7,6},{8,9},{9,8},{10,11... | collective-permute-start | bytes 1179656 | tf_op jit(solution)/shard_map/ppermute | solution.py:117
  527.3 28.3 %collective-permute-start.71 = (bf16[256,384]{0,1:T(8,128)(2,1)S(1)}, bf16[256,384]{0,1:T(8,128)(2,1)S(1)}, u32[]{:S(2)}, u32[]{:S(2)}) collective-permute-start(bf16[256,384]{0,1:T(8,128)(2,1)S(1)} %collective-permute-done.70), channel_id=1, source_target_pairs={{0,1},{1,0},{2,3},{3,2},{4,5},{5,4},{6,7},{7,6},{8,9},{9,8},{10,11... | collective-permute-start | bytes 589832 | tf_op jit(solution)/shard_map/ppermute | solution.py:105
  535.7 29.6 %collective-permute-start.73 = (bf16[256,384]{0,1:T(8,128)(2,1)S(1)}, bf16[256,384]{0,1:T(8,128)(2,1)S(1)}, u32[]{:S(2)}, u32[]{:S(2)}) collective-permute-start(bf16[256,384]{0,1:T(8,128)(2,1)S(1)} %collective-permute-done.72), channel_id=1, source_target_pairs={{0,1},{1,0},{2,3},{3,2},{4,5},{5,4},{6,7},{7,6},{8,9},{9,8},{10,11... | collective-permute-start | bytes 589832 | tf_op jit(solution)/shard_map/ppermute | solution.py:105
  555.8 19.7 %collective-permute-start.66 = (bf16[128,1536]{1,0:T(8,128)(2,1)S(1)}, bf16[128,1536]{1,0:T(8,128)(2,1)S(1)}, u32[]{:S(2)}, u32[]{:S(2)}) collective-permute-start(bf16[128,1536]{1,0:T(8,128)(2,1)S(1)} %add_convert_fusion.2), channel_id=1, source_target_pairs={{0,2},{2,4},{4,6},{6,0},{1,3},{3,5},{5,7},{7,1},{8,10},{10,12},{12... | collective-permute-start | bytes 1179656 | tf_op jit(solution)/shard_map/ppermute | solution.py:121
  591.6 16.1 %collective-permute-start.85 = (f32[37,128]{1,0:T(8,128)}, f32[37,128]{1,0:T(8,128)}, u32[]{:S(2)}, u32[]{:S(2)}) collective-permute-start(f32[37,128]{1,0:T(8,128)} %maximum_bitcast_fusion.1), channel_id=1, source_target_pairs={{0,3},{1,2},{2,5},{3,4},{4,7},{5,6},{6,1},{7,0},{8,11},{9,10},{10,... | collective-permute-start | bytes 56840 | tf_op jit(solution)/shard_map/ppermute | solution.py:154
  597.0 20.5 %collective-permute-start.62 = (bf16[128,1536]{1,0:T(8,128)(2,1)}, bf16[128,1536]{1,0:T(8,128)(2,1)S(1)}, u32[]{:S(2)}, u32[]{:S(2)}) collective-permute-start(bf16[128,1536]{1,0:T(8,128)(2,1)} %get-tuple-element.176), channel_id=1, source_target_pairs={{0,1},{1,0},{2,3},{3,2},{4,5},{5,4},{6,7},{7,6},{8,9},{9,8},{10,11... | collective-permute-start | bytes 1179656 | tf_op jit(solution)/shard_map/ppermute | solution.py:117
  597.5 20.0 %collective-permute-start.68 = (bf16[128,1536]{1,0:T(8,128)(2,1)}, bf16[128,1536]{1,0:T(8,128)(2,1)S(1)}, u32[]{:S(2)}, u32[]{:S(2)}) collective-permute-start(bf16[128,1536]{1,0:T(8,128)(2,1)} %add_convert_fusion), channel_id=1, source_target_pairs={{0,2},{2,4},{4,6},{6,0},{1,3},{3,5},{5,7},{7,1},{8,10},{10,12},{12... | collective-permute-start | bytes 1179656 | tf_op jit(solution)/shard_map/ppermute | solution.py:121
  601.7 24.1 %all-to-all-start.4 = ((bf16[8,32,512]{2,1,0:T(8,128)(2,1)}), bf16[8,32,512]{2,1,0:T(8,128)(2,1)}, u32[]{:S(2)}, u32[]{:S(2)}) async-start(bf16[8,32,512]{2,1,0:T(8,128)(2,1)} %bitcast.78), calls=%async_computation.4 | async-start | bytes 524288 | tf_op jit(solution)/shard_map/all_to_all | solution.py:91
  614.7 15.5 %collective-permute-start.104 = (bf16[48,1536]{1,0:T(8,128)(2,1)}, bf16[48,1536]{1,0:T(8,128)(2,1)}, u32[]{:S(2)}, u32[]{:S(2)}) collective-permute-start(bf16[48,1536]{1,0:T(8,128)(2,1)} %reduce-scatter.10.cloned.1.call-done), channel_id=1, source_target_pairs={{0,0},{8,1},{16,2},{24,3},{1,4},{9,5},{17,6},{25,7},{2,8},{10,9},{... | collective-permute-start | bytes 442376 | tf_op jit(solution)/shard_map/ppermute | solution.py:377
  619.7 17.2 %collective-permute-start.82 = (f32[12,128]{1,0:T(8,128)S(1)}, f32[12,128]{1,0:T(8,128)}, u32[]{:S(2)}, u32[]{:S(2)}) collective-permute-start(f32[12,128]{1,0:T(8,128)S(1)} %bitcast.407), channel_id=1, source_target_pairs={{0,7},{1,6},{2,1},{3,0},{4,3},{5,2},{6,5},{7,4},{8,15},{9,14},{10,... | collective-permute-start | bytes 18440 | tf_op jit(solution)/shard_map/ppermute | solution.py:154
  654.4 15.4 %collective-permute-start.95 = (f32[1,1024]{1,0:T(1,128)S(1)}, f32[1,1024]{1,0:T(1,128)S(1)}, u32[]{:S(2)}, u32[]{:S(2)}) collective-permute-start(f32[1,1024]{1,0:T(1,128)S(1)} %fusion.98), channel_id=1, source_target_pairs={{0,6},{1,7},{2,0},{3,1},{4,2},{5,3},{6,4},{7,5},{8,14},{9,15},{10,... | collective-permute-start | bytes 12296 | tf_op jit(solution)/shard_map/ppermute | solution.py:154
  657.2 16.2 %collective-permute-start.94 = (f32[1,1024]{1,0:T(1,128)S(1)}, f32[1,1024]{1,0:T(1,128)S(1)}, u32[]{:S(2)}, u32[]{:S(2)}) collective-permute-start(f32[1,1024]{1,0:T(1,128)S(1)} %fusion.98), channel_id=1, source_target_pairs={{0,5},{1,4},{2,7},{3,6},{4,1},{5,0},{6,3},{7,2},{8,13},{9,12},{10,... | collective-permute-start | bytes 12296 | tf_op jit(solution)/shard_map/ppermute | solution.py:154
  662.5 37.1 %all-to-all-start.5 = ((bf16[8,48,576]{2,1,0:T(8,128)(2,1)}), bf16[8,48,576]{2,1,0:T(8,128)(2,1)S(1)}, u32[]{:S(2)}, u32[]{:S(2)}) async-start(bf16[8,48,576]{2,1,0:T(8,128)(2,1)} %bitcast.382), calls=%async_computation.5 | async-start | bytes 983040 | tf_op jit(solution)/shard_map/all_to_all | solution.py:91
  681.2 16.4 %collective-permute-start.99 = (f32[512]{0:T(512)S(1)}, f32[512]{0:T(512)S(1)}, u32[]{:S(2)}, u32[]{:S(2)}) collective-permute-start(f32[512]{0:T(512)S(1)} %bitcast.429), channel_id=1, source_target_pairs={{0,3},{1,2},{2,5},{3,4},{4,7},{5,6},{6,1},{7,0},{8,11},{9,10},{10,... | collective-permute-start | bytes 6152 | tf_op jit(solution)/shard_map/ppermute | solution.py:154
  699.6 23.9 %all-to-all-start.6 = ((bf16[4,48,2048]{2,1,0:T(8,128)(2,1)}), bf16[4,48,2048]{2,1,0:T(8,128)(2,1)S(1)}, u32[]{:S(2)}, u32[]{:S(2)}) async-start(bf16[4,48,2048]{2,1,0:T(8,128)(2,1)} %bitcast.377), calls=%async_computation.8 | async-start | bytes 1572864 | tf_op jit(solution)/shard_map/all_to_all | solution.py:368
  (204 other events, 2434.7 us)
Sparse Core Ops, SparseCore 0:
  9.6 19.4 all-gather.11
  30.6 19.6 all-gather.13
  51.9 22.1 all-gather.15
  76.1 31.6 all-gather.17
  117.0 56.4 all-gather.19
  259.0 37.4 all-gather.21
  473.2 19.9 reduce-scatter.9
  495.8 30.6 reduce-scatter.15
  530.4 71.3 reduce-scatter.11
  605.0 48.7 reduce-scatter.13
  656.5 37.9 reduce-scatter.17

commit v3 on v2

--- a/solution.py
+++ b/solution.py
@@ -76,6 +76,10 @@
     return jnp.einsum(spec, a, b, preferred_element_type=f32)
 
 
+def tie(*arrays):
+    return lax.optimization_barrier(arrays)
+
+
 def make_body(clips, outer, ring, pair):
     inner = ring * pair
     shards = clips * outer
@@ -143,33 +147,31 @@
                 passed = lax.ppermute(total.astype(bf16), "ring", forward)
         return total
 
-    def direct(x, k, e):
-        if k == 0 and e == 0:
-            return x
-        moves = [
-            (z * pair + y, (z + k) % ring * pair + (y + e) % pair)
-            for z in range(ring)
-            for y in range(pair)
-        ]
-        return lax.ppermute(x, team, moves)
+    def small_sum(x):
+        for axis, size in (("pair", pair), ("ring", ring)):
+            if size & (size - 1):
+                x = lax.psum(x, axis)
+                continue
+            hop = 1
+            while hop < size:
+                x = x + lax.ppermute(x, axis, [(i, i ^ hop) for i in range(size)])
+                hop *= 2
+        return x
 
     def small_gather(x):
-        return [direct(x, k, e) for k, e in slots]
-
-    def small_sum(x):
-        parts = small_gather(x)
-        total = parts[0]
-        for part in parts[1:]:
-            total = total + part
-        return total
+        return swap_team(jnp.broadcast_to(x, (inner,) + x.shape))
 
     def in_order(parts):
         z, y = lax.axis_index("ring"), lax.axis_index("pair")
-        whole = jnp.zeros((inner,) + parts[0].shape, parts[0].dtype)
-        for (k, e), part in zip(slots, parts):
-            spot = lax.rem(z + ring - k, ring) * pair + lax.rem(y + pair - e, pair)
-            whole = lax.dynamic_update_index_in_dim(whole, part, spot, 0)
-        return whole
+        if pair > 1:
+            front = [jnp.where(y == 0, parts[2 * k], parts[2 * k + 1]) for k in range(ring)]
+            behind = [jnp.where(y == 0, parts[2 * k + 1], parts[2 * k]) for k in range(ring)]
+            rows = [jnp.stack([f, g]) for f, g in zip(front, behind)]
+        else:
+            rows = [part[None] for part in parts]
+        twice = jnp.stack((rows[1:] + rows)[::-1])
+        whole = lax.dynamic_slice_in_dim(twice, ring - 1 - z, ring)
+        return whole.reshape((inner,) + parts[0].shape)
 
     def slot_blocks(x):
         z, y = lax.axis_index("ring"), lax.axis_index("pair")
@@ -232,59 +234,69 @@
         cap_rows = caption.shape[1]
         cond_width = w_pool.shape[1]
         mod_width = b_ada.shape[0]
-        mod_own = mod_width // inner
         attn_scale = 1.0 / math.sqrt(head_dim)
         member = lax.axis_index(team)
         shard = lax.axis_index(spread)
         length_f = lengths[0].astype(f32)
 
-        cap_part = swap_team(by_columns(caption[0])).reshape(inner * cap_rows, -1)
+        cap_blocks = by_columns(caption[0])
+        cap_part = swap_team(cap_blocks).reshape(inner * cap_rows, -1)
         cap_own = cap_part
         if outer > 1:
             cap_part = lax.all_gather(cap_part, "outer", axis=0, tiled=True)
         cap_len = cap_part.shape[0]
-        pool_s = gather_spread(w_pool)
-        time_s = gather_spread(w_time)
-        rows = w_ada.shape[0]
-        ada_blocks = w_ada.reshape(rows, inner, mod_own).transpose(1, 0, 2)
-        ada_s = gather_spread(swap_team(ada_blocks).reshape(inner * rows, mod_own))
+        pool_rows, time_rows, ada_rows = w_pool.shape[0], w_time.shape[0], w_ada.shape[0]
+        pool_s = gather_spread(jnp.concatenate([w_pool, w_time], 0))
+        ada_s = gather_spread(w_ada)
         rows = w_qkv.shape[0]
         qkv_blocks = w_qkv.reshape(rows, 3, inner, own).transpose(2, 0, 1, 3)
         qkv_blocks = qkv_blocks.reshape(inner, rows, 3 * own)
         qkv_s = gather_spread(swap_team(qkv_blocks).reshape(inner * rows, 3 * own))
-        tokens_all = jnp.concatenate(ring_gather(tokens[0]), 0)
-        spots = jnp.concatenate(small_gather(positions[:, 0, :].astype(f32)), 1)
-        text_s = gather_spread(jnp.concatenate([w_key_text, w_value_text], -1))
+        spots = positions[:, 0, :].astype(bf16).T
+        spots = jnp.concatenate([spots, jnp.zeros((tok_rows, 125), bf16)], -1)
+        tokens_all = jnp.concatenate(
+            ring_gather(jnp.concatenate([tokens[0], spots], -1)), 0
+        )
+        spots = tokens_all[:, width : width + 3].astype(f32).T
+        tokens_all = tokens_all[:, :width]
         to_heads = [
             (r, (r % shards) * inner + r // shards) for r in range(shards * inner)
         ]
         from_heads = [(b, a) for a, b in to_heads]
-        out_s = gather_spread(lax.ppermute(w_out, every, to_heads))
-        ffn_blocks = jnp.concatenate([line_columns(w_gate), line_columns(w_up)], -1)
+        out_rows = lax.ppermute(w_out, every, to_heads)
+        text_rows = w_key_text.shape[0]
+
+        cap_mask = (jnp.arange(cap_len) < lengths[0]).astype(f32)
+        pooled = jnp.sum(cap_part.astype(f32) * cap_mask[:, None], 0) / length_f
+        pooled_b = pooled.astype(bf16)
+        embed_width = time_rows * shards * inner
+        time_embed = timestep_embed(timesteps[0], embed_width).astype(bf16)
+        time_own = lax.dynamic_index_in_dim(
+            time_embed.reshape(shards, inner, time_rows), member, 1, keepdims=False
+        )
+        facts = jnp.concatenate([pooled_b.reshape(shards, pool_rows), time_own], 1)
+        condition = small_sum(dot(facts.reshape(1, -1), pool_s))
+        cond_b = jax.nn.silu(condition).astype(bf16)
+        cond_own = lax.dynamic_index_in_dim(
+            cond_b.reshape(shards, inner, ada_rows), member, 1, keepdims=False
+        ).reshape(1, -1)
+        modulation = small_sum(dot(cond_own, ada_s)).reshape(-1) + b_ada
+        scale_attn, gate_attn, scale_ffn, gate_ffn = jnp.split(modulation, 4)
+        tanh_attn = jnp.tanh(gate_attn)
+        tanh_ffn = jnp.tanh(gate_ffn)
+        text_pack = jnp.concatenate([w_key_text, w_value_text, out_rows], 0)
+        text_pack = gather_spread(text_pack).reshape(shards, -1, width)
+        key_s = text_pack[:, :text_rows].reshape(-1, width)
+        value_s = text_pack[:, text_rows : 2 * text_rows].reshape(-1, width)
+        out_s = text_pack[:, 2 * text_rows :].reshape(-1, width)
+        gate_in, up_in, down_in, condition = tie(w_gate, w_up, w_down, condition)
+        ffn_blocks = jnp.concatenate([line_columns(gate_in), line_columns(up_in)], -1)
         ffn_blocks = lax.all_to_all(ffn_blocks, "ring", split_axis=0, concat_axis=0, tiled=True)
         ffn_s = gather_spread(ffn_blocks.reshape(ring * rows, -1), spread_ffn)
         ffn_s = ffn_s.reshape(shards, pair, ring, rows, -1).transpose(0, 2, 1, 3, 4)
         ffn_s = ffn_s.reshape(width, -1)
-        down_s = gather_spread(w_down, spread_ffn)
+        down_s = gather_spread(down_in, spread_ffn)
         ff_own = down_s.shape[0]
-        cot_all = line_gather(cotangent[0])
-
-        cap_mask = (jnp.arange(cap_len) < lengths[0]).astype(f32)
-        pooled = jnp.sum(cap_part.astype(f32) * cap_mask[:, None], 0) / length_f
-        pooled_b = pooled.astype(bf16)
-        time_rows = w_time.shape[0]
-        embed_width = time_rows * shards * inner
-        time_embed = timestep_embed(timesteps[0], embed_width).astype(bf16)
-        time_own = lax.dynamic_index_in_dim(
-            time_embed.reshape(shards, inner, time_rows), member, 1, keepdims=False
-        ).reshape(1, -1)
-        condition = small_sum(dot(pooled_b[None], pool_s) + dot(time_own, time_s))
-        cond_b = jax.nn.silu(condition).astype(bf16)
-        bias_own = lax.dynamic_slice_in_dim(b_ada, member * mod_own, mod_own)
-        modulation = in_order(small_gather(dot(cond_b, ada_s)[0] + bias_own)).reshape(-1)
-        scale_attn, gate_attn, scale_ffn, gate_ffn = jnp.split(modulation, 4)
-        tanh_attn = jnp.tanh(gate_attn)
-        tanh_ffn = jnp.tanh(gate_ffn)
         packed = jnp.concatenate(
             [
                 modulation,
@@ -298,6 +310,8 @@
         normed_all, _ = rms_norm(tokens_all.astype(f32), epsilon)
         gain1 = norm1_gain * (1.0 + scale_attn)
         mix_in = (normed_all * gain1).astype(bf16)
+        cot_in, mix_in = tie(cotangent[0], mix_in)
+        cot_all = line_gather(cot_in)
         qkv_own = dot(mix_in, qkv_s).reshape(team_rows, 3, heads, head_dim).transpose(1, 2, 0, 3)
         cos_tab, sin_tab = rope_tables(spots, head_dim // 2)
         queries_n, inverse_q = rms_norm(qkv_own[0], head_eps)
@@ -315,8 +329,8 @@
         self_out = ein("hqk,hkd->hqd", raised.astype(bf16), values_b) / total
         log_sum = top + jnp.log(total)
 
-        text_part = dot(cap_part, text_s).astype(bf16)
-        text_part = text_part.reshape(cap_len, 2, inner, own).transpose(2, 0, 1, 3)
+        text_part = jnp.stack([dot(cap_part, key_s), dot(cap_part, value_s)]).astype(bf16)
+        text_part = text_part.reshape(2, cap_len, inner, own).transpose(2, 1, 0, 3)
         text_own = ring_scatter(slot_blocks(text_part.reshape(inner, cap_len, 2 * own)))
         text_own = text_own.reshape(cap_len, 2, heads, head_dim).transpose(1, 2, 0, 3)
         text_keys_n, inverse_t = rms_norm(text_own[0], head_eps)
@@ -355,10 +369,7 @@
             -1,
         )
         d_ffn_in = line_scatter(dot_nt(d_gate_up, ffn_s).astype(bf16))
-        ffn_out = line_scatter(dot(hidden_b, down_s).astype(bf16))
-        mixed_out = (resid + tanh_ffn * ffn_out).astype(bf16)
         d_out = cotangent[0].astype(f32)
-        sum_gate_ffn = jnp.sum(d_out * ffn_out, 0)
         grad_down = dot_tn(hidden_b, d_ffn_b).astype(bf16)
         sum_down = scatter_spread(grad_down, spread_ffn).astype(f32)
         grad_ffn = dot_tn(ffn_in, d_gate_up).astype(bf16)
@@ -373,6 +384,10 @@
         d_resid = d_out + norm_back(normed2, inverse2, d_ffn_in * gain2)
         sum_gate_attn = jnp.sum(d_resid * attn_out, 0)
         d_attn_b = jnp.concatenate(ring_gather((tanh_attn * d_resid).astype(bf16)), 0)
+        hidden_b, d_attn_b = tie(hidden_b, d_attn_b)
+        ffn_out = line_scatter(dot(hidden_b, down_s).astype(bf16))
+        mixed_out = (resid + tanh_ffn * ffn_out).astype(bf16)
+        sum_gate_ffn = jnp.sum(d_out * ffn_out, 0)
         grad_out = dot_tn(mixed_b, d_attn_b).astype(bf16)
         sum_out = lax.ppermute(scatter_spread(grad_out), every, from_heads).astype(f32)
         d_mixed = dot_nt(d_attn_b, out_s).reshape(team_rows, heads, head_dim).transpose(1, 0, 2)
@@ -398,12 +413,12 @@
             text_grads = lax.dynamic_slice_in_dim(
                 text_grads, lax.axis_index("outer") * inner * cap_rows, inner * cap_rows
             )
-        text_rows = text_grads.shape[0]
-        text_grads = in_order(ring_gather(text_grads)).reshape(inner, text_rows, 2, own)
-        text_grads = text_grads.transpose(1, 2, 0, 3).reshape(text_rows, 2 * width)
+        grad_rows = text_grads.shape[0]
+        text_grads = in_order(ring_gather(text_grads)).reshape(inner, grad_rows, 2, own)
+        text_grads = text_grads.transpose(2, 1, 0, 3).reshape(2, grad_rows, width)
+        text_grads = jnp.concatenate([text_grads[0], text_grads[1]], -1)
         sum_text = scatter_spread(dot_tn(cap_own, text_grads).astype(bf16)).astype(f32)
-        d_cap = dot_nt(text_grads, text_s).astype(bf16).reshape(inner, cap_rows, -1)
-        d_cap = back_columns(swap_team(d_cap)).astype(f32)
+        d_cap = dot_nt(text_grads[:, :width], key_s) + dot_nt(text_grads[:, width:], value_s)
 
         row_dots = jnp.sum(d_self_b.astype(f32) * self_out, -1, keepdims=True)
         soft_probs = jnp.exp(scores - log_sum)
@@ -419,6 +434,7 @@
         d_keys_raw = norm_back(keys_n, inverse_k, rotate(d_keys, cos_tab, -sin_tab))
         d_qkv = jnp.stack([d_queries_raw, d_keys_raw, d_values]).astype(bf16)
         d_qkv = d_qkv.transpose(2, 0, 1, 3).reshape(team_rows, 3 * own)
+        d_qkv, sum_ffn, sum_down = tie(d_qkv, sum_ffn, sum_down)
         d_mix_in = ring_scatter(row_blocks(dot_nt(d_qkv, qkv_s).astype(bf16)))
         sum_qkv = scatter_spread(dot_tn(mix_in, d_qkv).astype(bf16))
         sum_qkv = swap_team(sum_qkv.reshape(inner, rows, 3 * own)).reshape(inner, rows, 3, own)
@@ -460,29 +476,30 @@
         grad_bias = jnp.sum(d_modulation, 0)
         grad_cross_gate = jnp.sum(sums[:, mod_width : mod_width + head_count], 0)
         row = shard * inner + member
-        ada_rows = w_ada.shape[0]
         cond_rows = lax.dynamic_slice_in_dim(
             jax.nn.silu(cond_all).astype(bf16).astype(f32), row * ada_rows, ada_rows, 1
         )
         sum_ada = jnp.sum(cond_rows[:, :, None] * d_modulation[:, None, :], 0)
         d_mod_clip = lax.dynamic_index_in_dim(d_modulation, lax.axis_index("clip"), 0)
-        d_mod_own = lax.dynamic_slice_in_dim(d_mod_clip, member * mod_own, mod_own, 1)
-        d_cond_act = small_sum(dot_nt(d_mod_own.astype(bf16), ada_s))
+        d_cond_own = dot_nt(d_mod_clip.astype(bf16), ada_s)
+        d_cond_act = small_gather(d_cond_own.reshape(shards, ada_rows))
+        d_cond_act = d_cond_act.transpose(1, 0, 2).reshape(1, cond_width)
         sigmoid_c = jax.nn.sigmoid(condition)
         d_condition = d_cond_act * sigmoid_c * (1.0 + condition * (1.0 - sigmoid_c))
         d_cond_all = lax.all_gather(d_condition[0], "clip", axis=0)
-        d_pooled = in_order(small_gather(dot_nt(d_condition.astype(bf16), pool_s)[0]))
-        d_pooled = d_pooled.reshape(inner, shards, -1).transpose(1, 0, 2).reshape(1, -1)
-        seq_row = lax.axis_index(("outer", "ring", "pair"))
-        local_mask = (seq_row * cap_rows + jnp.arange(cap_rows) < lengths[0]).astype(f32)
-        d_caption = d_cap + local_mask[:, None] * d_pooled / length_f
+        d_pooled = dot_nt(d_condition.astype(bf16), pool_s).reshape(shards, -1)
+        d_pooled = d_pooled[:, :pool_rows].reshape(1, -1)
+        first = lax.axis_index("outer") * grad_rows
+        own_mask = (first + jnp.arange(grad_rows) < lengths[0]).astype(f32)
+        d_cap = (d_cap + own_mask[:, None] * d_pooled / length_f).astype(bf16)
+        d_caption = back_columns(swap_team(d_cap.reshape(inner, cap_rows, -1))).astype(f32)
         embed_all = timestep_embed(steps_all, embed_width).astype(bf16).astype(f32)
         embed_rows = lax.dynamic_slice_in_dim(embed_all, row * time_rows, time_rows, 1)
         sum_time = jnp.sum(embed_rows[:, :, None] * d_cond_all[:, None, :], 0)
-        pool_rows = lax.dynamic_slice_in_dim(
-            pool_all.astype(bf16).astype(f32), shard * w_pool.shape[0], w_pool.shape[0], 1
-        )
-        sum_pool = jnp.sum(pool_rows[:, :, None] * d_cond_all[:, None, :], 0)
+        pooled_rows = lax.dynamic_slice_in_dim(
+            pool_all.astype(bf16).astype(f32), shard * pool_rows, pool_rows, 1
+        )
+        sum_pool = jnp.sum(pooled_rows[:, :, None] * d_cond_all[:, None, :], 0)
         return (
             mixed_out[None],
             d_tokens[None],

time: 745 us -> 674 us (0.905)
  starting transfers between devices: 146 us -> 106 us
  blocking collectives: 77.8 us -> 42.2 us
  matrix products: 93.6 us -> 103 us
    ppermute x50 -> x13, starting transfers between devices: 80.8 us -> 17.4 us  [the longest x12 16.8 us: small_sum(): x = x + lax.ppermute(x, axis, [(i, i ^ hop) for i in range(size)])]
    ppermute x9, waiting for transfers between devices: 29.7 us -> 53 us  [ring_scatter(): passed = lax.ppermute(total.astype(bf16), 'ring', forward)]
    ppermute x12, waiting for transfers between devices: 24.6 us -> 45.3 us  [ring_scatter(): total = total + lax.ppermute(block_of(k, 1), 'pair', crossed).astype(f32)]
    all_gather x2 -> x0, blocking collectives: 20.4 us -> none  [gather_spread(): return lax.all_gather(x, axes, axis=0, tiled=True)]
    ppermute x12, waiting for transfers between devices: 36.9 us -> 21 us  [ring_gather(): other = lax.ppermute(other, 'pair', crossed)]
    all_to_all x2 -> x1, blocking collectives: 36.3 us -> 21 us  [swap_team(): return lax.all_to_all(x, team, split_axis=0, concat_axis=0, tiled=True)]
    ppermute x9, waiting for transfers between devices: 56.5 us -> 45 us  [ring_gather(): now = lax.ppermute(now, 'ring', forward)]
    dynamic_update_slice x24 -> x0, local copies, waits for them, and re-layouts: 11.5 us -> none  [in_order(): whole = lax.dynamic_update_index_in_dim(whole, part, spot, 0)]
  transfers between devices with their start and end apart: 121 -> 85, of which waited for: 44 -> 50; matrix products, arithmetic and copies ran while one was open for 26% -> 33% of each run, Pallas kernels for 0% -> 0%
where the time goes in v3:
time: 674 us; the launch traced here: 667 us
  waiting for transfers between devices  256 us (38%)
  starting transfers between devices  106 us (16%)
  matrix products  103 us (15%)
  local copies, waits for them, and re-layouts  77.8 us (12%)
  other arithmetic  64.7 us (10%)
  blocking collectives  42.2 us (6%)
  between operations  18 us (3%)
    ppermute x9, waiting for transfers between devices, ring_scatter(): passed = lax.ppermute(total.astype(bf16), 'ring', forward)  53 us
    ppermute x12, waiting for transfers between devices, ring_scatter(): total = total + lax.ppermute(block_of(k, 1), 'pair', crossed).astype(f32)  45.3 us
    ppermute x9, waiting for transfers between devices, ring_gather(): now = lax.ppermute(now, 'ring', forward)  45 us
    ppermute x6, waiting for transfers between devices, line_scatter(): passed = lax.ppermute(total.astype(bf16), 'ring', forward)  34.1 us
    unnamed x293, local copies, waits for them, and re-layouts  31.6 us
    dot_general x11, matrix products, ein(): return jnp.einsum(spec, a, b, preferred_element_type=f32)  30.8 us
    ppermute x6, waiting for transfers between devices, line_gather(): parts.append(lax.ppermute(parts[-1], 'ring', forward))  29.4 us
    dot_general x8, matrix products, dot_nt(): lax.dot_general(a, b, (((1,), (1,)), ((), ())), preferred_element_type=f32)  27.1 us
  transfers between devices with their start and end apart: 85, of which 50 were waited for; matrix products, arithmetic and copies ran while one was open for 33% of the time, Pallas kernels for 0%

profile of v3, /device:TPU:0, one launch (start us, length us, event | category | flops | bytes accessed | tf_op | source)
XLA Modules:
  0.0 666.8 jit_solution(11242169963690383521)
XLA Ops:
  12.3 21.0 %all_to_all.35 = bf16[8,48,576]{2,1,0:T(8,128)(2,1)} all-to-all(bf16[8,48,576]{2,1,0:T(8,128)(2,1)S(1)} %reshape.647), channel_id=1, replica_groups=mesh['clip'=4,'outer'=1,'ring'=4,'pair'=2] {'ring','pair'}, dimensions={0} | all-to-all | bytes 884736 | tf_op jit(solution)/shard_map/all_to_all | solution.py:95
  36.2 12.6 %collective-permute-start.6 = (bf16[128,1664]{1,0:T(8,128)(2,1)}, bf16[128,1664]{1,0:T(8,128)(2,1)}, u32[]{:S(2)}, u32[]{:S(2)}) collective-permute-start(bf16[128,1664]{1,0:T(8,128)(2,1)} %concatenate.87), channel_id=1, source_target_pairs={{0,1},{1,0},{2,3},{3,2},{4,5},{5,4},{6,7},{7,6},{8,9},{9,8},{10,11... | collective-permute-start | bytes 1277960 | tf_op jit(solution)/shard_map/ppermute | solution.py:109
  49.7 5.1 all-to-all-start
  58.9 6.0 all-to-all-done
  77.0 4.6 collective-permute-done.2
  96.2 4.6 all-to-all-start.2
  108.6 14.6 %collective-permute-done.11 = bf16[128,1664]{1,0:T(8,128)(2,1)} collective-permute-done((bf16[128,1664]{1,0:T(8,128)(2,1)}, bf16[128,1664]{1,0:T(8,128)(2,1)}, u32[]{:S(2)}, u32[]{:S(2)}) %collective-permute-start.11) | collective-permute-done | bytes 426016 | tf_op jit(solution)/shard_map/ppermute | solution.py:112
  127.2 4.9 collective-permute-done.12
  141.3 6.3 collective-permute-start.4
  159.9 4.5 fusion.162
  173.4 8.3 %collective-permute-done.17 = bf16[256,384]{0,1:T(8,128)(2,1)S(1)} collective-permute-done((bf16[256,384]{0,1:T(8,128)(2,1)S(1)}, bf16[256,384]{0,1:T(8,128)(2,1)S(1)}, u32[]{:S(2)}, u32[]{:S(2)}) %collective-permute-start.17) | collective-permute-done | bytes 196640 | tf_op jit(solution)/shard_map/ppermute | solution.py:121
  193.3 6.0 collective-permute-done.19
  213.3 8.0 %fusion.52 = (bf16[1024,3,64]{0,2,1:T(8,128)(2,1)S(1)}, f32[3,1024,64]{1,2,0:T(8,128)}) fusion(f32[3,1024,64]{1,2,0:T(8,128)S(1)} %fusion.56, f32[3]{0:T(128)S(1)} %copy-done.112, f32[1024,3]{0,1:T(4,128)S(1)} %bitcast.442, f32[3,1024,1024]{1,2,0:T(8,128)} %copy-done, f32[3,1024]{1,0:T(4,128)S(1)} %get-tuple-element.280, f32[3,3,1024,64]{2,3,1,0:T(8,128)S(1)} %bitcast.369), kind=kOutput, calls=%fused_computation.95 | convolution fusion | flops 412876800 | bytes 14975488 | tf_op jit(solution)/shard_map/hqk,hkd->hqd/dot_general | solution.py:76
  225.7 12.9 %collective-permute-done.24 = bf16[128,1536]{1,0:T(8,128)(2,1)} collective-permute-done((bf16[128,1536]{1,0:T(8,128)(2,1)}, bf16[128,1536]{1,0:T(8,128)(2,1)}, u32[]{:S(2)}, u32[]{:S(2)}) %collective-permute-start.24) | collective-permute-done | bytes 393248 | tf_op jit(solution)/shard_map/ppermute | solution.py:121
  239.8 8.4 %collective-permute-done.23 = bf16[128,1536]{1,0:T(8,128)(2,1)S(1)} collective-permute-done((bf16[128,1536]{1,0:T(8,128)(2,1)}, bf16[128,1536]{1,0:T(8,128)(2,1)S(1)}, u32[]{:S(2)}, u32[]{:S(2)}) %collective-permute-start.23) | collective-permute-done | bytes 393248 | tf_op jit(solution)/shard_map/ppermute | solution.py:121
  248.2 4.8 collective-permute-done.25
  253.3 5.4 collective-permute-done.22
  258.7 7.2 %collective-permute-done.26 = bf16[128,1536]{1,0:T(8,128)(2,1)S(1)} collective-permute-done((bf16[128,1536]{1,0:T(8,128)(2,1)S(1)}, bf16[128,1536]{1,0:T(8,128)(2,1)S(1)}, u32[]{:S(2)}, u32[]{:S(2)}) %collective-permute-start.26) | collective-permute-done | bytes 393248 | tf_op jit(solution)/shard_map/ppermute | solution.py:125
  266.1 13.7 %collective-permute-done.27 = bf16[128,1536]{1,0:T(8,128)(2,1)S(1)} collective-permute-done((bf16[128,1536]{1,0:T(8,128)(2,1)S(1)}, bf16[128,1536]{1,0:T(8,128)(2,1)S(1)}, u32[]{:S(2)}, u32[]{:S(2)}) %collective-permute-start.27) | collective-permute-done | bytes 393248 | tf_op jit(solution)/shard_map/ppermute | solution.py:125
  281.9 13.8 %collective-permute-done.28 = bf16[128,1536]{1,0:T(8,128)(2,1)S(1)} collective-permute-done((bf16[128,1536]{1,0:T(8,128)(2,1)S(1)}, bf16[128,1536]{1,0:T(8,128)(2,1)S(1)}, u32[]{:S(2)}, u32[]{:S(2)}) %collective-permute-start.28) | collective-permute-done | bytes 393248 | tf_op jit(solution)/shard_map/ppermute | solution.py:135
  295.7 5.3 collective-permute-done.31
  305.4 5.3 collective-permute-done.32
  315.3 6.6 fusion.70
  321.9 7.2 %multiply_convert_fusion.4 = (bf16[512,1024]{1,0:T(8,128)(2,1)S(1)}, bf16[512,1024]{1,0:T(8,128)(2,1)S(1)}, bf16[512,1024]{1,0:T(8,128)(2,1)}) fusion(f32[512,2048]{1,0:T(8,128)} %fusion.70, bf16[1024,1536]{1,0:T(8,128)(2,1)} %all-gather.22.cloned.1.call-done, bf16[128,1536]{1,0:T(8,128)(2,1)} %collective-permute-done.33, ...), kind=kOutput, calls=%fused_computation.39 | convolution fusion | flops 1626341376 | bytes 12064768 | tf_op jit(solution)/shard_map/dot_general | solution.py:72
  329.1 5.6 convolution_convert_fusion
  338.0 6.9 %convolution_convert_fusion.7 = bf16[512,1536]{1,0:T(8,128)(2,1)S(1)} fusion(bf16[1536,2048]{1,0:T(8,128)(2,1)} %bitcast.376, bf16[512,1024]{1,0:T(8,128)(2,1)} %copy-done.129, bf16[512,1024]{1,0:T(8,128)(2,1)} %copy-done.128), kind=kOutput, calls=%fused_computation.31 | convolution fusion | flops 3226206208 | bytes 9961472 | tf_op jit(solution)/shard_map/dot_general | solution.py:72
  347.8 5.5 all_gather.46
  358.7 9.6 %collective-permute-done.35 = bf16[128,1536]{1,0:T(8,128)(2,1)S(1)} collective-permute-done((bf16[128,1536]{1,0:T(8,128)(2,1)S(1)}, bf16[128,1536]{1,0:T(8,128)(2,1)S(1)}, u32[]{:S(2)}, u32[]{:S(2)}) %collective-permute-start.35) | collective-permute-done | bytes 393248 | tf_op jit(solution)/shard_map/ppermute | solution.py:147
  372.0 7.3 %collective-permute-done.36 = bf16[128,1536]{1,0:T(8,128)(2,1)S(1)} collective-permute-done((bf16[128,1536]{1,0:T(8,128)(2,1)S(1)}, bf16[128,1536]{1,0:T(8,128)(2,1)S(1)}, u32[]{:S(2)}, u32[]{:S(2)}) %collective-permute-start.36) | collective-permute-done | bytes 393248 | tf_op jit(solution)/shard_map/ppermute | solution.py:147
  384.4 4.6 convolution_convert_fusion.4
  389.1 5.0 collective-permute-done.38
  399.2 6.9 %collective-permute-done.40 = bf16[128,1536]{1,0:T(8,128)(2,1)S(1)} collective-permute-done((bf16[128,1536]{1,0:T(8,128)(2,1)}, bf16[128,1536]{1,0:T(8,128)(2,1)S(1)}, u32[]{:S(2)}, u32[]{:S(2)}) %collective-permute-start.40) | collective-permute-done | bytes 393248 | tf_op jit(solution)/shard_map/ppermute | solution.py:112
  409.9 5.7 collective-permute-done.42
  418.3 7.1 %collective-permute-done.43 = bf16[128,1536]{1,0:T(8,128)(2,1)S(1)} collective-permute-done((bf16[128,1536]{1,0:T(8,128)(2,1)S(1)}, bf16[128,1536]{1,0:T(8,128)(2,1)S(1)}, u32[]{:S(2)}, u32[]{:S(2)}) %collective-permute-start.43) | collective-permute-done | bytes 393248 | tf_op jit(solution)/shard_map/ppermute | solution.py:109
  454.4 7.6 %fusion.31 = bf16[1,3,1024,64]{2,3,1,0:T(8,128)(2,1)} fusion(f32[3,1024,1024]{1,2,0:T(8,128)} %copy-done, f32[3,1024]{1,0:T(4,128)S(1)} %copy-done.78, f32[3,1024,64]{1,2,0:T(8,128)S(1)} %copy-done.28), kind=kOutput, calls=%fused_computation.60 | convolution fusion | flops 412483584 | bytes 13774848 | tf_op jit(solution)/shard_map/hqk,hqd->hkd/dot_general | solution.py:76
  465.7 6.4 collective-permute-done.55
  473.4 6.5 collective-permute-done.56
  490.8 4.7 copy.324
  506.1 14.1 %collective-permute-done.45 = bf16[128,1536]{1,0:T(8,128)(2,1)S(1)} collective-permute-done((bf16[128,1536]{1,0:T(8,128)(2,1)S(1)}, bf16[128,1536]{1,0:T(8,128)(2,1)S(1)}, u32[]{:S(2)}, u32[]{:S(2)}) %collective-permute-start.45) | collective-permute-done | bytes 393248 | tf_op jit(solution)/shard_map/ppermute | solution.py:147
  527.8 4.6 convolution_convert_fusion.2
  538.1 6.4 collective-permute-done.50
  563.2 5.3 collective-permute-done.52
  573.5 6.0 collective-permute-done.53
  581.5 5.3 all-gather.3
  590.5 5.5 convolution_convert_fusion.5
  600.1 5.2 all-gather.2
  608.6 6.3 all-to-all-start.4
  647.2 5.2 all-gather.4
  (633 shorter events, 298.5 us)
Async XLA Ops:
  7.2 59.6 %all-gather.12.cloned.1.call-start = ((), (), s32[]{:S(2)}) async-start(), calls=%async_computation.12 | async-start | bytes 1392640 | tf_op jit(solution)/shard_map/all_gather | solution.py:98
  9.1 126.1 %all-gather.14.cloned.1.call-start = ((), (), s32[]{:S(2)}) async-start(), calls=%async_computation.13 | async-start | bytes 1966080 | tf_op jit(solution)/shard_map/all_gather | solution.py:98
  9.8 150.1 %all-gather.16.cloned.1.call-start = ((), (), s32[]{:S(2)}) async-start(), calls=%async_computation.14 | async-start | bytes 2457600 | tf_op jit(solution)/shard_map/all_gather | solution.py:98
  33.3 131.4 %all-gather.18.cloned.1.call-start = ((), (), s32[]{:S(2)}) async-start(), calls=%async_computation.15 | async-start | bytes 4669440 | tf_op jit(solution)/shard_map/all_gather | solution.py:98
  36.2 39.7 %collective-permute-start.6 = (bf16[128,1664]{1,0:T(8,128)(2,1)}, bf16[128,1664]{1,0:T(8,128)(2,1)}, u32[]{:S(2)}, u32[]{:S(2)}) collective-permute-start(bf16[128,1664]{1,0:T(8,128)(2,1)} %concatenate.87), channel_id=1, source_target_pairs={{0,1},{1,0},{2,3},{3,2},{4,5},{5,4},{6,7},{7,6},{8,9},{9,8},{10,11... | collective-permute-start | bytes 1277960 | tf_op jit(solution)/shard_map/ppermute | solution.py:109
  48.8 23.2 %collective-permute-start.7 = (bf16[128,1664]{1,0:T(8,128)(2,1)}, bf16[128,1664]{1,0:T(8,128)(2,1)}, u32[]{:S(2)}, u32[]{:S(2)}) collective-permute-start(bf16[128,1664]{1,0:T(8,128)(2,1)} %concatenate.87), channel_id=1, source_target_pairs={{0,2},{2,4},{4,6},{6,0},{1,3},{3,5},{5,7},{7,1},{8,10},{10,12},{12... | collective-permute-start | bytes 1277960 | tf_op jit(solution)/shard_map/ppermute | solution.py:112
  49.7 15.2 %all-to-all-start = ((bf16[8,32,512]{2,1,0:T(8,128)(2,1)}), bf16[8,32,512]{2,1,0:T(8,128)(2,1)}, u32[]{:S(2)}, u32[]{:S(2)}) async-start(bf16[8,32,512]{2,1,0:T(8,128)(2,1)} %reshape.641), calls=%async_computation | async-start | bytes 524288 | tf_op jit(solution)/shard_map/all_to_all | solution.py:95
  72.0 34.6 %collective-permute-start.8 = (bf16[128,1664]{1,0:T(8,128)(2,1)}, bf16[128,1664]{1,0:T(8,128)(2,1)}, u32[]{:S(2)}, u32[]{:S(2)}) collective-permute-start(bf16[128,1664]{1,0:T(8,128)(2,1)} %collective-permute-done.7), channel_id=1, source_target_pairs={{0,1},{1,0},{2,3},{3,2},{4,5},{5,4},{6,7},{7,6},{8,9},{9,8},{10,11... | collective-permute-start | bytes 1277960 | tf_op jit(solution)/shard_map/ppermute | solution.py:109
  73.1 28.7 %collective-permute-start.9 = (bf16[128,1664]{1,0:T(8,128)(2,1)}, bf16[128,1664]{1,0:T(8,128)(2,1)}, u32[]{:S(2)}, u32[]{:S(2)}) collective-permute-start(bf16[128,1664]{1,0:T(8,128)(2,1)} %collective-permute-done.7), channel_id=1, source_target_pairs={{0,2},{2,4},{4,6},{6,0},{1,3},{3,5},{5,7},{7,1},{8,10},{10,12},{12... | collective-permute-start | bytes 1277960 | tf_op jit(solution)/shard_map/ppermute | solution.py:112
  96.2 30.7 %all-to-all-start.2 = ((bf16[4,48,2048]{2,1,0:T(8,128)(2,1)}), bf16[4,48,2048]{2,1,0:T(8,128)(2,1)}, u32[]{:S(2)}, u32[]{:S(2)}) async-start(bf16[4,48,2048]{2,1,0:T(8,128)(2,1)} %pad_maximum_fusion.7), calls=%async_computation.2 | async-start | bytes 1572864 | tf_op jit(solution)/shard_map/all_to_all | solution.py:294
  100.8 210.3 %all-gather.20.cloned.1.call-start = ((), (), s32[]{:S(2)}) async-start(), calls=%async_computation.16 | async-start | bytes 7077888 | tf_op jit(solution)/shard_map/all_gather | solution.py:98
  101.9 23.7 %collective-permute-start.10 = (bf16[128,1664]{1,0:T(8,128)(2,1)}, bf16[128,1664]{1,0:T(8,128)(2,1)S(1)}, u32[]{:S(2)}, u32[]{:S(2)}) collective-permute-start(bf16[128,1664]{1,0:T(8,128)(2,1)} %collective-permute-done.9), channel_id=1, source_target_pairs={{0,1},{1,0},{2,3},{3,2},{4,5},{5,4},{6,7},{7,6},{8,9},{9,8},{10,11... | collective-permute-start | bytes 1277960 | tf_op jit(solution)/shard_map/ppermute | solution.py:109
  103.7 19.6 %collective-permute-start.11 = (bf16[128,1664]{1,0:T(8,128)(2,1)}, bf16[128,1664]{1,0:T(8,128)(2,1)}, u32[]{:S(2)}, u32[]{:S(2)}) collective-permute-start(bf16[128,1664]{1,0:T(8,128)(2,1)} %collective-permute-done.9), channel_id=1, source_target_pairs={{0,2},{2,4},{4,6},{6,0},{1,3},{3,5},{5,7},{7,1},{8,10},{10,12},{12... | collective-permute-start | bytes 1277960 | tf_op jit(solution)/shard_map/ppermute | solution.py:112
  126.9 195.0 %all-gather.22.cloned.1.call-start = ((), (), s32[]{:S(2)}) async-start(), calls=%async_computation.17 | async-start | bytes 3538944 | tf_op jit(solution)/shard_map/all_gather | solution.py:98
  173.0 12.9 %collective-permute-start.16 = (bf16[256,384]{0,1:T(8,128)(2,1)S(1)}, bf16[256,384]{0,1:T(8,128)(2,1)S(1)}, u32[]{:S(2)}, u32[]{:S(2)}) collective-permute-start(bf16[256,384]{0,1:T(8,128)(2,1)S(1)} %get-tuple-element.238), channel_id=1, source_target_pairs={{0,1},{1,0},{2,3},{3,2},{4,5},{5,4},{6,7},{7,6},{8,9},{9,8},{10,11... | collective-permute-start | bytes 589832 | tf_op jit(solution)/shard_map/ppermute | solution.py:121
  223.5 15.1 %collective-permute-start.24 = (bf16[128,1536]{1,0:T(8,128)(2,1)}, bf16[128,1536]{1,0:T(8,128)(2,1)}, u32[]{:S(2)}, u32[]{:S(2)}) collective-permute-start(bf16[128,1536]{1,0:T(8,128)(2,1)} %get-tuple-element.225), channel_id=1, source_target_pairs={{0,1},{1,0},{2,3},{3,2},{4,5},{5,4},{6,7},{7,6},{8,9},{9,8},{10,11... | collective-permute-start | bytes 1179656 | tf_op jit(solution)/shard_map/ppermute | solution.py:121
  223.5 272.1 %reduce-scatter.10.cloned.1.call-start = ((), (), s32[]{:S(2)}) async-start(), calls=%async_computation.18 | async-start | bytes 7077888 | tf_op jit(solution)/shard_map/reduce_scatter | solution.py:101
  223.6 24.6 %collective-permute-start.23 = (bf16[128,1536]{1,0:T(8,128)(2,1)}, bf16[128,1536]{1,0:T(8,128)(2,1)S(1)}, u32[]{:S(2)}, u32[]{:S(2)}) collective-permute-start(bf16[128,1536]{1,0:T(8,128)(2,1)} %get-tuple-element.226), channel_id=1, source_target_pairs={{0,1},{1,0},{2,3},{3,2},{4,5},{5,4},{6,7},{7,6},{8,9},{9,8},{10,11... | collective-permute-start | bytes 1179656 | tf_op jit(solution)/shard_map/ppermute | solution.py:121
  239.6 13.4 %collective-permute-start.25 = (bf16[128,1536]{1,0:T(8,128)(2,1)S(1)}, bf16[128,1536]{1,0:T(8,128)(2,1)S(1)}, u32[]{:S(2)}, u32[]{:S(2)}) collective-permute-start(bf16[128,1536]{1,0:T(8,128)(2,1)S(1)} %add_convert_fusion.10), channel_id=1, source_target_pairs={{0,2},{2,4},{4,6},{6,0},{1,3},{3,5},{5,7},{7,1},{8,10},{10,12},{12... | collective-permute-start | bytes 1179656 | tf_op jit(solution)/shard_map/ppermute | solution.py:125
  239.7 18.9 %collective-permute-start.22 = (bf16[128,1536]{1,0:T(8,128)(2,1)}, bf16[128,1536]{1,0:T(8,128)(2,1)S(1)}, u32[]{:S(2)}, u32[]{:S(2)}) collective-permute-start(bf16[128,1536]{1,0:T(8,128)(2,1)} %get-tuple-element.227), channel_id=1, source_target_pairs={{0,1},{1,0},{2,3},{3,2},{4,5},{5,4},{6,7},{7,6},{8,9},{9,8},{10,11... | collective-permute-start | bytes 1179656 | tf_op jit(solution)/shard_map/ppermute | solution.py:121
  253.1 12.7 %collective-permute-start.26 = (bf16[128,1536]{1,0:T(8,128)(2,1)S(1)}, bf16[128,1536]{1,0:T(8,128)(2,1)S(1)}, u32[]{:S(2)}, u32[]{:S(2)}) collective-permute-start(bf16[128,1536]{1,0:T(8,128)(2,1)S(1)} %add_convert_fusion.9), channel_id=1, source_target_pairs={{0,2},{2,4},{4,6},{6,0},{1,3},{3,5},{5,7},{7,1},{8,10},{10,12},{12... | collective-permute-start | bytes 1179656 | tf_op jit(solution)/shard_map/ppermute | solution.py:125
  253.2 12.8 %collective-permute-start.21 = (bf16[128,1536]{1,0:T(8,128)(2,1)}, bf16[128,1536]{1,0:T(8,128)(2,1)S(1)}, u32[]{:S(2)}, u32[]{:S(2)}) collective-permute-start(bf16[128,1536]{1,0:T(8,128)(2,1)} %get-tuple-element.224), channel_id=1, source_target_pairs={{0,1},{1,0},{2,3},{3,2},{4,5},{5,4},{6,7},{7,6},{8,9},{9,8},{10,11... | collective-permute-start | bytes 1179656 | tf_op jit(solution)/shard_map/ppermute | solution.py:121
  266.0 13.8 %collective-permute-start.27 = (bf16[128,1536]{1,0:T(8,128)(2,1)S(1)}, bf16[128,1536]{1,0:T(8,128)(2,1)S(1)}, u32[]{:S(2)}, u32[]{:S(2)}) collective-permute-start(bf16[128,1536]{1,0:T(8,128)(2,1)S(1)} %add_convert_fusion.8), channel_id=1, source_target_pairs={{0,2},{2,4},{4,6},{6,0},{1,3},{3,5},{5,7},{7,1},{8,10},{10,12},{12... | collective-permute-start | bytes 1179656 | tf_op jit(solution)/shard_map/ppermute | solution.py:125
  281.8 13.9 %collective-permute-start.28 = (bf16[128,1536]{1,0:T(8,128)(2,1)S(1)}, bf16[128,1536]{1,0:T(8,128)(2,1)S(1)}, u32[]{:S(2)}, u32[]{:S(2)}) collective-permute-start(bf16[128,1536]{1,0:T(8,128)(2,1)S(1)} %multiply_convert_fusion.8), channel_id=1, source_target_pairs={{0,2},{2,4},{4,6},{6,0},{1,3},{3,5},{5,7},{7,1},{8,10},{10,12},{12... | collective-permute-start | bytes 1179656 | tf_op jit(solution)/shard_map/ppermute | solution.py:135
  281.8 19.2 %collective-permute-start.31 = (bf16[128,1536]{1,0:T(8,128)(2,1)S(1)}, bf16[128,1536]{1,0:T(8,128)(2,1)S(1)}, u32[]{:S(2)}, u32[]{:S(2)}) collective-permute-start(bf16[128,1536]{1,0:T(8,128)(2,1)S(1)} %bitcast.417), channel_id=1, source_target_pairs={{0,2},{2,4},{4,6},{6,0},{1,3},{3,5},{5,7},{7,1},{8,10},{10,12},{12... | collective-permute-start | bytes 1179656 | tf_op jit(solution)/shard_map/ppermute | solution.py:135
  337.9 186.2 %reduce-scatter.12.cloned.1.call-start = ((), (), s32[]{:S(2)}) async-start(), calls=%async_computation.19 | async-start | bytes 3538944 | tf_op jit(solution)/shard_map/reduce_scatter | solution.py:101
  383.7 13.4 %collective-permute-start.37 = (bf16[128,1536]{1,0:T(8,128)(2,1)}, bf16[128,1536]{1,0:T(8,128)(2,1)}, u32[]{:S(2)}, u32[]{:S(2)}) collective-permute-start(bf16[128,1536]{1,0:T(8,128)(2,1)} %get-tuple-element.208), channel_id=1, source_target_pairs={{0,1},{1,0},{2,3},{3,2},{4,5},{5,4},{6,7},{7,6},{8,9},{9,8},{10,11... | collective-permute-start | bytes 1179656 | tf_op jit(solution)/shard_map/ppermute | solution.py:109
  389.1 181.8 %reduce-scatter.14.cloned.1.call-start = ((), (), s32[]{:S(2)}) async-start(), calls=%async_computation.20 | async-start | bytes 737280 | tf_op jit(solution)/shard_map/reduce_scatter | solution.py:101
  394.1 15.8 %collective-permute-start.39 = (bf16[128,1536]{1,0:T(8,128)(2,1)}, bf16[128,1536]{1,0:T(8,128)(2,1)S(1)}, u32[]{:S(2)}, u32[]{:S(2)}) collective-permute-start(bf16[128,1536]{1,0:T(8,128)(2,1)} %collective-permute-done.38), channel_id=1, source_target_pairs={{0,1},{1,0},{2,3},{3,2},{4,5},{5,4},{6,7},{7,6},{8,9},{9,8},{10,11... | collective-permute-start | bytes 1179656 | tf_op jit(solution)/shard_map/ppermute | solution.py:109
  406.0 12.2 %collective-permute-start.41 = (bf16[128,1536]{1,0:T(8,128)(2,1)S(1)}, bf16[128,1536]{1,0:T(8,128)(2,1)S(1)}, u32[]{:S(2)}, u32[]{:S(2)}) collective-permute-start(bf16[128,1536]{1,0:T(8,128)(2,1)S(1)} %collective-permute-done.40), channel_id=1, source_target_pairs={{0,1},{1,0},{2,3},{3,2},{4,5},{5,4},{6,7},{7,6},{8,9},{9,8},{10,11... | collective-permute-start | bytes 1179656 | tf_op jit(solution)/shard_map/ppermute | solution.py:109
  432.6 32.1 %collective-permute-start.60 = (bf16[256,384]{0,1:T(8,128)(2,1)}, bf16[256,384]{0,1:T(8,128)(2,1)}, u32[]{:S(2)}, u32[]{:S(2)}) collective-permute-start(bf16[256,384]{0,1:T(8,128)(2,1)} %bitcast.76), channel_id=1, source_target_pairs={{0,1},{1,0},{2,3},{3,2},{4,5},{5,4},{6,7},{7,6},{8,9},{9,8},{10,11... | collective-permute-start | bytes 589832 | tf_op jit(solution)/shard_map/ppermute | solution.py:109
  432.6 30.1 %collective-permute-start.54 = (bf16[256,384]{0,1:T(8,128)(2,1)}, bf16[256,384]{0,1:T(8,128)(2,1)}, u32[]{:S(2)}, u32[]{:S(2)}) collective-permute-start(bf16[256,384]{0,1:T(8,128)(2,1)} %bitcast.76), channel_id=1, source_target_pairs={{0,2},{2,4},{4,6},{6,0},{1,3},{3,5},{5,7},{7,1},{8,10},{10,12},{12... | collective-permute-start | bytes 589832 | tf_op jit(solution)/shard_map/ppermute | solution.py:112
  438.0 62.1 %collective-permute-start.44 = (bf16[128,1536]{1,0:T(8,128)(2,1)}, bf16[128,1536]{1,0:T(8,128)(2,1)}, u32[]{:S(2)}, u32[]{:S(2)}) collective-permute-start(bf16[128,1536]{1,0:T(8,128)(2,1)} %slice.316), channel_id=1, source_target_pairs={{0,2},{2,4},{4,6},{6,0},{1,3},{3,5},{5,7},{7,1},{8,10},{10,12},{12... | collective-permute-start | bytes 1179656 | tf_op jit(solution)/shard_map/ppermute | solution.py:147
  462.0 126.1 %reduce-scatter.18.cloned.1.call-start = ((), (), s32[]{:S(2)}) async-start(), calls=%async_computation.22 | async-start | bytes 3932160
  495.6 32.1 %all-to-all-start.3 = ((bf16[4,48,2048]{2,1,0:T(8,128)(2,1)}), bf16[4,48,2048]{2,1,0:T(8,128)(2,1)}, u32[]{:S(2)}, u32[]{:S(2)}) async-start(bf16[4,48,2048]{2,1,0:T(8,128)(2,1)} %bitcast.425), calls=%async_computation.4 | async-start | bytes 1572864 | tf_op jit(solution)/shard_map/all_to_all | solution.py:379
  500.0 139.9 %reduce-scatter.16.cloned.1.call-start = ((), (), s32[]{:S(2)}) async-start(), calls=%async_computation.21 | async-start | bytes 2457600 | tf_op jit(solution)/shard_map/reduce_scatter | solution.py:101
  501.3 18.9 %collective-permute-start.45 = (bf16[128,1536]{1,0:T(8,128)(2,1)S(1)}, bf16[128,1536]{1,0:T(8,128)(2,1)S(1)}, u32[]{:S(2)}, u32[]{:S(2)}) collective-permute-start(bf16[128,1536]{1,0:T(8,128)(2,1)S(1)} %add_convert_fusion.5), channel_id=1, source_target_pairs={{0,2},{2,4},{4,6},{6,0},{1,3},{3,5},{5,7},{7,1},{8,10},{10,12},{12... | collective-permute-start | bytes 1179656 | tf_op jit(solution)/shard_map/ppermute | solution.py:147
  522.1 12.7 %collective-permute-start.46 = (bf16[128,1536]{1,0:T(8,128)(2,1)}, bf16[128,1536]{1,0:T(8,128)(2,1)}, u32[]{:S(2)}, u32[]{:S(2)}) collective-permute-start(bf16[128,1536]{1,0:T(8,128)(2,1)} %add_convert_fusion.4), channel_id=1, source_target_pairs={{0,2},{2,4},{4,6},{6,0},{1,3},{3,5},{5,7},{7,1},{8,10},{10,12},{12... | collective-permute-start | bytes 1179656 | tf_op jit(solution)/shard_map/ppermute | solution.py:147
  533.3 11.3 %collective-permute-start.50 = (bf16[128,1536]{1,0:T(8,128)(2,1)S(1)}, bf16[128,1536]{1,0:T(8,128)(2,1)S(1)}, u32[]{:S(2)}, u32[]{:S(2)}) collective-permute-start(bf16[128,1536]{1,0:T(8,128)(2,1)S(1)} %get-tuple-element.221), channel_id=1, source_target_pairs={{0,1},{1,0},{2,3},{3,2},{4,5},{5,4},{6,7},{7,6},{8,9},{9,8},{10,11... | collective-permute-start | bytes 1179656 | tf_op jit(solution)/shard_map/ppermute | solution.py:121
  537.1 16.5 %collective-permute-start.49 = (bf16[128,1536]{1,0:T(8,128)(2,1)S(1)}, bf16[128,1536]{1,0:T(8,128)(2,1)S(1)}, u32[]{:S(2)}, u32[]{:S(2)}) collective-permute-start(bf16[128,1536]{1,0:T(8,128)(2,1)S(1)} %get-tuple-element.222), channel_id=1, source_target_pairs={{0,1},{1,0},{2,3},{3,2},{4,5},{5,4},{6,7},{7,6},{8,9},{9,8},{10,11... | collective-permute-start | bytes 1179656 | tf_op jit(solution)/shard_map/ppermute | solution.py:121
  544.7 11.9 %collective-permute-start.51 = (bf16[128,1536]{1,0:T(8,128)(2,1)S(1)}, bf16[128,1536]{1,0:T(8,128)(2,1)S(1)}, u32[]{:S(2)}, u32[]{:S(2)}) collective-permute-start(bf16[128,1536]{1,0:T(8,128)(2,1)S(1)} %add_convert_fusion.2), channel_id=1, source_target_pairs={{0,2},{2,4},{4,6},{6,0},{1,3},{3,5},{5,7},{7,1},{8,10},{10,12},{12... | collective-permute-start | bytes 1179656 | tf_op jit(solution)/shard_map/ppermute | solution.py:125
  556.8 11.7 %collective-permute-start.52 = (bf16[128,1536]{1,0:T(8,128)(2,1)S(1)}, bf16[128,1536]{1,0:T(8,128)(2,1)S(1)}, u32[]{:S(2)}, u32[]{:S(2)}) collective-permute-start(bf16[128,1536]{1,0:T(8,128)(2,1)S(1)} %add_convert_fusion.1), channel_id=1, source_target_pairs={{0,2},{2,4},{4,6},{6,0},{1,3},{3,5},{5,7},{7,1},{8,10},{10,12},{12... | collective-permute-start | bytes 1179656 | tf_op jit(solution)/shard_map/ppermute | solution.py:125
  559.8 13.0 %collective-permute-start.66 = (f32[37,128]{1,0:T(8,128)}, f32[37,128]{1,0:T(8,128)}, u32[]{:S(2)}, u32[]{:S(2)}) collective-permute-start(f32[37,128]{1,0:T(8,128)} %fusion.202), channel_id=1, source_target_pairs={{0,4},{2,6},{4,0},{6,2},{1,5},{3,7},{5,1},{7,3},{8,12},{10,14},{12... | collective-permute-start | bytes 56840 | tf_op jit(solution)/shard_map/ppermute | solution.py:157
  559.8 13.7 %collective-permute-start.47 = (bf16[128,1536]{1,0:T(8,128)(2,1)}, bf16[128,1536]{1,0:T(8,128)(2,1)}, u32[]{:S(2)}, u32[]{:S(2)}) collective-permute-start(bf16[128,1536]{1,0:T(8,128)(2,1)} %get-tuple-element.220), channel_id=1, source_target_pairs={{0,1},{1,0},{2,3},{3,2},{4,5},{5,4},{6,7},{7,6},{8,9},{9,8},{10,11... | collective-permute-start | bytes 1179656 | tf_op jit(solution)/shard_map/ppermute | solution.py:121
  570.8 16.6 %collective-permute-start.67 = (bf16[48,1536]{1,0:T(8,128)(2,1)}, bf16[48,1536]{1,0:T(8,128)(2,1)S(1)}, u32[]{:S(2)}, u32[]{:S(2)}) collective-permute-start(bf16[48,1536]{1,0:T(8,128)(2,1)} %reduce-scatter.14.cloned.1.call-done), channel_id=1, source_target_pairs={{0,0},{8,1},{16,2},{24,3},{1,4},{9,5},{17,6},{25,7},{2,8},{10,9},{... | collective-permute-start | bytes 442376 | tf_op jit(solution)/shard_map/ppermute | solution.py:392
  608.6 12.7 %all-to-all-start.4 = ((f32[8,1,128]{2,1,0:T(1,128)}), f32[8,1,128]{2,1,0:T(1,128)S(1)}, u32[]{:S(2)}, u32[]{:S(2)}) async-start(f32[8,1,128]{2,1,0:T(1,128)} %reshape.727), calls=%async_computation.6 | async-start | bytes 8192 | tf_op jit(solution)/shard_map/all_to_all | solution.py:95
  626.7 13.2 %all-to-all-start.5 = ((bf16[8,32,512]{2,1,0:T(8,128)(2,1)}), bf16[8,32,512]{2,1,0:T(8,128)(2,1)S(1)}, u32[]{:S(2)}, u32[]{:S(2)}) async-start(bf16[8,32,512]{2,1,0:T(8,128)(2,1)} %bitcast.118), calls=%async_computation.7 | async-start | bytes 524288 | tf_op jit(solution)/shard_map/all_to_all | solution.py:95
  639.9 17.1 %all-to-all-start.6 = ((bf16[8,48,576]{2,1,0:T(8,128)(2,1)}), bf16[8,48,576]{2,1,0:T(8,128)(2,1)S(1)}, u32[]{:S(2)}, u32[]{:S(2)}) async-start(bf16[8,48,576]{2,1,0:T(8,128)(2,1)} %bitcast.429), calls=%async_computation.8 | async-start | bytes 983040 | tf_op jit(solution)/shard_map/all_to_all | solution.py:95
  (170 other events, 2166.3 us)
Sparse Core Ops, SparseCore 0:
  10.2 19.7 all-gather.11
  31.6 19.6 all-gather.13
  52.8 22.1 all-gather.15
  76.5 31.8 all-gather.17
  127.1 54.9 all-gather.19
  223.6 39.7 all-gather.21
  338.0 68.2 reduce-scatter.9
  410.1 50.5 reduce-scatter.11
  463.8 22.0 reduce-scatter.13
  495.7 36.2 reduce-scatter.17
  600.2 31.6 reduce-scatter.15

commit v4 on v3

--- a/solution.py
+++ b/solution.py
@@ -305,7 +305,6 @@
                 jnp.full((128,), timesteps[0].astype(f32)),
             ]
         )
-        clip_facts = lax.all_gather(packed.reshape(-1, 128), "clip", axis=0).reshape(clips, -1)
 
         normed_all, _ = rms_norm(tokens_all.astype(f32), epsilon)
         gain1 = norm1_gain * (1.0 + scale_attn)
@@ -331,7 +330,8 @@
 
         text_part = jnp.stack([dot(cap_part, key_s), dot(cap_part, value_s)]).astype(bf16)
         text_part = text_part.reshape(2, cap_len, inner, own).transpose(2, 1, 0, 3)
-        text_own = ring_scatter(slot_blocks(text_part.reshape(inner, cap_len, 2 * own)))
+        text_own = swap_team(text_part.reshape(inner, cap_len, 2 * own))
+        text_own = jnp.sum(text_own.astype(f32), 0)
         text_own = text_own.reshape(cap_len, 2, heads, head_dim).transpose(1, 2, 0, 3)
         text_keys_n, inverse_t = rms_norm(text_own[0], head_eps)
         keys_text_b = text_keys_n.astype(bf16)
@@ -414,7 +414,7 @@
                 text_grads, lax.axis_index("outer") * inner * cap_rows, inner * cap_rows
             )
         grad_rows = text_grads.shape[0]
-        text_grads = in_order(ring_gather(text_grads)).reshape(inner, grad_rows, 2, own)
+        text_grads = small_gather(text_grads).reshape(inner, grad_rows, 2, own)
         text_grads = text_grads.transpose(2, 1, 0, 3).reshape(2, grad_rows, width)
         text_grads = jnp.concatenate([text_grads[0], text_grads[1]], -1)
         sum_text = scatter_spread(dot_tn(cap_own, text_grads).astype(bf16)).astype(f32)
@@ -451,9 +451,11 @@
         if outer > 1:
             early = lax.psum(early, "outer")
             late = lax.psum(late, "outer")
-        early = lax.all_gather(early, "clip", axis=0).reshape(clips, -1)
-        late = lax.all_gather(late, "clip", axis=0).reshape(clips, -1)
-        sums = jnp.concatenate([late, early], -1)
+        clip_sums = jnp.concatenate([late, early], 0)
+        clip_facts = jnp.concatenate([clip_sums, packed.reshape(-1, 128)], 0)
+        clip_facts = lax.all_gather(clip_facts, "clip", axis=0).reshape(clips, -1)
+        sums = clip_facts[:, : clip_sums.size]
+        clip_facts = clip_facts[:, clip_sums.size :]
         mods = clip_facts[:, :mod_width].reshape(clips, 4, width)
         at = mod_width
         cond_all = clip_facts[:, at : at + cond_width]

time: 674 us -> 657 us (0.975)
  blocking collectives: 42.2 us -> 12.4 us
  waiting for transfers between devices: 256 us -> 276 us
    all_to_all x4 -> x7, waiting for transfers between devices: 12.5 us -> 51.5 us  [swap_team(): return lax.all_to_all(x, team, split_axis=0, concat_axis=0, tiled=True)]
    ppermute x9 -> x6, waiting for transfers between devices: 53 us -> 23.1 us  [ring_scatter(): passed = lax.ppermute(total.astype(bf16), 'ring', forward)]
    ppermute x12 -> x8, waiting for transfers between devices: 45.3 us -> 15.7 us  [ring_scatter(): total = total + lax.ppermute(block_of(k, 1), 'pair', crossed).astype(f32)]
    all_to_all x1 -> x0, blocking collectives: 21 us -> none  [swap_team(): return lax.all_to_all(x, team, split_axis=0, concat_axis=0, tiled=True)]
    all_to_all x4 -> x7, starting transfers between devices: 19.4 us -> 38.9 us  [swap_team(): return lax.all_to_all(x, team, split_axis=0, concat_axis=0, tiled=True)]
    ppermute x12, waiting for transfers between devices: 12.6 us -> 27 us  [small_sum(): x = x + lax.ppermute(x, axis, [(i, i ^ hop) for i in range(size)])]
    ppermute x12 -> x8, starting transfers between devices: 25.5 us -> 11.4 us  [ring_gather(): other = lax.ppermute(other, 'pair', crossed)]
    ppermute x6, waiting for transfers between devices: 34.1 us -> 46.9 us  [line_scatter(): passed = lax.ppermute(total.astype(bf16), 'ring', forward)]
  transfers between devices with their start and end apart: 85 -> 74, of which waited for: 50 -> 45; matrix products, arithmetic and copies ran while one was open for 33% -> 32% of each run, Pallas kernels for 0% -> 0%
where the time goes in v4:
time: 657 us; the launch traced here: 646 us
  waiting for transfers between devices  276 us (42%)
  starting transfers between devices  103 us (16%)
  matrix products  97.2 us (15%)
  local copies, waits for them, and re-layouts  71.2 us (11%)
  other arithmetic  68.6 us (10%)
  between operations  17.8 us (3%)
  blocking collectives  12.4 us (2%)
    all_to_all x7, waiting for transfers between devices, swap_team(): return lax.all_to_all(x, team, split_axis=0, concat_axis=0, tiled=True)  51.5 us
    ppermute x6, waiting for transfers between devices, ring_gather(): now = lax.ppermute(now, 'ring', forward)  49.4 us
    ppermute x6, waiting for transfers between devices, line_scatter(): passed = lax.ppermute(total.astype(bf16), 'ring', forward)  46.9 us
    all_to_all x7, starting transfers between devices, swap_team(): return lax.all_to_all(x, team, split_axis=0, concat_axis=0, tiled=True)  38.9 us
    unnamed x295, local copies, waits for them, and re-layouts  34.9 us
    ppermute x8, waiting for transfers between devices, ring_gather(): other = lax.ppermute(other, 'pair', crossed)  31.9 us
    dot_general x11, matrix products, ein(): return jnp.einsum(spec, a, b, preferred_element_type=f32)  31.2 us
    ppermute x6, waiting for transfers between devices, line_gather(): parts.append(lax.ppermute(parts[-1], 'ring', forward))  29.5 us
  transfers between devices with their start and end apart: 74, of which 45 were waited for; matrix products, arithmetic and copies ran while one was open for 32% of the time, Pallas kernels for 0%

profile of v4, /device:TPU:0, one launch (start us, length us, event | category | flops | bytes accessed | tf_op | source)
XLA Modules:
  0.0 646.3 jit_solution(2261800773748133440)
XLA Ops:
  15.7 16.0 %all-to-all-start.1 = ((bf16[8,48,576]{2,1,0:T(8,128)(2,1)}), bf16[8,48,576]{2,1,0:T(8,128)(2,1)S(1)}, u32[]{:S(2)}, u32[]{:S(2)}) async-start(bf16[8,48,576]{2,1,0:T(8,128)(2,1)} %reshape.639), calls=%async_computation.1 | async-start | bytes 983040 | tf_op jit(solution)/shard_map/all_to_all | solution.py:95
  32.7 12.8 %all-to-all-done.1 = bf16[8,48,576]{2,1,0:T(8,128)(2,1)S(1)} async-done(((bf16[8,48,576]{2,1,0:T(8,128)(2,1)}), bf16[8,48,576]{2,1,0:T(8,128)(2,1)S(1)}, u32[]{:S(2)}, u32[]{:S(2)}) %all-to-all-start.1) | async-done | bytes 442400 | tf_op jit(solution)/shard_map/all_to_all | solution.py:95
  50.6 7.6 %all-to-all-done = bf16[8,32,512]{2,1,0:T(8,128)(2,1)S(1)} async-done(((bf16[8,32,512]{2,1,0:T(8,128)(2,1)}), bf16[8,32,512]{2,1,0:T(8,128)(2,1)S(1)}, u32[]{:S(2)}, u32[]{:S(2)}) %all-to-all-start) | async-done | bytes 262176 | tf_op jit(solution)/shard_map/all_to_all | solution.py:95
  75.4 4.2 all-to-all-start.3
  87.1 15.4 %collective-permute-done.7 = bf16[128,1664]{1,0:T(8,128)(2,1)} collective-permute-done((bf16[128,1664]{1,0:T(8,128)(2,1)}, bf16[128,1664]{1,0:T(8,128)(2,1)}, u32[]{:S(2)}, u32[]{:S(2)}) %collective-permute-start.7) | collective-permute-done | bytes 426016 | tf_op jit(solution)/shard_map/ppermute | solution.py:112
  105.7 7.1 %collective-permute-done.9 = bf16[128,1664]{1,0:T(8,128)(2,1)} collective-permute-done((bf16[128,1664]{1,0:T(8,128)(2,1)}, bf16[128,1664]{1,0:T(8,128)(2,1)}, u32[]{:S(2)}, u32[]{:S(2)}) %collective-permute-start.9) | collective-permute-done | bytes 426016 | tf_op jit(solution)/shard_map/ppermute | solution.py:112
  117.1 8.0 %collective-permute-done.11 = bf16[128,1664]{1,0:T(8,128)(2,1)} collective-permute-done((bf16[128,1664]{1,0:T(8,128)(2,1)}, bf16[128,1664]{1,0:T(8,128)(2,1)}, u32[]{:S(2)}, u32[]{:S(2)}) %collective-permute-start.11) | collective-permute-done | bytes 426016 | tf_op jit(solution)/shard_map/ppermute | solution.py:112
  127.4 12.7 %collective-permute-done.12 = bf16[128,1664]{1,0:T(8,128)(2,1)} collective-permute-done((bf16[128,1664]{1,0:T(8,128)(2,1)}, bf16[128,1664]{1,0:T(8,128)(2,1)}, u32[]{:S(2)}, u32[]{:S(2)}) %collective-permute-start.12) | collective-permute-done | bytes 426016 | tf_op jit(solution)/shard_map/ppermute | solution.py:109
  167.2 4.3 all-to-all-start.2
  171.8 4.5 fusion.150
  186.7 7.8 %all-to-all-done.2 = bf16[8,256,384]{1,2,0:T(8,128)(2,1)} async-done(((bf16[8,256,384]{1,2,0:T(8,128)(2,1)}), bf16[8,256,384]{1,2,0:T(8,128)(2,1)}, u32[]{:S(2)}, u32[]{:S(2)}) %all-to-all-start.2) | async-done | bytes 1572896 | tf_op jit(solution)/shard_map/all_to_all | solution.py:95
  201.6 8.0 %fusion.52 = (bf16[1024,3,64]{0,2,1:T(8,128)(2,1)S(1)}, f32[3,1024,64]{1,2,0:T(8,128)}) fusion(f32[3,1024,64]{1,2,0:T(8,128)S(1)} %fusion.56, f32[3]{0:T(128)S(1)} %copy-done.116, f32[1024,3]{0,1:T(4,128)S(1)} %bitcast.368, f32[3,1024,1024]{1,2,0:T(8,128)} %copy-done, f32[3,1024]{1,0:T(4,128)S(1)} %get-tuple-element.270, f32[3,3,1024,64]{2,3,1,0:T(8,128)S(1)} %bitcast.299), kind=kOutput, calls=%fused_computation.96 | convolution fusion | flops 412876800 | bytes 14975488 | tf_op jit(solution)/shard_map/hqk,hkd->hqd/dot_general | solution.py:76
  214.0 6.5 %collective-permute-done.17 = bf16[128,1536]{1,0:T(8,128)(2,1)} collective-permute-done((bf16[128,1536]{1,0:T(8,128)(2,1)}, bf16[128,1536]{1,0:T(8,128)(2,1)}, u32[]{:S(2)}, u32[]{:S(2)}) %collective-permute-start.17) | collective-permute-done | bytes 393248 | tf_op jit(solution)/shard_map/ppermute | solution.py:121
  224.3 7.4 %collective-permute-done.16 = bf16[128,1536]{1,0:T(8,128)(2,1)S(1)} collective-permute-done((bf16[128,1536]{1,0:T(8,128)(2,1)}, bf16[128,1536]{1,0:T(8,128)(2,1)S(1)}, u32[]{:S(2)}, u32[]{:S(2)}) %collective-permute-start.16) | collective-permute-done | bytes 393248 | tf_op jit(solution)/shard_map/ppermute | solution.py:121
  237.2 6.4 collective-permute-done.19
  245.7 12.2 %collective-permute-done.20 = bf16[128,1536]{1,0:T(8,128)(2,1)S(1)} collective-permute-done((bf16[128,1536]{1,0:T(8,128)(2,1)S(1)}, bf16[128,1536]{1,0:T(8,128)(2,1)S(1)}, u32[]{:S(2)}, u32[]{:S(2)}) %collective-permute-start.20) | collective-permute-done | bytes 393248 | tf_op jit(solution)/shard_map/ppermute | solution.py:125
  262.2 11.5 %collective-permute-done.21 = bf16[128,1536]{1,0:T(8,128)(2,1)S(1)} collective-permute-done((bf16[128,1536]{1,0:T(8,128)(2,1)S(1)}, bf16[128,1536]{1,0:T(8,128)(2,1)S(1)}, u32[]{:S(2)}, u32[]{:S(2)}) %collective-permute-start.21) | collective-permute-done | bytes 393248 | tf_op jit(solution)/shard_map/ppermute | solution.py:135
  273.6 7.4 %collective-permute-done.24 = bf16[128,1536]{1,0:T(8,128)(2,1)S(1)} collective-permute-done((bf16[128,1536]{1,0:T(8,128)(2,1)S(1)}, bf16[128,1536]{1,0:T(8,128)(2,1)S(1)}, u32[]{:S(2)}, u32[]{:S(2)}) %collective-permute-start.24) | collective-permute-done | bytes 393248 | tf_op jit(solution)/shard_map/ppermute | solution.py:135
  281.1 4.3 collective-permute-done.22
  285.4 5.4 collective-permute-done.25
  295.3 6.7 %fusion.63 = f32[512,2048]{1,0:T(8,128)} fusion(bf16[1536,2048]{1,0:T(8,128)(2,1)S(1)} %bitcast.305, bf16[128,1536]{1,0:T(8,128)(2,1)} %collective-permute-done.23, bf16[128,1536]{1,0:T(8,128)(2,1)} %collective-permute-done.22, bf16[128,1536]{1,0:T(8,128)(2,1)S(1)} %copy-done.127, bf16[128,1536]{1,0:T(8,128)(2,1)S(1)} %copy-done.78), kind=kOutput, calls=%fused_computation.157 | convolution fusion | flops 3227516928 | bytes 12058624 | tf_op jit(solution)/shard_map/dot_general | solution.py:64
  302.0 7.2 %multiply_convert_fusion.4 = (bf16[512,1024]{1,0:T(8,128)(2,1)S(1)}, bf16[512,1024]{1,0:T(8,128)(2,1)S(1)}, bf16[512,1024]{1,0:T(8,128)(2,1)}) fusion(f32[512,2048]{1,0:T(8,128)} %fusion.63, bf16[1024,1536]{1,0:T(8,128)(2,1)} %all-gather.20.cloned.1.call-done, bf16[128,1536]{1,0:T(8,128)(2,1)} %collective-permute-done.26, ...), kind=kOutput, calls=%fused_computation.40 | convolution fusion | flops 1626341376 | bytes 12064768 | tf_op jit(solution)/shard_map/dot_general | solution.py:72
  309.2 5.6 convolution_convert_fusion
  318.1 6.9 %convolution_convert_fusion.7 = bf16[512,1536]{1,0:T(8,128)(2,1)S(1)} fusion(bf16[1536,2048]{1,0:T(8,128)(2,1)} %bitcast.306, bf16[512,1024]{1,0:T(8,128)(2,1)} %copy-done.131, bf16[512,1024]{1,0:T(8,128)(2,1)} %copy-done.130), kind=kOutput, calls=%fused_computation.32 | convolution fusion | flops 3226206208 | bytes 9961472 | tf_op jit(solution)/shard_map/dot_general | solution.py:72
  325.1 9.6 %collective-permute-done.27 = bf16[128,1536]{1,0:T(8,128)(2,1)S(1)} collective-permute-done((bf16[128,1536]{1,0:T(8,128)(2,1)S(1)}, bf16[128,1536]{1,0:T(8,128)(2,1)S(1)}, u32[]{:S(2)}, u32[]{:S(2)}) %collective-permute-start.27) | collective-permute-done | bytes 393248 | tf_op jit(solution)/shard_map/ppermute | solution.py:147
  334.9 10.6 %collective-permute-done.28 = bf16[128,1536]{1,0:T(8,128)(2,1)S(1)} collective-permute-done((bf16[128,1536]{1,0:T(8,128)(2,1)S(1)}, bf16[128,1536]{1,0:T(8,128)(2,1)S(1)}, u32[]{:S(2)}, u32[]{:S(2)}) %collective-permute-start.28) | collective-permute-done | bytes 393248 | tf_op jit(solution)/shard_map/ppermute | solution.py:147
  348.4 9.3 %collective-permute-done.29 = bf16[128,1536]{1,0:T(8,128)(2,1)} collective-permute-done((bf16[128,1536]{1,0:T(8,128)(2,1)}, bf16[128,1536]{1,0:T(8,128)(2,1)}, u32[]{:S(2)}, u32[]{:S(2)}) %collective-permute-start.29) | collective-permute-done | bytes 393248 | tf_op jit(solution)/shard_map/ppermute | solution.py:147
  364.6 5.9 collective-permute-start.30
  370.5 4.6 convolution_convert_fusion.4
  375.2 5.2 collective-permute-done.31
  385.9 4.3 collective-permute-done.33
  392.3 9.5 %collective-permute-done.35 = bf16[128,1536]{1,0:T(8,128)(2,1)S(1)} collective-permute-done((bf16[128,1536]{1,0:T(8,128)(2,1)S(1)}, bf16[128,1536]{1,0:T(8,128)(2,1)S(1)}, u32[]{:S(2)}, u32[]{:S(2)}) %collective-permute-start.35) | collective-permute-done | bytes 393248 | tf_op jit(solution)/shard_map/ppermute | solution.py:112
  401.8 8.7 %collective-permute-done.34 = bf16[128,1536]{1,0:T(8,128)(2,1)S(1)} collective-permute-done((bf16[128,1536]{1,0:T(8,128)(2,1)S(1)}, bf16[128,1536]{1,0:T(8,128)(2,1)S(1)}, u32[]{:S(2)}, u32[]{:S(2)}) %collective-permute-start.34) | collective-permute-done | bytes 393248 | tf_op jit(solution)/shard_map/ppermute | solution.py:109
  410.6 7.0 %collective-permute-done.36 = bf16[128,1536]{1,0:T(8,128)(2,1)S(1)} collective-permute-done((bf16[128,1536]{1,0:T(8,128)(2,1)S(1)}, bf16[128,1536]{1,0:T(8,128)(2,1)S(1)}, u32[]{:S(2)}, u32[]{:S(2)}) %collective-permute-start.36) | collective-permute-done | bytes 393248 | tf_op jit(solution)/shard_map/ppermute | solution.py:109
  425.6 4.3 all-to-all-start.5
  429.9 4.1 convolution_convert_fusion.6
  440.0 6.6 %multiply_convert_fusion = bf16[3,1024,1024]{1,2,0:T(8,128)(2,1)S(1)} fusion(f32[3,1024,1024]{1,2,0:T(8,128)} %copy-done, f32[3,1024]{1,0:T(4,128)S(1)} %copy-done.108, f32[3,1024]{1,0:T(4,128)S(1)} %copy-done.85, f32[3,3,1024,64]{2,3,1,0:T(8,128)} %bitcast.300, f32[3,1024,64]{1,2,0:T(8,128)S(1)} %copy-done.31), kind=kOutput, calls=%fused_computation.1 | convolution fusion | flops 418578432 | bytes 20078592 | tf_op jit(solution)/shard_map/hqd,hkd->hqk/dot_general | solution.py:76
  451.3 4.3 fusion.22
  461.7 6.1 all-to-all-done.5
  471.9 4.7 copy.325
  476.7 4.3 all-to-all-start.4
  486.0 15.6 %collective-permute-done.38 = bf16[128,1536]{1,0:T(8,128)(2,1)S(1)} collective-permute-done((bf16[128,1536]{1,0:T(8,128)(2,1)S(1)}, bf16[128,1536]{1,0:T(8,128)(2,1)S(1)}, u32[]{:S(2)}, u32[]{:S(2)}) %collective-permute-start.38) | collective-permute-done | bytes 393248 | tf_op jit(solution)/shard_map/ppermute | solution.py:147
  523.6 10.1 %collective-permute-done.51 = f32[37,128]{1,0:T(8,128)} collective-permute-done((f32[37,128]{1,0:T(8,128)}, f32[37,128]{1,0:T(8,128)}, u32[]{:S(2)}, u32[]{:S(2)}) %collective-permute-start.51) | collective-permute-done | bytes 18976 | tf_op jit(solution)/shard_map/ppermute | solution.py:157
  581.3 6.9 %all-gather.1 = f32[4,110,128]{2,1,0:T(8,128)S(1)} all-gather(f32[1,110,128]{2,1,0:T(8,128)S(1)} %maximum_bitcast_fusion), channel_id=2, replica_groups=mesh['clip'=4,'outer'=1,'ring'=4,'pair'=2] {'clip'}, dimensions={0}, use_global_device_ids=true | all-gather | bytes 281600 | tf_op jit(solution)/shard_map/all_gather | solution.py:456
  592.2 3.8 all-to-all-start.6
  596.0 6.4 all-to-all-done.6
  611.8 8.0 %all-to-all-done.7 = bf16[8,32,512]{2,1,0:T(8,128)(2,1)S(1)} async-done(((bf16[8,32,512]{2,1,0:T(8,128)(2,1)}), bf16[8,32,512]{2,1,0:T(8,128)(2,1)S(1)}, u32[]{:S(2)}, u32[]{:S(2)}) %all-to-all-start.7) | async-done | bytes 262176 | tf_op jit(solution)/shard_map/all_to_all | solution.py:95
  625.1 5.5 all-gather.2
  (595 shorter events, 267.6 us)
Async XLA Ops:
  7.2 51.8 %all-gather.10.cloned.1.call-start = ((), (), s32[]{:S(2)}) async-start(), calls=%async_computation.14 | async-start | bytes 1392640 | tf_op jit(solution)/shard_map/all_gather | solution.py:98
  9.0 134.3 %all-gather.12.cloned.1.call-start = ((), (), s32[]{:S(2)}) async-start(), calls=%async_computation.15 | async-start | bytes 1966080 | tf_op jit(solution)/shard_map/all_gather | solution.py:98
  9.8 152.7 %all-gather.16.cloned.1.call-start = ((), (), s32[]{:S(2)}) async-start(), calls=%async_computation.17 | async-start | bytes 4669440 | tf_op jit(solution)/shard_map/all_gather | solution.py:98
  15.7 29.7 %all-to-all-start.1 = ((bf16[8,48,576]{2,1,0:T(8,128)(2,1)}), bf16[8,48,576]{2,1,0:T(8,128)(2,1)S(1)}, u32[]{:S(2)}, u32[]{:S(2)}) async-start(bf16[8,48,576]{2,1,0:T(8,128)(2,1)} %reshape.639), calls=%async_computation.1 | async-start | bytes 983040 | tf_op jit(solution)/shard_map/all_to_all | solution.py:95
  45.4 12.7 %all-to-all-start = ((bf16[8,32,512]{2,1,0:T(8,128)(2,1)}), bf16[8,32,512]{2,1,0:T(8,128)(2,1)S(1)}, u32[]{:S(2)}, u32[]{:S(2)}) async-start(bf16[8,32,512]{2,1,0:T(8,128)(2,1)} %reshape.633), calls=%async_computation | async-start | bytes 524288 | tf_op jit(solution)/shard_map/all_to_all | solution.py:95
  49.1 122.7 %all-gather.14.cloned.1.call-start = ((), (), s32[]{:S(2)}) async-start(), calls=%async_computation.16 | async-start | bytes 2457600 | tf_op jit(solution)/shard_map/all_gather | solution.py:98
  75.4 39.6 %all-to-all-start.3 = ((bf16[4,48,2048]{2,1,0:T(8,128)(2,1)}), bf16[4,48,2048]{2,1,0:T(8,128)(2,1)}, u32[]{:S(2)}, u32[]{:S(2)}) async-start(bf16[4,48,2048]{2,1,0:T(8,128)(2,1)} %pad_maximum_fusion.7), calls=%async_computation.3 | async-start | bytes 1572864 | tf_op jit(solution)/shard_map/all_to_all | solution.py:294
  79.6 211.2 %all-gather.18.cloned.1.call-start = ((), (), s32[]{:S(2)}) async-start(), calls=%async_computation.18 | async-start | bytes 7077888 | tf_op jit(solution)/shard_map/all_gather | solution.py:98
  80.5 23.1 %collective-permute-start.6 = (bf16[128,1664]{1,0:T(8,128)(2,1)}, bf16[128,1664]{1,0:T(8,128)(2,1)}, u32[]{:S(2)}, u32[]{:S(2)}) collective-permute-start(bf16[128,1664]{1,0:T(8,128)(2,1)} %concatenate.87), channel_id=1, source_target_pairs={{0,1},{1,0},{2,3},{3,2},{4,5},{5,4},{6,7},{7,6},{8,9},{9,8},{10,11... | collective-permute-start | bytes 1277960 | tf_op jit(solution)/shard_map/ppermute | solution.py:109
  81.9 20.5 %collective-permute-start.7 = (bf16[128,1664]{1,0:T(8,128)(2,1)}, bf16[128,1664]{1,0:T(8,128)(2,1)}, u32[]{:S(2)}, u32[]{:S(2)}) collective-permute-start(bf16[128,1664]{1,0:T(8,128)(2,1)} %concatenate.87), channel_id=1, source_target_pairs={{0,2},{2,4},{4,6},{6,0},{1,3},{3,5},{5,7},{7,1},{8,10},{10,12},{12... | collective-permute-start | bytes 1277960 | tf_op jit(solution)/shard_map/ppermute | solution.py:112
  102.4 12.6 %collective-permute-start.8 = (bf16[128,1664]{1,0:T(8,128)(2,1)}, bf16[128,1664]{1,0:T(8,128)(2,1)}, u32[]{:S(2)}, u32[]{:S(2)}) collective-permute-start(bf16[128,1664]{1,0:T(8,128)(2,1)} %collective-permute-done.7), channel_id=1, source_target_pairs={{0,1},{1,0},{2,3},{3,2},{4,5},{5,4},{6,7},{7,6},{8,9},{9,8},{10,11... | collective-permute-start | bytes 1277960 | tf_op jit(solution)/shard_map/ppermute | solution.py:109
  112.8 12.3 %collective-permute-start.10 = (bf16[128,1664]{1,0:T(8,128)(2,1)}, bf16[128,1664]{1,0:T(8,128)(2,1)}, u32[]{:S(2)}, u32[]{:S(2)}) collective-permute-start(bf16[128,1664]{1,0:T(8,128)(2,1)} %collective-permute-done.9), channel_id=1, source_target_pairs={{0,1},{1,0},{2,3},{3,2},{4,5},{5,4},{6,7},{7,6},{8,9},{9,8},{10,11... | collective-permute-start | bytes 1277960 | tf_op jit(solution)/shard_map/ppermute | solution.py:109
  125.1 15.1 %collective-permute-start.12 = (bf16[128,1664]{1,0:T(8,128)(2,1)}, bf16[128,1664]{1,0:T(8,128)(2,1)}, u32[]{:S(2)}, u32[]{:S(2)}) collective-permute-start(bf16[128,1664]{1,0:T(8,128)(2,1)} %collective-permute-done.11), channel_id=1, source_target_pairs={{0,1},{1,0},{2,3},{3,2},{4,5},{5,4},{6,7},{7,6},{8,9},{9,8},{10,11... | collective-permute-start | bytes 1277960 | tf_op jit(solution)/shard_map/ppermute | solution.py:109
  167.2 27.4 %all-to-all-start.2 = ((bf16[8,256,384]{1,2,0:T(8,128)(2,1)}), bf16[8,256,384]{1,2,0:T(8,128)(2,1)}, u32[]{:S(2)}, u32[]{:S(2)}) async-start(bf16[8,256,384]{1,2,0:T(8,128)(2,1)} %bitcast.33), calls=%async_computation.2 | async-start | bytes 3145728 | tf_op jit(solution)/shard_map/all_to_all | solution.py:95
  171.5 130.5 %all-gather.20.cloned.1.call-start = ((), (), s32[]{:S(2)}) async-start(), calls=%async_computation.19 | async-start | bytes 3538944 | tf_op jit(solution)/shard_map/all_gather | solution.py:98
  213.2 263.4 %reduce-scatter.10.cloned.1.call-start = ((), (), s32[]{:S(2)}) async-start(), calls=%async_computation.20 | async-start | bytes 7077888 | tf_op jit(solution)/shard_map/reduce_scatter | solution.py:101
  213.3 18.4 %collective-permute-start.16 = (bf16[128,1536]{1,0:T(8,128)(2,1)}, bf16[128,1536]{1,0:T(8,128)(2,1)S(1)}, u32[]{:S(2)}, u32[]{:S(2)}) collective-permute-start(bf16[128,1536]{1,0:T(8,128)(2,1)} %get-tuple-element.226), channel_id=1, source_target_pairs={{0,1},{1,0},{2,3},{3,2},{4,5},{5,4},{6,7},{7,6},{8,9},{9,8},{10,11... | collective-permute-start | bytes 1179656 | tf_op jit(solution)/shard_map/ppermute | solution.py:121
  221.6 11.3 %collective-permute-start.18 = (bf16[128,1536]{1,0:T(8,128)(2,1)S(1)}, bf16[128,1536]{1,0:T(8,128)(2,1)S(1)}, u32[]{:S(2)}, u32[]{:S(2)}) collective-permute-start(bf16[128,1536]{1,0:T(8,128)(2,1)S(1)} %add_convert_fusion.10), channel_id=1, source_target_pairs={{0,2},{2,4},{4,6},{6,0},{1,3},{3,5},{5,7},{7,1},{8,10},{10,12},{12... | collective-permute-start | bytes 1179656 | tf_op jit(solution)/shard_map/ppermute | solution.py:125
  222.5 14.7 %collective-permute-start.15 = (bf16[128,1536]{1,0:T(8,128)(2,1)}, bf16[128,1536]{1,0:T(8,128)(2,1)S(1)}, u32[]{:S(2)}, u32[]{:S(2)}) collective-permute-start(bf16[128,1536]{1,0:T(8,128)(2,1)} %get-tuple-element.227), channel_id=1, source_target_pairs={{0,1},{1,0},{2,3},{3,2},{4,5},{5,4},{6,7},{7,6},{8,9},{9,8},{10,11... | collective-permute-start | bytes 1179656 | tf_op jit(solution)/shard_map/ppermute | solution.py:121
  233.0 10.5 %collective-permute-start.19 = (bf16[128,1536]{1,0:T(8,128)(2,1)S(1)}, bf16[128,1536]{1,0:T(8,128)(2,1)S(1)}, u32[]{:S(2)}, u32[]{:S(2)}) collective-permute-start(bf16[128,1536]{1,0:T(8,128)(2,1)S(1)} %add_convert_fusion.9), channel_id=1, source_target_pairs={{0,2},{2,4},{4,6},{6,0},{1,3},{3,5},{5,7},{7,1},{8,10},{10,12},{12... | collective-permute-start | bytes 1179656 | tf_op jit(solution)/shard_map/ppermute | solution.py:125
  233.9 11.7 %collective-permute-start.14 = (bf16[128,1536]{1,0:T(8,128)(2,1)}, bf16[128,1536]{1,0:T(8,128)(2,1)S(1)}, u32[]{:S(2)}, u32[]{:S(2)}) collective-permute-start(bf16[128,1536]{1,0:T(8,128)(2,1)} %get-tuple-element.224), channel_id=1, source_target_pairs={{0,1},{1,0},{2,3},{3,2},{4,5},{5,4},{6,7},{7,6},{8,9},{9,8},{10,11... | collective-permute-start | bytes 1179656 | tf_op jit(solution)/shard_map/ppermute | solution.py:121
  243.7 14.2 %collective-permute-start.20 = (bf16[128,1536]{1,0:T(8,128)(2,1)S(1)}, bf16[128,1536]{1,0:T(8,128)(2,1)S(1)}, u32[]{:S(2)}, u32[]{:S(2)}) collective-permute-start(bf16[128,1536]{1,0:T(8,128)(2,1)S(1)} %add_convert_fusion.8), channel_id=1, source_target_pairs={{0,2},{2,4},{4,6},{6,0},{1,3},{3,5},{5,7},{7,1},{8,10},{10,12},{12... | collective-permute-start | bytes 1179656 | tf_op jit(solution)/shard_map/ppermute | solution.py:125
  259.8 13.8 %collective-permute-start.21 = (bf16[128,1536]{1,0:T(8,128)(2,1)S(1)}, bf16[128,1536]{1,0:T(8,128)(2,1)S(1)}, u32[]{:S(2)}, u32[]{:S(2)}) collective-permute-start(bf16[128,1536]{1,0:T(8,128)(2,1)S(1)} %multiply_convert_fusion.8), channel_id=1, source_target_pairs={{0,2},{2,4},{4,6},{6,0},{1,3},{3,5},{5,7},{7,1},{8,10},{10,12},{12... | collective-permute-start | bytes 1179656 | tf_op jit(solution)/shard_map/ppermute | solution.py:135
  259.9 21.2 %collective-permute-start.24 = (bf16[128,1536]{1,0:T(8,128)(2,1)S(1)}, bf16[128,1536]{1,0:T(8,128)(2,1)S(1)}, u32[]{:S(2)}, u32[]{:S(2)}) collective-permute-start(bf16[128,1536]{1,0:T(8,128)(2,1)S(1)} %bitcast.344), channel_id=1, source_target_pairs={{0,2},{2,4},{4,6},{6,0},{1,3},{3,5},{5,7},{7,1},{8,10},{10,12},{12... | collective-permute-start | bytes 1179656 | tf_op jit(solution)/shard_map/ppermute | solution.py:135
  273.6 11.7 %collective-permute-start.22 = (bf16[128,1536]{1,0:T(8,128)(2,1)S(1)}, bf16[128,1536]{1,0:T(8,128)(2,1)}, u32[]{:S(2)}, u32[]{:S(2)}) collective-permute-start(bf16[128,1536]{1,0:T(8,128)(2,1)S(1)} %collective-permute-done.21), channel_id=1, source_target_pairs={{0,2},{2,4},{4,6},{6,0},{1,3},{3,5},{5,7},{7,1},{8,10},{10,12},{12... | collective-permute-start | bytes 1179656 | tf_op jit(solution)/shard_map/ppermute | solution.py:135
  290.7 11.2 %collective-permute-start.26 = (bf16[128,1536]{1,0:T(8,128)(2,1)}, bf16[128,1536]{1,0:T(8,128)(2,1)}, u32[]{:S(2)}, u32[]{:S(2)}) collective-permute-start(bf16[128,1536]{1,0:T(8,128)(2,1)} %collective-permute-done.25), channel_id=1, source_target_pairs={{0,2},{2,4},{4,6},{6,0},{1,3},{3,5},{5,7},{7,1},{8,10},{10,12},{12... | collective-permute-start | bytes 1179656 | tf_op jit(solution)/shard_map/ppermute | solution.py:135
  318.1 185.5 %reduce-scatter.12.cloned.1.call-start = ((), (), s32[]{:S(2)}) async-start(), calls=%async_computation.21 | async-start | bytes 3538944 | tf_op jit(solution)/shard_map/reduce_scatter | solution.py:101
  334.8 10.7 %collective-permute-start.28 = (bf16[128,1536]{1,0:T(8,128)(2,1)S(1)}, bf16[128,1536]{1,0:T(8,128)(2,1)S(1)}, u32[]{:S(2)}, u32[]{:S(2)}) collective-permute-start(bf16[128,1536]{1,0:T(8,128)(2,1)S(1)} %add_convert_fusion.7), channel_id=1, source_target_pairs={{0,2},{2,4},{4,6},{6,0},{1,3},{3,5},{5,7},{7,1},{8,10},{10,12},{12... | collective-permute-start | bytes 1179656 | tf_op jit(solution)/shard_map/ppermute | solution.py:147
  346.3 11.4 %collective-permute-start.29 = (bf16[128,1536]{1,0:T(8,128)(2,1)}, bf16[128,1536]{1,0:T(8,128)(2,1)}, u32[]{:S(2)}, u32[]{:S(2)}) collective-permute-start(bf16[128,1536]{1,0:T(8,128)(2,1)} %add_convert_fusion.6), channel_id=1, source_target_pairs={{0,2},{2,4},{4,6},{6,0},{1,3},{3,5},{5,7},{7,1},{8,10},{10,12},{12... | collective-permute-start | bytes 1179656 | tf_op jit(solution)/shard_map/ppermute | solution.py:147
  364.6 19.2 %collective-permute-start.30 = (bf16[128,1536]{1,0:T(8,128)(2,1)}, bf16[128,1536]{1,0:T(8,128)(2,1)}, u32[]{:S(2)}, u32[]{:S(2)}) collective-permute-start(bf16[128,1536]{1,0:T(8,128)(2,1)} %get-tuple-element.208), channel_id=1, source_target_pairs={{0,1},{1,0},{2,3},{3,2},{4,5},{5,4},{6,7},{7,6},{8,9},{9,8},{10,11... | collective-permute-start | bytes 1179656 | tf_op jit(solution)/shard_map/ppermute | solution.py:109
  380.4 11.8 %collective-permute-start.32 = (bf16[128,1536]{1,0:T(8,128)(2,1)}, bf16[128,1536]{1,0:T(8,128)(2,1)S(1)}, u32[]{:S(2)}, u32[]{:S(2)}) collective-permute-start(bf16[128,1536]{1,0:T(8,128)(2,1)} %collective-permute-done.31), channel_id=1, source_target_pairs={{0,1},{1,0},{2,3},{3,2},{4,5},{5,4},{6,7},{7,6},{8,9},{9,8},{10,11... | collective-permute-start | bytes 1179656 | tf_op jit(solution)/shard_map/ppermute | solution.py:109
  390.2 20.3 %collective-permute-start.34 = (bf16[128,1536]{1,0:T(8,128)(2,1)S(1)}, bf16[128,1536]{1,0:T(8,128)(2,1)S(1)}, u32[]{:S(2)}, u32[]{:S(2)}) collective-permute-start(bf16[128,1536]{1,0:T(8,128)(2,1)S(1)} %collective-permute-done.33), channel_id=1, source_target_pairs={{0,1},{1,0},{2,3},{3,2},{4,5},{5,4},{6,7},{7,6},{8,9},{9,8},{10,11... | collective-permute-start | bytes 1179656 | tf_op jit(solution)/shard_map/ppermute | solution.py:109
  401.8 15.8 %collective-permute-start.36 = (bf16[128,1536]{1,0:T(8,128)(2,1)S(1)}, bf16[128,1536]{1,0:T(8,128)(2,1)S(1)}, u32[]{:S(2)}, u32[]{:S(2)}) collective-permute-start(bf16[128,1536]{1,0:T(8,128)(2,1)S(1)} %collective-permute-done.35), channel_id=1, source_target_pairs={{0,1},{1,0},{2,3},{3,2},{4,5},{5,4},{6,7},{7,6},{8,9},{9,8},{10,11... | collective-permute-start | bytes 1179656 | tf_op jit(solution)/shard_map/ppermute | solution.py:109
  425.6 42.2 %all-to-all-start.5 = ((bf16[8,256,384]{1,2,0:T(8,128)(2,1)}), bf16[8,256,384]{1,2,0:T(8,128)(2,1)}, u32[]{:S(2)}, u32[]{:S(2)}) async-start(bf16[8,256,384]{1,2,0:T(8,128)(2,1)} %broadcast_in_dim.83), calls=%async_computation.7 | async-start | bytes 3145728 | tf_op jit(solution)/shard_map/all_to_all | solution.py:95
  429.9 91.9 %reduce-scatter.14.cloned.1.call-start = ((), (), s32[]{:S(2)}) async-start(), calls=%async_computation.22 | async-start | bytes 737280 | tf_op jit(solution)/shard_map/reduce_scatter | solution.py:101
  434.9 46.2 %collective-permute-start.37 = (bf16[128,1536]{1,0:T(8,128)(2,1)}, bf16[128,1536]{1,0:T(8,128)(2,1)}, u32[]{:S(2)}, u32[]{:S(2)}) collective-permute-start(bf16[128,1536]{1,0:T(8,128)(2,1)} %slice.324), channel_id=1, source_target_pairs={{0,2},{2,4},{4,6},{6,0},{1,3},{3,5},{5,7},{7,1},{8,10},{10,12},{12... | collective-permute-start | bytes 1179656 | tf_op jit(solution)/shard_map/ppermute | solution.py:147
  439.6 119.0 %reduce-scatter.18.cloned.1.call-start = ((), (), s32[]{:S(2)}) async-start(), calls=%async_computation.24 | async-start | bytes 3932160
  476.7 29.0 %all-to-all-start.4 = ((bf16[4,48,2048]{2,1,0:T(8,128)(2,1)}), bf16[4,48,2048]{2,1,0:T(8,128)(2,1)}, u32[]{:S(2)}, u32[]{:S(2)}) async-start(bf16[4,48,2048]{2,1,0:T(8,128)(2,1)} %bitcast.359), calls=%async_computation.5 | async-start | bytes 1572864 | tf_op jit(solution)/shard_map/all_to_all | solution.py:379
  481.0 138.8 %reduce-scatter.16.cloned.1.call-start = ((), (), s32[]{:S(2)}) async-start(), calls=%async_computation.23 | async-start | bytes 2457600 | tf_op jit(solution)/shard_map/reduce_scatter | solution.py:101
  482.3 19.3 %collective-permute-start.38 = (bf16[128,1536]{1,0:T(8,128)(2,1)S(1)}, bf16[128,1536]{1,0:T(8,128)(2,1)S(1)}, u32[]{:S(2)}, u32[]{:S(2)}) collective-permute-start(bf16[128,1536]{1,0:T(8,128)(2,1)S(1)} %add_convert_fusion.5), channel_id=1, source_target_pairs={{0,2},{2,4},{4,6},{6,0},{1,3},{3,5},{5,7},{7,1},{8,10},{10,12},{12... | collective-permute-start | bytes 1179656 | tf_op jit(solution)/shard_map/ppermute | solution.py:147
  516.8 17.8 %collective-permute-start.42 = (bf16[128,1536]{1,0:T(8,128)(2,1)}, bf16[128,1536]{1,0:T(8,128)(2,1)S(1)}, u32[]{:S(2)}, u32[]{:S(2)}) collective-permute-start(bf16[128,1536]{1,0:T(8,128)(2,1)} %get-tuple-element.222), channel_id=1, source_target_pairs={{0,1},{1,0},{2,3},{3,2},{4,5},{5,4},{6,7},{7,6},{8,9},{9,8},{10,11... | collective-permute-start | bytes 1179656 | tf_op jit(solution)/shard_map/ppermute | solution.py:121
  518.6 16.0 %collective-permute-start.44 = (bf16[128,1536]{1,0:T(8,128)(2,1)}, bf16[128,1536]{1,0:T(8,128)(2,1)}, u32[]{:S(2)}, u32[]{:S(2)}) collective-permute-start(bf16[128,1536]{1,0:T(8,128)(2,1)} %add_convert_fusion.2), channel_id=1, source_target_pairs={{0,2},{2,4},{4,6},{6,0},{1,3},{3,5},{5,7},{7,1},{8,10},{10,12},{12... | collective-permute-start | bytes 1179656 | tf_op jit(solution)/shard_map/ppermute | solution.py:125
  521.1 12.5 %collective-permute-start.51 = (f32[37,128]{1,0:T(8,128)}, f32[37,128]{1,0:T(8,128)}, u32[]{:S(2)}, u32[]{:S(2)}) collective-permute-start(f32[37,128]{1,0:T(8,128)} %fusion.189), channel_id=1, source_target_pairs={{0,2},{2,0},{4,6},{6,4},{1,3},{3,1},{5,7},{7,5},{8,10},{10,8},{12,... | collective-permute-start | bytes 56840 | tf_op jit(solution)/shard_map/ppermute | solution.py:157
  521.8 18.3 %collective-permute-start.53 = (bf16[48,1536]{1,0:T(8,128)(2,1)}, bf16[48,1536]{1,0:T(8,128)(2,1)S(1)}, u32[]{:S(2)}, u32[]{:S(2)}) collective-permute-start(bf16[48,1536]{1,0:T(8,128)(2,1)} %reduce-scatter.14.cloned.1.call-done), channel_id=1, source_target_pairs={{0,0},{8,1},{16,2},{24,3},{1,4},{9,5},{17,6},{25,7},{2,8},{10,9},{... | collective-permute-start | bytes 442376 | tf_op jit(solution)/shard_map/ppermute | solution.py:392
  542.2 17.9 %collective-permute-start.40 = (bf16[128,1536]{1,0:T(8,128)(2,1)}, bf16[128,1536]{1,0:T(8,128)(2,1)S(1)}, u32[]{:S(2)}, u32[]{:S(2)}) collective-permute-start(bf16[128,1536]{1,0:T(8,128)(2,1)} %get-tuple-element.220), channel_id=1, source_target_pairs={{0,1},{1,0},{2,3},{3,2},{4,5},{5,4},{6,7},{7,6},{8,9},{9,8},{10,11... | collective-permute-start | bytes 1179656 | tf_op jit(solution)/shard_map/ppermute | solution.py:121
  547.6 12.6 %collective-permute-start.46 = (bf16[128,1536]{1,0:T(8,128)(2,1)}, bf16[128,1536]{1,0:T(8,128)(2,1)S(1)}, u32[]{:S(2)}, u32[]{:S(2)}) collective-permute-start(bf16[128,1536]{1,0:T(8,128)(2,1)} %add_convert_fusion), channel_id=1, source_target_pairs={{0,2},{2,4},{4,6},{6,0},{1,3},{3,5},{5,7},{7,1},{8,10},{10,12},{12... | collective-permute-start | bytes 1179656 | tf_op jit(solution)/shard_map/ppermute | solution.py:125
  608.0 11.8 %all-to-all-start.7 = ((bf16[8,32,512]{2,1,0:T(8,128)(2,1)}), bf16[8,32,512]{2,1,0:T(8,128)(2,1)S(1)}, u32[]{:S(2)}, u32[]{:S(2)}) async-start(bf16[8,32,512]{2,1,0:T(8,128)(2,1)} %bitcast.95), calls=%async_computation.9 | async-start | bytes 524288 | tf_op jit(solution)/shard_map/all_to_all | solution.py:95
  619.8 16.8 %all-to-all-start.8 = ((bf16[8,48,576]{2,1,0:T(8,128)(2,1)}), bf16[8,48,576]{2,1,0:T(8,128)(2,1)S(1)}, u32[]{:S(2)}, u32[]{:S(2)}) async-start(bf16[8,48,576]{2,1,0:T(8,128)(2,1)} %bitcast.362), calls=%async_computation.10 | async-start | bytes 983040 | tf_op jit(solution)/shard_map/all_to_all | solution.py:95
  (161 other events, 1798.4 us)
Sparse Core Ops, SparseCore 0:
  10.2 19.7 all-gather.9
  31.6 19.6 all-gather.11
  52.8 31.9 all-gather.15
  86.8 21.7 all-gather.13
  115.1 60.1 all-gather.17
  213.3 39.5 all-gather.19
  318.2 92.5 reduce-scatter.9
  414.6 54.4 reduce-scatter.11
  472.2 22.0 reduce-scatter.13
  496.6 37.9 reduce-scatter.17
  558.7 32.9 reduce-scatter.15

commit v5 on v4

--- a/solution.py
+++ b/solution.py
@@ -375,10 +375,7 @@
         grad_ffn = dot_tn(ffn_in, d_gate_up).astype(bf16)
         grad_ffn = grad_ffn.reshape(shards, ring, pair, rows, -1).transpose(0, 2, 1, 3, 4)
         sum_ffn = scatter_spread(grad_ffn.reshape(width, -1), spread_ffn)
-        sum_ffn = sum_ffn.reshape(ring, rows, 2 * ff_own)
-        sum_ffn = lax.all_to_all(sum_ffn, "ring", split_axis=0, concat_axis=0, tiled=True)
-        sum_gate = back_line_columns(sum_ffn[:, :, :ff_own]).astype(f32)
-        sum_up = back_line_columns(sum_ffn[:, :, ff_own:]).astype(f32)
+        ffn_ready = sum_ffn
 
         sum_norm2 = jnp.sum(d_ffn_in * normed2, 0)
         d_resid = d_out + norm_back(normed2, inverse2, d_ffn_in * gain2)
@@ -434,9 +431,16 @@
         d_keys_raw = norm_back(keys_n, inverse_k, rotate(d_keys, cos_tab, -sin_tab))
         d_qkv = jnp.stack([d_queries_raw, d_keys_raw, d_values]).astype(bf16)
         d_qkv = d_qkv.transpose(2, 0, 1, 3).reshape(team_rows, 3 * own)
-        d_qkv, sum_ffn, sum_down = tie(d_qkv, sum_ffn, sum_down)
-        d_mix_in = ring_scatter(row_blocks(dot_nt(d_qkv, qkv_s).astype(bf16)))
-        sum_qkv = scatter_spread(dot_tn(mix_in, d_qkv).astype(bf16))
+        d_qkv, ffn_ready = tie(d_qkv, ffn_ready)
+        grad_qkv = dot_tn(mix_in, d_qkv).astype(bf16)
+        grad_qkv, d_mix_part = tie(grad_qkv, dot_nt(d_qkv, qkv_s).astype(bf16))
+        d_mix_in = ring_scatter(row_blocks(d_mix_part))
+        d_mix_in, ffn_ready = tie(d_mix_in, ffn_ready)
+        sum_ffn = ffn_ready.reshape(ring, rows, 2 * ff_own)
+        sum_ffn = lax.all_to_all(sum_ffn, "ring", split_axis=0, concat_axis=0, tiled=True)
+        sum_gate = back_line_columns(sum_ffn[:, :, :ff_own]).astype(f32)
+        sum_up = back_line_columns(sum_ffn[:, :, ff_own:]).astype(f32)
+        sum_qkv = scatter_spread(grad_qkv)
         sum_qkv = swap_team(sum_qkv.reshape(inner, rows, 3 * own)).reshape(inner, rows, 3, own)
         sum_qkv = sum_qkv.transpose(1, 2, 0, 3).reshape(rows, 3 * width).astype(f32)
 

time: 657 us -> 650 us (0.989)
  other arithmetic: 68.6 us -> 52.7 us
  waiting for transfers between devices: 276 us -> 287 us
    all_to_all x7, waiting for transfers between devices: 51.5 us -> 65.1 us  [swap_team(): return lax.all_to_all(x, team, split_axis=0, concat_axis=0, tiled=True)]
    ppermute x12, waiting for transfers between devices: 27 us -> 17.2 us  [small_sum(): x = x + lax.ppermute(x, axis, [(i, i ^ hop) for i in range(size)])]
    ppermute x6, waiting for transfers between devices: 49.4 us -> 40.7 us  [ring_gather(): now = lax.ppermute(now, 'ring', forward)]
    ppermute x8, waiting for transfers between devices: 15.7 us -> 24.3 us  [ring_scatter(): total = total + lax.ppermute(block_of(k, 1), 'pair', crossed).astype(f32)]
    ppermute x6, waiting for transfers between devices: 46.9 us -> 39.3 us  [line_scatter(): passed = lax.ppermute(total.astype(bf16), 'ring', forward)]
    ppermute x12, starting transfers between devices: 15.6 us -> 8.6 us  [small_sum(): x = x + lax.ppermute(x, axis, [(i, i ^ hop) for i in range(size)])]
    all_to_all x7, starting transfers between devices: 38.9 us -> 45.8 us  [swap_team(): return lax.all_to_all(x, team, split_axis=0, concat_axis=0, tiled=True)]
    all_to_all x1, waiting for transfers between devices: 0.01 us -> 6.59 us  [body(): lax.all_to_all(sum_ffn, 'ring', split_axis=0, concat_axis=0, tiled=True)]
  transfers between devices with their start and end apart: 74 -> 74, of which waited for: 45 -> 47; matrix products, arithmetic and copies ran while one was open for 32% -> 29% of each run, Pallas kernels for 0% -> 0%
where the time goes in v5:
time: 650 us; the launch traced here: 640 us
  waiting for transfers between devices  287 us (44%)
  starting transfers between devices  103 us (16%)
  matrix products  97.1 us (15%)
  local copies, waits for them, and re-layouts  70.7 us (11%)
  other arithmetic  52.7 us (8%)
  between operations  17.8 us (3%)
  blocking collectives  10.9 us (2%)
    all_to_all x7, waiting for transfers between devices, swap_team(): return lax.all_to_all(x, team, split_axis=0, concat_axis=0, tiled=True)  65.1 us
    all_to_all x7, starting transfers between devices, swap_team(): return lax.all_to_all(x, team, split_axis=0, concat_axis=0, tiled=True)  45.8 us
    ppermute x6, waiting for transfers between devices, ring_gather(): now = lax.ppermute(now, 'ring', forward)  40.7 us
    ppermute x6, waiting for transfers between devices, line_scatter(): passed = lax.ppermute(total.astype(bf16), 'ring', forward)  39.3 us
    ppermute x8, waiting for transfers between devices, ring_gather(): other = lax.ppermute(other, 'pair', crossed)  37.5 us
    unnamed x301, local copies, waits for them, and re-layouts  35 us
    dot_general x8, matrix products, dot_nt(): lax.dot_general(a, b, (((1,), (1,)), ((), ())), preferred_element_type=f32)  29.7 us
    ppermute x6, waiting for transfers between devices, line_gather(): parts.append(lax.ppermute(parts[-1], 'ring', forward))  29.5 us
  transfers between devices with their start and end apart: 74, of which 47 were waited for; matrix products, arithmetic and copies ran while one was open for 29% of the time, Pallas kernels for 0%

profile of v5, /device:TPU:0, one launch (start us, length us, event | category | flops | bytes accessed | tf_op | source)
XLA Modules:
  0.0 639.6 jit_solution(17879358024705391473)
XLA Ops:
  15.7 16.0 %all-to-all-start.1 = ((bf16[8,48,576]{2,1,0:T(8,128)(2,1)}), bf16[8,48,576]{2,1,0:T(8,128)(2,1)S(1)}, u32[]{:S(2)}, u32[]{:S(2)}) async-start(bf16[8,48,576]{2,1,0:T(8,128)(2,1)} %reshape.639), calls=%async_computation.1 | async-start | bytes 983040 | tf_op jit(solution)/shard_map/all_to_all | solution.py:95
  32.7 12.8 %all-to-all-done.1 = bf16[8,48,576]{2,1,0:T(8,128)(2,1)S(1)} async-done(((bf16[8,48,576]{2,1,0:T(8,128)(2,1)}), bf16[8,48,576]{2,1,0:T(8,128)(2,1)S(1)}, u32[]{:S(2)}, u32[]{:S(2)}) %all-to-all-start.1) | async-done | bytes 442400 | tf_op jit(solution)/shard_map/all_to_all | solution.py:95
  50.6 7.6 %all-to-all-done = bf16[8,32,512]{2,1,0:T(8,128)(2,1)S(1)} async-done(((bf16[8,32,512]{2,1,0:T(8,128)(2,1)}), bf16[8,32,512]{2,1,0:T(8,128)(2,1)S(1)}, u32[]{:S(2)}, u32[]{:S(2)}) %all-to-all-start) | async-done | bytes 262176 | tf_op jit(solution)/shard_map/all_to_all | solution.py:95
  87.2 15.3 %collective-permute-done.7 = bf16[128,1664]{1,0:T(8,128)(2,1)} collective-permute-done((bf16[128,1664]{1,0:T(8,128)(2,1)}, bf16[128,1664]{1,0:T(8,128)(2,1)}, u32[]{:S(2)}, u32[]{:S(2)}) %collective-permute-start.7) | collective-permute-done | bytes 426016 | tf_op jit(solution)/shard_map/ppermute | solution.py:112
  105.7 7.1 %collective-permute-done.9 = bf16[128,1664]{1,0:T(8,128)(2,1)} collective-permute-done((bf16[128,1664]{1,0:T(8,128)(2,1)}, bf16[128,1664]{1,0:T(8,128)(2,1)}, u32[]{:S(2)}, u32[]{:S(2)}) %collective-permute-start.9) | collective-permute-done | bytes 426016 | tf_op jit(solution)/shard_map/ppermute | solution.py:112
  117.1 8.0 %collective-permute-done.11 = bf16[128,1664]{1,0:T(8,128)(2,1)} collective-permute-done((bf16[128,1664]{1,0:T(8,128)(2,1)}, bf16[128,1664]{1,0:T(8,128)(2,1)}, u32[]{:S(2)}, u32[]{:S(2)}) %collective-permute-start.11) | collective-permute-done | bytes 426016 | tf_op jit(solution)/shard_map/ppermute | solution.py:112
  127.4 12.7 %collective-permute-done.12 = bf16[128,1664]{1,0:T(8,128)(2,1)} collective-permute-done((bf16[128,1664]{1,0:T(8,128)(2,1)}, bf16[128,1664]{1,0:T(8,128)(2,1)}, u32[]{:S(2)}, u32[]{:S(2)}) %collective-permute-start.12) | collective-permute-done | bytes 426016 | tf_op jit(solution)/shard_map/ppermute | solution.py:109
  171.9 4.5 fusion.150
  186.7 8.0 %all-to-all-done.2 = bf16[8,256,384]{1,2,0:T(8,128)(2,1)} async-done(((bf16[8,256,384]{1,2,0:T(8,128)(2,1)}), bf16[8,256,384]{1,2,0:T(8,128)(2,1)}, u32[]{:S(2)}, u32[]{:S(2)}) %all-to-all-start.2) | async-done | bytes 1572896 | tf_op jit(solution)/shard_map/all_to_all | solution.py:95
  201.7 8.0 %fusion.52 = (bf16[1024,3,64]{0,2,1:T(8,128)(2,1)S(1)}, f32[3,1024,64]{1,2,0:T(8,128)}) fusion(f32[3,1024,64]{1,2,0:T(8,128)S(1)} %fusion.56, f32[3]{0:T(128)S(1)} %copy-done.118, f32[1024,3]{0,1:T(4,128)S(1)} %bitcast.368, f32[3,1024,1024]{1,2,0:T(8,128)} %copy-done, f32[3,1024]{1,0:T(4,128)S(1)} %get-tuple-element.278, f32[3,3,1024,64]{2,3,1,0:T(8,128)S(1)} %bitcast.299), kind=kOutput, calls=%fused_computation.96 | convolution fusion | flops 412876800 | bytes 14975488 | tf_op jit(solution)/shard_map/hqk,hkd->hqd/dot_general | solution.py:76
  214.1 6.5 %collective-permute-done.17 = bf16[128,1536]{1,0:T(8,128)(2,1)} collective-permute-done((bf16[128,1536]{1,0:T(8,128)(2,1)}, bf16[128,1536]{1,0:T(8,128)(2,1)}, u32[]{:S(2)}, u32[]{:S(2)}) %collective-permute-start.17) | collective-permute-done | bytes 393248 | tf_op jit(solution)/shard_map/ppermute | solution.py:121
  224.4 7.4 %collective-permute-done.16 = bf16[128,1536]{1,0:T(8,128)(2,1)S(1)} collective-permute-done((bf16[128,1536]{1,0:T(8,128)(2,1)}, bf16[128,1536]{1,0:T(8,128)(2,1)S(1)}, u32[]{:S(2)}, u32[]{:S(2)}) %collective-permute-start.16) | collective-permute-done | bytes 393248 | tf_op jit(solution)/shard_map/ppermute | solution.py:121
  237.3 6.3 collective-permute-done.19
  245.8 12.2 %collective-permute-done.20 = bf16[128,1536]{1,0:T(8,128)(2,1)S(1)} collective-permute-done((bf16[128,1536]{1,0:T(8,128)(2,1)S(1)}, bf16[128,1536]{1,0:T(8,128)(2,1)S(1)}, u32[]{:S(2)}, u32[]{:S(2)}) %collective-permute-start.20) | collective-permute-done | bytes 393248 | tf_op jit(solution)/shard_map/ppermute | solution.py:125
  262.3 11.5 %collective-permute-done.21 = bf16[128,1536]{1,0:T(8,128)(2,1)S(1)} collective-permute-done((bf16[128,1536]{1,0:T(8,128)(2,1)S(1)}, bf16[128,1536]{1,0:T(8,128)(2,1)S(1)}, u32[]{:S(2)}, u32[]{:S(2)}) %collective-permute-start.21) | collective-permute-done | bytes 393248 | tf_op jit(solution)/shard_map/ppermute | solution.py:135
  273.8 7.4 %collective-permute-done.24 = bf16[128,1536]{1,0:T(8,128)(2,1)S(1)} collective-permute-done((bf16[128,1536]{1,0:T(8,128)(2,1)S(1)}, bf16[128,1536]{1,0:T(8,128)(2,1)S(1)}, u32[]{:S(2)}, u32[]{:S(2)}) %collective-permute-start.24) | collective-permute-done | bytes 393248 | tf_op jit(solution)/shard_map/ppermute | solution.py:135
  281.2 4.3 collective-permute-done.22
  285.5 5.4 collective-permute-done.25
  295.4 6.7 %fusion.63 = f32[512,2048]{1,0:T(8,128)} fusion(bf16[1536,2048]{1,0:T(8,128)(2,1)S(1)} %bitcast.305, bf16[128,1536]{1,0:T(8,128)(2,1)} %collective-permute-done.23, bf16[128,1536]{1,0:T(8,128)(2,1)} %collective-permute-done.22, bf16[128,1536]{1,0:T(8,128)(2,1)S(1)} %copy-done.130, bf16[128,1536]{1,0:T(8,128)(2,1)S(1)} %copy-done.70), kind=kOutput, calls=%fused_computation.157 | convolution fusion | flops 3227516928 | bytes 12058624 | tf_op jit(solution)/shard_map/dot_general | solution.py:64
  302.1 7.2 %multiply_convert_fusion.4 = (bf16[512,1024]{1,0:T(8,128)(2,1)S(1)}, bf16[512,1024]{1,0:T(8,128)(2,1)S(1)}, bf16[512,1024]{1,0:T(8,128)(2,1)}) fusion(f32[512,2048]{1,0:T(8,128)} %fusion.63, bf16[1024,1536]{1,0:T(8,128)(2,1)} %all-gather.20.cloned.1.call-done, bf16[128,1536]{1,0:T(8,128)(2,1)} %collective-permute-done.26, ...), kind=kOutput, calls=%fused_computation.40 | convolution fusion | flops 1626341376 | bytes 12064768 | tf_op jit(solution)/shard_map/dot_general | solution.py:72
  309.4 5.6 convolution_convert_fusion
  318.2 6.9 %convolution_convert_fusion.7 = bf16[512,1536]{1,0:T(8,128)(2,1)S(1)} fusion(bf16[1536,2048]{1,0:T(8,128)(2,1)} %bitcast.306, bf16[512,1024]{1,0:T(8,128)(2,1)} %copy-done.134, bf16[512,1024]{1,0:T(8,128)(2,1)} %copy-done.133), kind=kOutput, calls=%fused_computation.32 | convolution fusion | flops 3226206208 | bytes 9961472 | tf_op jit(solution)/shard_map/dot_general | solution.py:72
  325.3 9.6 %collective-permute-done.27 = bf16[128,1536]{1,0:T(8,128)(2,1)S(1)} collective-permute-done((bf16[128,1536]{1,0:T(8,128)(2,1)S(1)}, bf16[128,1536]{1,0:T(8,128)(2,1)S(1)}, u32[]{:S(2)}, u32[]{:S(2)}) %collective-permute-start.27) | collective-permute-done | bytes 393248 | tf_op jit(solution)/shard_map/ppermute | solution.py:147
  335.0 9.6 %collective-permute-done.28 = bf16[128,1536]{1,0:T(8,128)(2,1)S(1)} collective-permute-done((bf16[128,1536]{1,0:T(8,128)(2,1)S(1)}, bf16[128,1536]{1,0:T(8,128)(2,1)S(1)}, u32[]{:S(2)}, u32[]{:S(2)}) %collective-permute-start.28) | collective-permute-done | bytes 393248 | tf_op jit(solution)/shard_map/ppermute | solution.py:147
  344.9 9.6 %collective-permute-done.29 = bf16[128,1536]{1,0:T(8,128)(2,1)S(1)} collective-permute-done((bf16[128,1536]{1,0:T(8,128)(2,1)S(1)}, bf16[128,1536]{1,0:T(8,128)(2,1)S(1)}, u32[]{:S(2)}, u32[]{:S(2)}) %collective-permute-start.29) | collective-permute-done | bytes 393248 | tf_op jit(solution)/shard_map/ppermute | solution.py:147
  356.6 4.6 collective-permute-start.30
  361.2 5.0 collective-permute-done.31
  366.1 4.4 collective-permute-start.32
  370.6 8.6 %collective-permute-done.30 = bf16[128,1536]{1,0:T(8,128)(2,1)S(1)} collective-permute-done((bf16[128,1536]{1,0:T(8,128)(2,1)S(1)}, bf16[128,1536]{1,0:T(8,128)(2,1)S(1)}, u32[]{:S(2)}, u32[]{:S(2)}) %collective-permute-start.30) | collective-permute-done | bytes 393248 | tf_op jit(solution)/shard_map/ppermute | solution.py:109
  386.3 4.6 collective-permute-done.35
  391.8 12.4 %collective-permute-done.36 = bf16[128,1536]{1,0:T(8,128)(2,1)S(1)} collective-permute-done((bf16[128,1536]{1,0:T(8,128)(2,1)S(1)}, bf16[128,1536]{1,0:T(8,128)(2,1)S(1)}, u32[]{:S(2)}, u32[]{:S(2)}) %collective-permute-start.36) | collective-permute-done | bytes 393248 | tf_op jit(solution)/shard_map/ppermute | solution.py:109
  407.8 5.3 convolution_convert_fusion.4
  423.0 9.0 %all-to-all-start.4 = ((bf16[8,256,384]{1,2,0:T(8,128)(2,1)}), bf16[8,256,384]{1,2,0:T(8,128)(2,1)}, u32[]{:S(2)}, u32[]{:S(2)}) async-start(bf16[8,256,384]{1,2,0:T(8,128)(2,1)} %broadcast_in_dim.83), calls=%async_computation.5 | async-start | bytes 3145728 | tf_op jit(solution)/shard_map/all_to_all | solution.py:95
  432.1 6.3 multiply_convert_fusion
  458.3 17.1 %all-to-all-done.4 = bf16[8,256,384]{1,2,0:T(8,128)(2,1)} async-done(((bf16[8,256,384]{1,2,0:T(8,128)(2,1)}), bf16[8,256,384]{1,2,0:T(8,128)(2,1)}, u32[]{:S(2)}, u32[]{:S(2)}) %all-to-all-start.4) | async-done | bytes 1572896 | tf_op jit(solution)/shard_map/all_to_all | solution.py:95
  479.5 4.8 copy.325
  485.6 4.7 convolution_convert_fusion.2
  497.0 4.5 collective-permute-done.43
  501.7 5.5 collective-permute-done.38
  511.9 5.1 collective-permute-done.39
  550.7 5.7 all-gather.1
  559.7 4.9 all-to-all-start.5
  564.6 6.4 all-to-all-done.5
  582.1 7.0 %all-to-all-done.6 = bf16[8,32,512]{2,1,0:T(8,128)(2,1)S(1)} async-done(((bf16[8,32,512]{2,1,0:T(8,128)(2,1)}), bf16[8,32,512]{2,1,0:T(8,128)(2,1)S(1)}, u32[]{:S(2)}, u32[]{:S(2)}) %all-to-all-start.6) | async-done | bytes 262176 | tf_op jit(solution)/shard_map/all_to_all | solution.py:95
  594.6 5.2 all-gather.2
  604.4 6.6 %all-to-all-done.8 = bf16[4,48,2048]{2,1,0:T(8,128)(2,1)S(1)} async-done(((bf16[4,48,2048]{2,1,0:T(8,128)(2,1)}), bf16[4,48,2048]{2,1,0:T(8,128)(2,1)S(1)}, u32[]{:S(2)}, u32[]{:S(2)}) %all-to-all-start.8) | async-done | bytes 786464 | tf_op jit(solution)/shard_map/all_to_all | solution.py:440
  611.0 4.4 all-to-all-start.7
  622.4 6.4 all-to-all-done.7
  (602 shorter events, 257.7 us)
Async XLA Ops:
  7.2 51.8 %all-gather.10.cloned.1.call-start = ((), (), s32[]{:S(2)}) async-start(), calls=%async_computation.14 | async-start | bytes 1392640 | tf_op jit(solution)/shard_map/all_gather | solution.py:98
  9.0 134.3 %all-gather.12.cloned.1.call-start = ((), (), s32[]{:S(2)}) async-start(), calls=%async_computation.15 | async-start | bytes 1966080 | tf_op jit(solution)/shard_map/all_gather | solution.py:98
  9.8 152.7 %all-gather.16.cloned.1.call-start = ((), (), s32[]{:S(2)}) async-start(), calls=%async_computation.17 | async-start | bytes 4669440 | tf_op jit(solution)/shard_map/all_gather | solution.py:98
  15.7 29.7 %all-to-all-start.1 = ((bf16[8,48,576]{2,1,0:T(8,128)(2,1)}), bf16[8,48,576]{2,1,0:T(8,128)(2,1)S(1)}, u32[]{:S(2)}, u32[]{:S(2)}) async-start(bf16[8,48,576]{2,1,0:T(8,128)(2,1)} %reshape.639), calls=%async_computation.1 | async-start | bytes 983040 | tf_op jit(solution)/shard_map/all_to_all | solution.py:95
  45.5 12.7 %all-to-all-start = ((bf16[8,32,512]{2,1,0:T(8,128)(2,1)}), bf16[8,32,512]{2,1,0:T(8,128)(2,1)S(1)}, u32[]{:S(2)}, u32[]{:S(2)}) async-start(bf16[8,32,512]{2,1,0:T(8,128)(2,1)} %reshape.633), calls=%async_computation | async-start | bytes 524288 | tf_op jit(solution)/shard_map/all_to_all | solution.py:95
  49.1 122.8 %all-gather.14.cloned.1.call-start = ((), (), s32[]{:S(2)}) async-start(), calls=%async_computation.16 | async-start | bytes 2457600 | tf_op jit(solution)/shard_map/all_gather | solution.py:98
  75.4 39.6 %all-to-all-start.3 = ((bf16[4,48,2048]{2,1,0:T(8,128)(2,1)}), bf16[4,48,2048]{2,1,0:T(8,128)(2,1)}, u32[]{:S(2)}, u32[]{:S(2)}) async-start(bf16[4,48,2048]{2,1,0:T(8,128)(2,1)} %pad_maximum_fusion.7), calls=%async_computation.3 | async-start | bytes 1572864 | tf_op jit(solution)/shard_map/all_to_all | solution.py:294
  79.6 211.3 %all-gather.18.cloned.1.call-start = ((), (), s32[]{:S(2)}) async-start(), calls=%async_computation.18 | async-start | bytes 7077888 | tf_op jit(solution)/shard_map/all_gather | solution.py:98
  80.5 23.1 %collective-permute-start.6 = (bf16[128,1664]{1,0:T(8,128)(2,1)}, bf16[128,1664]{1,0:T(8,128)(2,1)}, u32[]{:S(2)}, u32[]{:S(2)}) collective-permute-start(bf16[128,1664]{1,0:T(8,128)(2,1)} %concatenate.87), channel_id=1, source_target_pairs={{0,1},{1,0},{2,3},{3,2},{4,5},{5,4},{6,7},{7,6},{8,9},{9,8},{10,11... | collective-permute-start | bytes 1277960 | tf_op jit(solution)/shard_map/ppermute | solution.py:109
  81.9 20.5 %collective-permute-start.7 = (bf16[128,1664]{1,0:T(8,128)(2,1)}, bf16[128,1664]{1,0:T(8,128)(2,1)}, u32[]{:S(2)}, u32[]{:S(2)}) collective-permute-start(bf16[128,1664]{1,0:T(8,128)(2,1)} %concatenate.87), channel_id=1, source_target_pairs={{0,2},{2,4},{4,6},{6,0},{1,3},{3,5},{5,7},{7,1},{8,10},{10,12},{12... | collective-permute-start | bytes 1277960 | tf_op jit(solution)/shard_map/ppermute | solution.py:112
  102.5 12.5 %collective-permute-start.8 = (bf16[128,1664]{1,0:T(8,128)(2,1)}, bf16[128,1664]{1,0:T(8,128)(2,1)}, u32[]{:S(2)}, u32[]{:S(2)}) collective-permute-start(bf16[128,1664]{1,0:T(8,128)(2,1)} %collective-permute-done.7), channel_id=1, source_target_pairs={{0,1},{1,0},{2,3},{3,2},{4,5},{5,4},{6,7},{7,6},{8,9},{9,8},{10,11... | collective-permute-start | bytes 1277960 | tf_op jit(solution)/shard_map/ppermute | solution.py:109
  102.5 10.3 %collective-permute-start.9 = (bf16[128,1664]{1,0:T(8,128)(2,1)}, bf16[128,1664]{1,0:T(8,128)(2,1)}, u32[]{:S(2)}, u32[]{:S(2)}) collective-permute-start(bf16[128,1664]{1,0:T(8,128)(2,1)} %collective-permute-done.7), channel_id=1, source_target_pairs={{0,2},{2,4},{4,6},{6,0},{1,3},{3,5},{5,7},{7,1},{8,10},{10,12},{12... | collective-permute-start | bytes 1277960 | tf_op jit(solution)/shard_map/ppermute | solution.py:112
  112.8 12.3 %collective-permute-start.10 = (bf16[128,1664]{1,0:T(8,128)(2,1)}, bf16[128,1664]{1,0:T(8,128)(2,1)}, u32[]{:S(2)}, u32[]{:S(2)}) collective-permute-start(bf16[128,1664]{1,0:T(8,128)(2,1)} %collective-permute-done.9), channel_id=1, source_target_pairs={{0,1},{1,0},{2,3},{3,2},{4,5},{5,4},{6,7},{7,6},{8,9},{9,8},{10,11... | collective-permute-start | bytes 1277960 | tf_op jit(solution)/shard_map/ppermute | solution.py:109
  114.8 10.2 %collective-permute-start.11 = (bf16[128,1664]{1,0:T(8,128)(2,1)}, bf16[128,1664]{1,0:T(8,128)(2,1)}, u32[]{:S(2)}, u32[]{:S(2)}) collective-permute-start(bf16[128,1664]{1,0:T(8,128)(2,1)} %collective-permute-done.9), channel_id=1, source_target_pairs={{0,2},{2,4},{4,6},{6,0},{1,3},{3,5},{5,7},{7,1},{8,10},{10,12},{12... | collective-permute-start | bytes 1277960 | tf_op jit(solution)/shard_map/ppermute | solution.py:112
  125.1 15.1 %collective-permute-start.12 = (bf16[128,1664]{1,0:T(8,128)(2,1)}, bf16[128,1664]{1,0:T(8,128)(2,1)}, u32[]{:S(2)}, u32[]{:S(2)}) collective-permute-start(bf16[128,1664]{1,0:T(8,128)(2,1)} %collective-permute-done.11), channel_id=1, source_target_pairs={{0,1},{1,0},{2,3},{3,2},{4,5},{5,4},{6,7},{7,6},{8,9},{9,8},{10,11... | collective-permute-start | bytes 1277960 | tf_op jit(solution)/shard_map/ppermute | solution.py:109
  167.3 27.4 %all-to-all-start.2 = ((bf16[8,256,384]{1,2,0:T(8,128)(2,1)}), bf16[8,256,384]{1,2,0:T(8,128)(2,1)}, u32[]{:S(2)}, u32[]{:S(2)}) async-start(bf16[8,256,384]{1,2,0:T(8,128)(2,1)} %bitcast.33), calls=%async_computation.2 | async-start | bytes 3145728 | tf_op jit(solution)/shard_map/all_to_all | solution.py:95
  171.6 130.5 %all-gather.20.cloned.1.call-start = ((), (), s32[]{:S(2)}) async-start(), calls=%async_computation.19 | async-start | bytes 3538944 | tf_op jit(solution)/shard_map/all_gather | solution.py:98
  213.3 271.1 %reduce-scatter.10.cloned.1.call-start = ((), (), s32[]{:S(2)}) async-start(), calls=%async_computation.20 | async-start | bytes 7077888 | tf_op jit(solution)/shard_map/reduce_scatter | solution.py:101
  213.4 18.4 %collective-permute-start.16 = (bf16[128,1536]{1,0:T(8,128)(2,1)}, bf16[128,1536]{1,0:T(8,128)(2,1)S(1)}, u32[]{:S(2)}, u32[]{:S(2)}) collective-permute-start(bf16[128,1536]{1,0:T(8,128)(2,1)} %get-tuple-element.234), channel_id=1, source_target_pairs={{0,1},{1,0},{2,3},{3,2},{4,5},{5,4},{6,7},{7,6},{8,9},{9,8},{10,11... | collective-permute-start | bytes 1179656 | tf_op jit(solution)/shard_map/ppermute | solution.py:121
  221.7 11.3 %collective-permute-start.18 = (bf16[128,1536]{1,0:T(8,128)(2,1)S(1)}, bf16[128,1536]{1,0:T(8,128)(2,1)S(1)}, u32[]{:S(2)}, u32[]{:S(2)}) collective-permute-start(bf16[128,1536]{1,0:T(8,128)(2,1)S(1)} %add_convert_fusion.10), channel_id=1, source_target_pairs={{0,2},{2,4},{4,6},{6,0},{1,3},{3,5},{5,7},{7,1},{8,10},{10,12},{12... | collective-permute-start | bytes 1179656 | tf_op jit(solution)/shard_map/ppermute | solution.py:125
  222.6 14.7 %collective-permute-start.15 = (bf16[128,1536]{1,0:T(8,128)(2,1)}, bf16[128,1536]{1,0:T(8,128)(2,1)S(1)}, u32[]{:S(2)}, u32[]{:S(2)}) collective-permute-start(bf16[128,1536]{1,0:T(8,128)(2,1)} %get-tuple-element.235), channel_id=1, source_target_pairs={{0,1},{1,0},{2,3},{3,2},{4,5},{5,4},{6,7},{7,6},{8,9},{9,8},{10,11... | collective-permute-start | bytes 1179656 | tf_op jit(solution)/shard_map/ppermute | solution.py:121
  233.2 10.4 %collective-permute-start.19 = (bf16[128,1536]{1,0:T(8,128)(2,1)S(1)}, bf16[128,1536]{1,0:T(8,128)(2,1)S(1)}, u32[]{:S(2)}, u32[]{:S(2)}) collective-permute-start(bf16[128,1536]{1,0:T(8,128)(2,1)S(1)} %add_convert_fusion.9), channel_id=1, source_target_pairs={{0,2},{2,4},{4,6},{6,0},{1,3},{3,5},{5,7},{7,1},{8,10},{10,12},{12... | collective-permute-start | bytes 1179656 | tf_op jit(solution)/shard_map/ppermute | solution.py:125
  234.1 11.7 %collective-permute-start.14 = (bf16[128,1536]{1,0:T(8,128)(2,1)}, bf16[128,1536]{1,0:T(8,128)(2,1)S(1)}, u32[]{:S(2)}, u32[]{:S(2)}) collective-permute-start(bf16[128,1536]{1,0:T(8,128)(2,1)} %get-tuple-element.232), channel_id=1, source_target_pairs={{0,1},{1,0},{2,3},{3,2},{4,5},{5,4},{6,7},{7,6},{8,9},{9,8},{10,11... | collective-permute-start | bytes 1179656 | tf_op jit(solution)/shard_map/ppermute | solution.py:121
  243.8 14.2 %collective-permute-start.20 = (bf16[128,1536]{1,0:T(8,128)(2,1)S(1)}, bf16[128,1536]{1,0:T(8,128)(2,1)S(1)}, u32[]{:S(2)}, u32[]{:S(2)}) collective-permute-start(bf16[128,1536]{1,0:T(8,128)(2,1)S(1)} %add_convert_fusion.8), channel_id=1, source_target_pairs={{0,2},{2,4},{4,6},{6,0},{1,3},{3,5},{5,7},{7,1},{8,10},{10,12},{12... | collective-permute-start | bytes 1179656 | tf_op jit(solution)/shard_map/ppermute | solution.py:125
  259.9 13.8 %collective-permute-start.21 = (bf16[128,1536]{1,0:T(8,128)(2,1)S(1)}, bf16[128,1536]{1,0:T(8,128)(2,1)S(1)}, u32[]{:S(2)}, u32[]{:S(2)}) collective-permute-start(bf16[128,1536]{1,0:T(8,128)(2,1)S(1)} %multiply_convert_fusion.8), channel_id=1, source_target_pairs={{0,2},{2,4},{4,6},{6,0},{1,3},{3,5},{5,7},{7,1},{8,10},{10,12},{12... | collective-permute-start | bytes 1179656 | tf_op jit(solution)/shard_map/ppermute | solution.py:135
  260.0 21.2 %collective-permute-start.24 = (bf16[128,1536]{1,0:T(8,128)(2,1)S(1)}, bf16[128,1536]{1,0:T(8,128)(2,1)S(1)}, u32[]{:S(2)}, u32[]{:S(2)}) collective-permute-start(bf16[128,1536]{1,0:T(8,128)(2,1)S(1)} %bitcast.345), channel_id=1, source_target_pairs={{0,2},{2,4},{4,6},{6,0},{1,3},{3,5},{5,7},{7,1},{8,10},{10,12},{12... | collective-permute-start | bytes 1179656 | tf_op jit(solution)/shard_map/ppermute | solution.py:135
  273.8 11.7 %collective-permute-start.22 = (bf16[128,1536]{1,0:T(8,128)(2,1)S(1)}, bf16[128,1536]{1,0:T(8,128)(2,1)}, u32[]{:S(2)}, u32[]{:S(2)}) collective-permute-start(bf16[128,1536]{1,0:T(8,128)(2,1)S(1)} %collective-permute-done.21), channel_id=1, source_target_pairs={{0,2},{2,4},{4,6},{6,0},{1,3},{3,5},{5,7},{7,1},{8,10},{10,12},{12... | collective-permute-start | bytes 1179656 | tf_op jit(solution)/shard_map/ppermute | solution.py:135
  290.8 11.3 %collective-permute-start.26 = (bf16[128,1536]{1,0:T(8,128)(2,1)}, bf16[128,1536]{1,0:T(8,128)(2,1)}, u32[]{:S(2)}, u32[]{:S(2)}) collective-permute-start(bf16[128,1536]{1,0:T(8,128)(2,1)} %collective-permute-done.25), channel_id=1, source_target_pairs={{0,2},{2,4},{4,6},{6,0},{1,3},{3,5},{5,7},{7,1},{8,10},{10,12},{12... | collective-permute-start | bytes 1179656 | tf_op jit(solution)/shard_map/ppermute | solution.py:135
  318.2 203.8 %reduce-scatter.12.cloned.1.call-start = ((), (), s32[]{:S(2)}) async-start(), calls=%async_computation.21 | async-start | bytes 737280 | tf_op jit(solution)/shard_map/reduce_scatter | solution.py:101
  356.6 22.6 %collective-permute-start.30 = (bf16[128,1536]{1,0:T(8,128)(2,1)S(1)}, bf16[128,1536]{1,0:T(8,128)(2,1)S(1)}, u32[]{:S(2)}, u32[]{:S(2)}) collective-permute-start(bf16[128,1536]{1,0:T(8,128)(2,1)S(1)} %get-tuple-element.216), channel_id=1, source_target_pairs={{0,1},{1,0},{2,3},{3,2},{4,5},{5,4},{6,7},{7,6},{8,9},{9,8},{10,11... | collective-permute-start | bytes 1179656 | tf_op jit(solution)/shard_map/ppermute | solution.py:109
  366.1 20.1 %collective-permute-start.32 = (bf16[128,1536]{1,0:T(8,128)(2,1)S(1)}, bf16[128,1536]{1,0:T(8,128)(2,1)S(1)}, u32[]{:S(2)}, u32[]{:S(2)}) collective-permute-start(bf16[128,1536]{1,0:T(8,128)(2,1)S(1)} %collective-permute-done.31), channel_id=1, source_target_pairs={{0,1},{1,0},{2,3},{3,2},{4,5},{5,4},{6,7},{7,6},{8,9},{9,8},{10,11... | collective-permute-start | bytes 1179656 | tf_op jit(solution)/shard_map/ppermute | solution.py:109
  380.1 11.6 %collective-permute-start.34 = (bf16[128,1536]{1,0:T(8,128)(2,1)S(1)}, bf16[128,1536]{1,0:T(8,128)(2,1)S(1)}, u32[]{:S(2)}, u32[]{:S(2)}) collective-permute-start(bf16[128,1536]{1,0:T(8,128)(2,1)S(1)} %collective-permute-done.33), channel_id=1, source_target_pairs={{0,1},{1,0},{2,3},{3,2},{4,5},{5,4},{6,7},{7,6},{8,9},{9,8},{10,11... | collective-permute-start | bytes 1179656 | tf_op jit(solution)/shard_map/ppermute | solution.py:109
  390.8 13.4 %collective-permute-start.36 = (bf16[128,1536]{1,0:T(8,128)(2,1)S(1)}, bf16[128,1536]{1,0:T(8,128)(2,1)S(1)}, u32[]{:S(2)}, u32[]{:S(2)}) collective-permute-start(bf16[128,1536]{1,0:T(8,128)(2,1)S(1)} %collective-permute-done.35), channel_id=1, source_target_pairs={{0,1},{1,0},{2,3},{3,2},{4,5},{5,4},{6,7},{7,6},{8,9},{9,8},{10,11... | collective-permute-start | bytes 1179656 | tf_op jit(solution)/shard_map/ppermute | solution.py:109
  405.9 135.9 %reduce-scatter.14.cloned.1.call-start = ((), (), s32[]{:S(2)}) async-start(), calls=%async_computation.22 | async-start | bytes 3538944 | tf_op jit(solution)/shard_map/reduce_scatter | solution.py:101
  423.0 52.3 %all-to-all-start.4 = ((bf16[8,256,384]{1,2,0:T(8,128)(2,1)}), bf16[8,256,384]{1,2,0:T(8,128)(2,1)}, u32[]{:S(2)}, u32[]{:S(2)}) async-start(bf16[8,256,384]{1,2,0:T(8,128)(2,1)} %broadcast_in_dim.83), calls=%async_computation.5 | async-start | bytes 3145728 | tf_op jit(solution)/shard_map/all_to_all | solution.py:95
  432.0 170.9 %reduce-scatter.18.cloned.1.call-start = ((), (), s32[]{:S(2)}) async-start(), calls=%async_computation.24 | async-start | bytes 3932160
  447.0 47.5 %collective-permute-start.37 = (bf16[128,1536]{1,0:T(8,128)(2,1)}, bf16[128,1536]{1,0:T(8,128)(2,1)}, u32[]{:S(2)}, u32[]{:S(2)}) collective-permute-start(bf16[128,1536]{1,0:T(8,128)(2,1)} %slice.324), channel_id=1, source_target_pairs={{0,2},{2,4},{4,6},{6,0},{1,3},{3,5},{5,7},{7,1},{8,10},{10,12},{12... | collective-permute-start | bytes 1179656 | tf_op jit(solution)/shard_map/ppermute | solution.py:147
  484.3 126.7 %reduce-scatter.16.cloned.1.call-start = ((), (), s32[]{:S(2)}) async-start(), calls=%async_computation.23 | async-start | bytes 2457600 | tf_op jit(solution)/shard_map/reduce_scatter | solution.py:101
  496.0 11.2 %collective-permute-start.38 = (bf16[128,1536]{1,0:T(8,128)(2,1)S(1)}, bf16[128,1536]{1,0:T(8,128)(2,1)S(1)}, u32[]{:S(2)}, u32[]{:S(2)}) collective-permute-start(bf16[128,1536]{1,0:T(8,128)(2,1)S(1)} %add_convert_fusion.5), channel_id=1, source_target_pairs={{0,2},{2,4},{4,6},{6,0},{1,3},{3,5},{5,7},{7,1},{8,10},{10,12},{12... | collective-permute-start | bytes 1179656 | tf_op jit(solution)/shard_map/ppermute | solution.py:147
  496.1 12.2 %collective-permute-start.42 = (bf16[128,1536]{1,0:T(8,128)(2,1)S(1)}, bf16[128,1536]{1,0:T(8,128)(2,1)S(1)}, u32[]{:S(2)}, u32[]{:S(2)}) collective-permute-start(bf16[128,1536]{1,0:T(8,128)(2,1)S(1)} %get-tuple-element.230), channel_id=1, source_target_pairs={{0,1},{1,0},{2,3},{3,2},{4,5},{5,4},{6,7},{7,6},{8,9},{9,8},{10,11... | collective-permute-start | bytes 1179656 | tf_op jit(solution)/shard_map/ppermute | solution.py:121
  507.4 13.2 %collective-permute-start.41 = (bf16[128,1536]{1,0:T(8,128)(2,1)S(1)}, bf16[128,1536]{1,0:T(8,128)(2,1)S(1)}, u32[]{:S(2)}, u32[]{:S(2)}) collective-permute-start(bf16[128,1536]{1,0:T(8,128)(2,1)S(1)} %get-tuple-element.231), channel_id=1, source_target_pairs={{0,1},{1,0},{2,3},{3,2},{4,5},{5,4},{6,7},{7,6},{8,9},{9,8},{10,11... | collective-permute-start | bytes 1179656 | tf_op jit(solution)/shard_map/ppermute | solution.py:121
  521.4 9.9 %collective-permute-start.46 = (bf16[128,1536]{1,0:T(8,128)(2,1)S(1)}, bf16[128,1536]{1,0:T(8,128)(2,1)}, u32[]{:S(2)}, u32[]{:S(2)}) collective-permute-start(bf16[128,1536]{1,0:T(8,128)(2,1)S(1)} %add_convert_fusion), channel_id=1, source_target_pairs={{0,2},{2,4},{4,6},{6,0},{1,3},{3,5},{5,7},{7,1},{8,10},{10,12},{12... | collective-permute-start | bytes 1179656 | tf_op jit(solution)/shard_map/ppermute | solution.py:125
  522.0 19.0 %collective-permute-start.53 = (bf16[48,1536]{1,0:T(8,128)(2,1)}, bf16[48,1536]{1,0:T(8,128)(2,1)S(1)}, u32[]{:S(2)}, u32[]{:S(2)}) collective-permute-start(bf16[48,1536]{1,0:T(8,128)(2,1)} %reduce-scatter.12.cloned.1.call-done), channel_id=1, source_target_pairs={{0,0},{8,1},{16,2},{24,3},{1,4},{9,5},{17,6},{25,7},{2,8},{10,9},{... | collective-permute-start | bytes 442376 | tf_op jit(solution)/shard_map/ppermute | solution.py:389
  524.7 10.2 %collective-permute-start.51 = (f32[37,128]{1,0:T(8,128)S(1)}, f32[37,128]{1,0:T(8,128)S(1)}, u32[]{:S(2)}, u32[]{:S(2)}) collective-permute-start(f32[37,128]{1,0:T(8,128)S(1)} %fusion.189), channel_id=1, source_target_pairs={{0,2},{2,0},{4,6},{6,4},{1,3},{3,1},{5,7},{7,5},{8,10},{10,8},{12,... | collective-permute-start | bytes 56840 | tf_op jit(solution)/shard_map/ppermute | solution.py:157
  559.7 11.3 %all-to-all-start.5 = ((f32[8,1,128]{2,1,0:T(1,128)}), f32[8,1,128]{2,1,0:T(1,128)S(1)}, u32[]{:S(2)}, u32[]{:S(2)}) async-start(f32[8,1,128]{2,1,0:T(1,128)} %reshape.710), calls=%async_computation.6 | async-start | bytes 8192 | tf_op jit(solution)/shard_map/all_to_all | solution.py:95
  577.2 11.9 %all-to-all-start.6 = ((bf16[8,32,512]{2,1,0:T(8,128)(2,1)}), bf16[8,32,512]{2,1,0:T(8,128)(2,1)S(1)}, u32[]{:S(2)}, u32[]{:S(2)}) async-start(bf16[8,32,512]{2,1,0:T(8,128)(2,1)} %bitcast.94), calls=%async_computation.7 | async-start | bytes 524288 | tf_op jit(solution)/shard_map/all_to_all | solution.py:95
  589.1 21.9 %all-to-all-start.8 = ((bf16[4,48,2048]{2,1,0:T(8,128)(2,1)}), bf16[4,48,2048]{2,1,0:T(8,128)(2,1)S(1)}, u32[]{:S(2)}, u32[]{:S(2)}) async-start(bf16[4,48,2048]{2,1,0:T(8,128)(2,1)} %bitcast.359), calls=%async_computation.10 | async-start | bytes 1572864 | tf_op jit(solution)/shard_map/all_to_all | solution.py:440
  611.0 17.7 %all-to-all-start.7 = ((bf16[8,48,576]{2,1,0:T(8,128)(2,1)}), bf16[8,48,576]{2,1,0:T(8,128)(2,1)}, u32[]{:S(2)}, u32[]{:S(2)}) async-start(bf16[8,48,576]{2,1,0:T(8,128)(2,1)} %bitcast.362), calls=%async_computation.8 | async-start | bytes 983040 | tf_op jit(solution)/shard_map/all_to_all | solution.py:95
  (164 other events, 1940.9 us)
Sparse Core Ops, SparseCore 0:
  10.2 19.7 all-gather.9
  31.6 19.6 all-gather.11
  52.8 31.8 all-gather.15
  86.7 21.8 all-gather.13
  115.1 60.1 all-gather.17
  213.4 39.5 all-gather.19
  318.3 85.8 reduce-scatter.9
  407.4 26.7 reduce-scatter.11
  438.0 49.8 reduce-scatter.13
  490.3 40.6 reduce-scatter.17
  550.1 30.0 reduce-scatter.15

commit v6 on v5

--- a/solution.py
+++ b/solution.py
@@ -368,7 +368,9 @@
             ],
             -1,
         )
-        d_ffn_in = line_scatter(dot_nt(d_gate_up, ffn_s).astype(bf16))
+        d_ffn_part = dot_nt(d_gate_up, ffn_s).astype(bf16)
+        d_ffn_part, d_gate_up = tie(d_ffn_part, d_gate_up)
+        d_ffn_in = line_scatter(d_ffn_part)
         d_out = cotangent[0].astype(f32)
         grad_down = dot_tn(hidden_b, d_ffn_b).astype(bf16)
         sum_down = scatter_spread(grad_down, spread_ffn).astype(f32)

time: 650 us -> 649 us (level)
  waiting for transfers between devices: 287 us -> 275 us
  starting transfers between devices: 103 us -> 113 us
    ppermute x12, starting transfers between devices: 8.6 us -> 26.8 us  [small_sum(): x = x + lax.ppermute(x, axis, [(i, i ^ hop) for i in range(size)])]
    all_to_all x7, waiting for transfers between devices: 65.1 us -> 48.2 us  [swap_team(): return lax.all_to_all(x, team, split_axis=0, concat_axis=0, tiled=True)]
    ppermute x8, waiting for transfers between devices: 37.5 us -> 46.2 us  [ring_gather(): other = lax.ppermute(other, 'pair', crossed)]
    ppermute x8, starting transfers between devices: 14.5 us -> 7.59 us  [ring_gather(): other = lax.ppermute(other, 'pair', crossed)]
    unnamed x301 -> x303, local copies, waits for them, and re-layouts: 35 us -> 34.5 us
  transfers between devices with their start and end apart: 74 -> 74, of which waited for: 47 -> 46; matrix products, arithmetic and copies ran while one was open for 29% -> 28% of each run, Pallas kernels for 0% -> 0%
where the time goes in v6:
time: 649 us; the launch traced here: 638 us
  waiting for transfers between devices  275 us (42%)
  starting transfers between devices  113 us (17%)
  matrix products  94.1 us (14%)
  local copies, waits for them, and re-layouts  71.2 us (11%)
  other arithmetic  55.6 us (9%)
  between operations  17.8 us (3%)
  blocking collectives  12.3 us (2%)
    all_to_all x7, waiting for transfers between devices, swap_team(): return lax.all_to_all(x, team, split_axis=0, concat_axis=0, tiled=True)  48.2 us
    ppermute x8, waiting for transfers between devices, ring_gather(): other = lax.ppermute(other, 'pair', crossed)  46.2 us
    all_to_all x7, starting transfers between devices, swap_team(): return lax.all_to_all(x, team, split_axis=0, concat_axis=0, tiled=True)  42 us
    ppermute x6, waiting for transfers between devices, ring_gather(): now = lax.ppermute(now, 'ring', forward)  39 us
    ppermute x6, waiting for transfers between devices, line_scatter(): passed = lax.ppermute(total.astype(bf16), 'ring', forward)  38.3 us
    unnamed x303, local copies, waits for them, and re-layouts  34.5 us
    ppermute x6, waiting for transfers between devices, line_gather(): parts.append(lax.ppermute(parts[-1], 'ring', forward))  29.6 us
    dot_general x11, matrix products, ein(): return jnp.einsum(spec, a, b, preferred_element_type=f32)  27.6 us
  transfers between devices with their start and end apart: 74, of which 46 were waited for; matrix products, arithmetic and copies ran while one was open for 28% of the time, Pallas kernels for 0%

profile of v6, /device:TPU:0, one launch (start us, length us, event | category | flops | bytes accessed | tf_op | source)
XLA Modules:
  0.0 638.3 jit_solution(7992893348865110998)
XLA Ops:
  15.8 16.0 %all-to-all-start.1 = ((bf16[8,48,576]{2,1,0:T(8,128)(2,1)}), bf16[8,48,576]{2,1,0:T(8,128)(2,1)S(1)}, u32[]{:S(2)}, u32[]{:S(2)}) async-start(bf16[8,48,576]{2,1,0:T(8,128)(2,1)} %reshape.639), calls=%async_computation.1 | async-start | bytes 983040 | tf_op jit(solution)/shard_map/all_to_all | solution.py:95
  32.7 12.8 %all-to-all-done.1 = bf16[8,48,576]{2,1,0:T(8,128)(2,1)S(1)} async-done(((bf16[8,48,576]{2,1,0:T(8,128)(2,1)}), bf16[8,48,576]{2,1,0:T(8,128)(2,1)S(1)}, u32[]{:S(2)}, u32[]{:S(2)}) %all-to-all-start.1) | async-done | bytes 442400 | tf_op jit(solution)/shard_map/all_to_all | solution.py:95
  50.6 7.6 %all-to-all-done = bf16[8,32,512]{2,1,0:T(8,128)(2,1)S(1)} async-done(((bf16[8,32,512]{2,1,0:T(8,128)(2,1)}), bf16[8,32,512]{2,1,0:T(8,128)(2,1)S(1)}, u32[]{:S(2)}, u32[]{:S(2)}) %all-to-all-start) | async-done | bytes 262176 | tf_op jit(solution)/shard_map/all_to_all | solution.py:95
  75.4 4.2 all-to-all-start.3
  87.2 15.3 %collective-permute-done.7 = bf16[128,1664]{1,0:T(8,128)(2,1)} collective-permute-done((bf16[128,1664]{1,0:T(8,128)(2,1)}, bf16[128,1664]{1,0:T(8,128)(2,1)}, u32[]{:S(2)}, u32[]{:S(2)}) %collective-permute-start.7) | collective-permute-done | bytes 426016 | tf_op jit(solution)/shard_map/ppermute | solution.py:112
  105.7 7.1 %collective-permute-done.9 = bf16[128,1664]{1,0:T(8,128)(2,1)} collective-permute-done((bf16[128,1664]{1,0:T(8,128)(2,1)}, bf16[128,1664]{1,0:T(8,128)(2,1)}, u32[]{:S(2)}, u32[]{:S(2)}) %collective-permute-start.9) | collective-permute-done | bytes 426016 | tf_op jit(solution)/shard_map/ppermute | solution.py:112
  117.1 8.0 %collective-permute-done.11 = bf16[128,1664]{1,0:T(8,128)(2,1)} collective-permute-done((bf16[128,1664]{1,0:T(8,128)(2,1)}, bf16[128,1664]{1,0:T(8,128)(2,1)}, u32[]{:S(2)}, u32[]{:S(2)}) %collective-permute-start.11) | collective-permute-done | bytes 426016 | tf_op jit(solution)/shard_map/ppermute | solution.py:112
  127.4 12.7 %collective-permute-done.12 = bf16[128,1664]{1,0:T(8,128)(2,1)} collective-permute-done((bf16[128,1664]{1,0:T(8,128)(2,1)}, bf16[128,1664]{1,0:T(8,128)(2,1)}, u32[]{:S(2)}, u32[]{:S(2)}) %collective-permute-start.12) | collective-permute-done | bytes 426016 | tf_op jit(solution)/shard_map/ppermute | solution.py:109
  167.2 4.3 all-to-all-start.2
  171.8 4.5 fusion.149
  186.7 7.9 %all-to-all-done.2 = bf16[8,256,384]{1,2,0:T(8,128)(2,1)} async-done(((bf16[8,256,384]{1,2,0:T(8,128)(2,1)}), bf16[8,256,384]{1,2,0:T(8,128)(2,1)}, u32[]{:S(2)}, u32[]{:S(2)}) %all-to-all-start.2) | async-done | bytes 1572896 | tf_op jit(solution)/shard_map/all_to_all | solution.py:95
  201.6 8.0 %fusion.52 = (bf16[1024,3,64]{0,2,1:T(8,128)(2,1)S(1)}, f32[3,1024,64]{1,2,0:T(8,128)}) fusion(f32[3,1024,64]{1,2,0:T(8,128)S(1)} %fusion.56, f32[3]{0:T(128)S(1)} %copy-done.119, f32[1024,3]{0,1:T(4,128)S(1)} %bitcast.371, f32[3,1024,1024]{1,2,0:T(8,128)} %copy-done, f32[3,1024]{1,0:T(4,128)S(1)} %get-tuple-element.282, f32[3,3,1024,64]{2,3,1,0:T(8,128)S(1)} %bitcast.300), kind=kOutput, calls=%fused_computation.96 | convolution fusion | flops 412876800 | bytes 14975488 | tf_op jit(solution)/shard_map/hqk,hkd->hqd/dot_general | solution.py:76
  214.0 6.5 %collective-permute-done.17 = bf16[128,1536]{1,0:T(8,128)(2,1)} collective-permute-done((bf16[128,1536]{1,0:T(8,128)(2,1)}, bf16[128,1536]{1,0:T(8,128)(2,1)}, u32[]{:S(2)}, u32[]{:S(2)}) %collective-permute-start.17) | collective-permute-done | bytes 393248 | tf_op jit(solution)/shard_map/ppermute | solution.py:121
  224.3 7.4 %collective-permute-done.16 = bf16[128,1536]{1,0:T(8,128)(2,1)S(1)} collective-permute-done((bf16[128,1536]{1,0:T(8,128)(2,1)}, bf16[128,1536]{1,0:T(8,128)(2,1)S(1)}, u32[]{:S(2)}, u32[]{:S(2)}) %collective-permute-start.16) | collective-permute-done | bytes 393248 | tf_op jit(solution)/shard_map/ppermute | solution.py:121
  237.2 6.3 collective-permute-done.19
  245.6 12.3 %collective-permute-done.20 = bf16[128,1536]{1,0:T(8,128)(2,1)S(1)} collective-permute-done((bf16[128,1536]{1,0:T(8,128)(2,1)S(1)}, bf16[128,1536]{1,0:T(8,128)(2,1)S(1)}, u32[]{:S(2)}, u32[]{:S(2)}) %collective-permute-start.20) | collective-permute-done | bytes 393248 | tf_op jit(solution)/shard_map/ppermute | solution.py:125
  262.1 11.6 %collective-permute-done.21 = bf16[128,1536]{1,0:T(8,128)(2,1)S(1)} collective-permute-done((bf16[128,1536]{1,0:T(8,128)(2,1)S(1)}, bf16[128,1536]{1,0:T(8,128)(2,1)S(1)}, u32[]{:S(2)}, u32[]{:S(2)}) %collective-permute-start.21) | collective-permute-done | bytes 393248 | tf_op jit(solution)/shard_map/ppermute | solution.py:135
  273.6 7.4 %collective-permute-done.24 = bf16[128,1536]{1,0:T(8,128)(2,1)S(1)} collective-permute-done((bf16[128,1536]{1,0:T(8,128)(2,1)S(1)}, bf16[128,1536]{1,0:T(8,128)(2,1)S(1)}, u32[]{:S(2)}, u32[]{:S(2)}) %collective-permute-start.24) | collective-permute-done | bytes 393248 | tf_op jit(solution)/shard_map/ppermute | solution.py:135
  281.0 4.3 collective-permute-done.22
  285.4 5.4 collective-permute-done.25
  295.2 6.8 %fusion.63 = f32[512,2048]{1,0:T(8,128)} fusion(bf16[1536,2048]{1,0:T(8,128)(2,1)S(1)} %bitcast.306, bf16[128,1536]{1,0:T(8,128)(2,1)} %collective-permute-done.23, bf16[128,1536]{1,0:T(8,128)(2,1)} %collective-permute-done.22, bf16[128,1536]{1,0:T(8,128)(2,1)S(1)} %copy-done.131, bf16[128,1536]{1,0:T(8,128)(2,1)S(1)} %copy-done.71), kind=kOutput, calls=%fused_computation.157 | convolution fusion | flops 3227516928 | bytes 12058624 | tf_op jit(solution)/shard_map/dot_general | solution.py:64
  302.1 7.2 %multiply_convert_fusion.4 = (bf16[512,1024]{1,0:T(8,128)(2,1)S(1)}, bf16[512,1024]{1,0:T(8,128)(2,1)S(1)}, bf16[512,1024]{1,0:T(8,128)(2,1)}) fusion(f32[512,2048]{1,0:T(8,128)} %fusion.63, bf16[1024,1536]{1,0:T(8,128)(2,1)} %all-gather.20.cloned.1.call-done, bf16[128,1536]{1,0:T(8,128)(2,1)} %collective-permute-done.26, ...), kind=kOutput, calls=%fused_computation.40 | convolution fusion | flops 1626341376 | bytes 12064768 | tf_op jit(solution)/shard_map/dot_general | solution.py:72
  309.5 4.6 convolution_convert_fusion.7
  314.2 4.8 convolution_convert_fusion
  323.5 10.0 %collective-permute-done.27 = bf16[128,1536]{1,0:T(8,128)(2,1)S(1)} collective-permute-done((bf16[128,1536]{1,0:T(8,128)(2,1)S(1)}, bf16[128,1536]{1,0:T(8,128)(2,1)S(1)}, u32[]{:S(2)}, u32[]{:S(2)}) %collective-permute-start.27) | collective-permute-done | bytes 393248 | tf_op jit(solution)/shard_map/ppermute | solution.py:147
  334.7 10.8 %collective-permute-done.28 = bf16[128,1536]{1,0:T(8,128)(2,1)S(1)} collective-permute-done((bf16[128,1536]{1,0:T(8,128)(2,1)S(1)}, bf16[128,1536]{1,0:T(8,128)(2,1)S(1)}, u32[]{:S(2)}, u32[]{:S(2)}) %collective-permute-start.28) | collective-permute-done | bytes 393248 | tf_op jit(solution)/shard_map/ppermute | solution.py:147
  346.7 11.0 %collective-permute-done.29 = bf16[128,1536]{1,0:T(8,128)(2,1)S(1)} collective-permute-done((bf16[128,1536]{1,0:T(8,128)(2,1)S(1)}, bf16[128,1536]{1,0:T(8,128)(2,1)S(1)}, u32[]{:S(2)}, u32[]{:S(2)}) %collective-permute-start.29) | collective-permute-done | bytes 393248 | tf_op jit(solution)/shard_map/ppermute | solution.py:147
  361.7 8.5 %collective-permute-done.31 = bf16[128,1536]{1,0:T(8,128)(2,1)S(1)} collective-permute-done((bf16[128,1536]{1,0:T(8,128)(2,1)S(1)}, bf16[128,1536]{1,0:T(8,128)(2,1)S(1)}, u32[]{:S(2)}, u32[]{:S(2)}) %collective-permute-start.31) | collective-permute-done | bytes 393248 | tf_op jit(solution)/shard_map/ppermute | solution.py:112
  371.2 9.9 %collective-permute-done.30 = bf16[128,1536]{1,0:T(8,128)(2,1)S(1)} collective-permute-done((bf16[128,1536]{1,0:T(8,128)(2,1)S(1)}, bf16[128,1536]{1,0:T(8,128)(2,1)S(1)}, u32[]{:S(2)}, u32[]{:S(2)}) %collective-permute-start.30) | collective-permute-done | bytes 393248 | tf_op jit(solution)/shard_map/ppermute | solution.py:109
  381.9 9.3 %collective-permute-done.32 = bf16[128,1536]{1,0:T(8,128)(2,1)S(1)} collective-permute-done((bf16[128,1536]{1,0:T(8,128)(2,1)S(1)}, bf16[128,1536]{1,0:T(8,128)(2,1)S(1)}, u32[]{:S(2)}, u32[]{:S(2)}) %collective-permute-start.32) | collective-permute-done | bytes 393248 | tf_op jit(solution)/shard_map/ppermute | solution.py:109
  395.6 11.7 %collective-permute-done.36 = bf16[128,1536]{1,0:T(8,128)(2,1)S(1)} collective-permute-done((bf16[128,1536]{1,0:T(8,128)(2,1)S(1)}, bf16[128,1536]{1,0:T(8,128)(2,1)S(1)}, u32[]{:S(2)}, u32[]{:S(2)}) %collective-permute-start.36) | collective-permute-done | bytes 393248 | tf_op jit(solution)/shard_map/ppermute | solution.py:109
  410.8 5.1 convolution_convert_fusion.4
  425.9 4.4 all-to-all-start.4
  430.4 6.3 multiply_convert_fusion
  460.8 4.7 copy.325
  466.7 4.6 convolution_convert_fusion.2
  480.2 5.2 collective-permute-done.43
  511.1 3.9 collective-permute-done.46
  522.3 9.9 %collective-permute-start.52 = (f32[37,128]{1,0:T(8,128)S(1)}, f32[37,128]{1,0:T(8,128)S(1)}, u32[]{:S(2)}, u32[]{:S(2)}) collective-permute-start(f32[37,128]{1,0:T(8,128)S(1)} %fusion.190), channel_id=1, source_target_pairs={{0,4},{2,6},{4,0},{6,2},{1,5},{3,7},{5,1},{7,3},{8,12},{10,14},{12... | collective-permute-start | bytes 56840 | tf_op jit(solution)/shard_map/ppermute | solution.py:157
  542.5 4.0 copy.323
  547.2 7.1 %all-gather.1 = f32[4,110,128]{2,1,0:T(8,128)S(1)} all-gather(f32[1,110,128]{2,1,0:T(8,128)S(1)} %maximum_bitcast_fusion), channel_id=2, replica_groups=mesh['clip'=4,'outer'=1,'ring'=4,'pair'=2] {'clip'}, dimensions={0}, use_global_device_ids=true | all-gather | bytes 281600 | tf_op jit(solution)/shard_map/all_gather | solution.py:462
  557.7 5.7 all-to-all-start.5
  563.4 6.4 all-to-all-done.5
  580.8 7.0 %all-to-all-done.6 = bf16[8,32,512]{2,1,0:T(8,128)(2,1)S(1)} async-done(((bf16[8,32,512]{2,1,0:T(8,128)(2,1)}), bf16[8,32,512]{2,1,0:T(8,128)(2,1)S(1)}, u32[]{:S(2)}, u32[]{:S(2)}) %all-to-all-start.6) | async-done | bytes 262176 | tf_op jit(solution)/shard_map/all_to_all | solution.py:95
  593.4 5.2 all-gather.2
  603.1 6.6 %all-to-all-done.8 = bf16[4,48,2048]{2,1,0:T(8,128)(2,1)S(1)} async-done(((bf16[4,48,2048]{2,1,0:T(8,128)(2,1)}), bf16[4,48,2048]{2,1,0:T(8,128)(2,1)S(1)}, u32[]{:S(2)}, u32[]{:S(2)}) %all-to-all-start.8) | async-done | bytes 786464 | tf_op jit(solution)/shard_map/all_to_all | solution.py:442
  609.7 4.4 all-to-all-start.7
  621.1 6.4 all-to-all-done.7
  (606 shorter events, 259.5 us)
Async XLA Ops:
  7.2 51.8 %all-gather.10.cloned.1.call-start = ((), (), s32[]{:S(2)}) async-start(), calls=%async_computation.14 | async-start | bytes 1392640 | tf_op jit(solution)/shard_map/all_gather | solution.py:98
  9.0 134.3 %all-gather.12.cloned.1.call-start = ((), (), s32[]{:S(2)}) async-start(), calls=%async_computation.15 | async-start | bytes 1966080 | tf_op jit(solution)/shard_map/all_gather | solution.py:98
  9.8 152.8 %all-gather.16.cloned.1.call-start = ((), (), s32[]{:S(2)}) async-start(), calls=%async_computation.17 | async-start | bytes 4669440 | tf_op jit(solution)/shard_map/all_gather | solution.py:98
  15.8 29.7 %all-to-all-start.1 = ((bf16[8,48,576]{2,1,0:T(8,128)(2,1)}), bf16[8,48,576]{2,1,0:T(8,128)(2,1)S(1)}, u32[]{:S(2)}, u32[]{:S(2)}) async-start(bf16[8,48,576]{2,1,0:T(8,128)(2,1)} %reshape.639), calls=%async_computation.1 | async-start | bytes 983040 | tf_op jit(solution)/shard_map/all_to_all | solution.py:95
  45.5 12.7 %all-to-all-start = ((bf16[8,32,512]{2,1,0:T(8,128)(2,1)}), bf16[8,32,512]{2,1,0:T(8,128)(2,1)S(1)}, u32[]{:S(2)}, u32[]{:S(2)}) async-start(bf16[8,32,512]{2,1,0:T(8,128)(2,1)} %reshape.633), calls=%async_computation | async-start | bytes 524288 | tf_op jit(solution)/shard_map/all_to_all | solution.py:95
  49.1 122.7 %all-gather.14.cloned.1.call-start = ((), (), s32[]{:S(2)}) async-start(), calls=%async_computation.16 | async-start | bytes 2457600 | tf_op jit(solution)/shard_map/all_gather | solution.py:98
  75.4 39.6 %all-to-all-start.3 = ((bf16[4,48,2048]{2,1,0:T(8,128)(2,1)}), bf16[4,48,2048]{2,1,0:T(8,128)(2,1)}, u32[]{:S(2)}, u32[]{:S(2)}) async-start(bf16[4,48,2048]{2,1,0:T(8,128)(2,1)} %pad_maximum_fusion.5), calls=%async_computation.3 | async-start | bytes 1572864 | tf_op jit(solution)/shard_map/all_to_all | solution.py:294
  79.6 211.1 %all-gather.18.cloned.1.call-start = ((), (), s32[]{:S(2)}) async-start(), calls=%async_computation.18 | async-start | bytes 7077888 | tf_op jit(solution)/shard_map/all_gather | solution.py:98
  80.5 23.1 %collective-permute-start.6 = (bf16[128,1664]{1,0:T(8,128)(2,1)}, bf16[128,1664]{1,0:T(8,128)(2,1)}, u32[]{:S(2)}, u32[]{:S(2)}) collective-permute-start(bf16[128,1664]{1,0:T(8,128)(2,1)} %concatenate.87), channel_id=1, source_target_pairs={{0,1},{1,0},{2,3},{3,2},{4,5},{5,4},{6,7},{7,6},{8,9},{9,8},{10,11... | collective-permute-start | bytes 1277960 | tf_op jit(solution)/shard_map/ppermute | solution.py:109
  81.9 20.5 %collective-permute-start.7 = (bf16[128,1664]{1,0:T(8,128)(2,1)}, bf16[128,1664]{1,0:T(8,128)(2,1)}, u32[]{:S(2)}, u32[]{:S(2)}) collective-permute-start(bf16[128,1664]{1,0:T(8,128)(2,1)} %concatenate.87), channel_id=1, source_target_pairs={{0,2},{2,4},{4,6},{6,0},{1,3},{3,5},{5,7},{7,1},{8,10},{10,12},{12... | collective-permute-start | bytes 1277960 | tf_op jit(solution)/shard_map/ppermute | solution.py:112
  102.5 12.6 %collective-permute-start.8 = (bf16[128,1664]{1,0:T(8,128)(2,1)}, bf16[128,1664]{1,0:T(8,128)(2,1)}, u32[]{:S(2)}, u32[]{:S(2)}) collective-permute-start(bf16[128,1664]{1,0:T(8,128)(2,1)} %collective-permute-done.7), channel_id=1, source_target_pairs={{0,1},{1,0},{2,3},{3,2},{4,5},{5,4},{6,7},{7,6},{8,9},{9,8},{10,11... | collective-permute-start | bytes 1277960 | tf_op jit(solution)/shard_map/ppermute | solution.py:109
  112.8 12.3 %collective-permute-start.10 = (bf16[128,1664]{1,0:T(8,128)(2,1)}, bf16[128,1664]{1,0:T(8,128)(2,1)}, u32[]{:S(2)}, u32[]{:S(2)}) collective-permute-start(bf16[128,1664]{1,0:T(8,128)(2,1)} %collective-permute-done.9), channel_id=1, source_target_pairs={{0,1},{1,0},{2,3},{3,2},{4,5},{5,4},{6,7},{7,6},{8,9},{9,8},{10,11... | collective-permute-start | bytes 1277960 | tf_op jit(solution)/shard_map/ppermute | solution.py:109
  125.1 15.1 %collective-permute-start.12 = (bf16[128,1664]{1,0:T(8,128)(2,1)}, bf16[128,1664]{1,0:T(8,128)(2,1)}, u32[]{:S(2)}, u32[]{:S(2)}) collective-permute-start(bf16[128,1664]{1,0:T(8,128)(2,1)} %collective-permute-done.11), channel_id=1, source_target_pairs={{0,1},{1,0},{2,3},{3,2},{4,5},{5,4},{6,7},{7,6},{8,9},{9,8},{10,11... | collective-permute-start | bytes 1277960 | tf_op jit(solution)/shard_map/ppermute | solution.py:109
  167.2 27.4 %all-to-all-start.2 = ((bf16[8,256,384]{1,2,0:T(8,128)(2,1)}), bf16[8,256,384]{1,2,0:T(8,128)(2,1)}, u32[]{:S(2)}, u32[]{:S(2)}) async-start(bf16[8,256,384]{1,2,0:T(8,128)(2,1)} %bitcast.33), calls=%async_computation.2 | async-start | bytes 3145728 | tf_op jit(solution)/shard_map/all_to_all | solution.py:95
  171.5 130.5 %all-gather.20.cloned.1.call-start = ((), (), s32[]{:S(2)}) async-start(), calls=%async_computation.19 | async-start | bytes 3538944 | tf_op jit(solution)/shard_map/all_gather | solution.py:98
  213.2 252.3 %reduce-scatter.10.cloned.1.call-start = ((), (), s32[]{:S(2)}) async-start(), calls=%async_computation.20 | async-start | bytes 7077888 | tf_op jit(solution)/shard_map/reduce_scatter | solution.py:101
  213.3 18.4 %collective-permute-start.16 = (bf16[128,1536]{1,0:T(8,128)(2,1)}, bf16[128,1536]{1,0:T(8,128)(2,1)S(1)}, u32[]{:S(2)}, u32[]{:S(2)}) collective-permute-start(bf16[128,1536]{1,0:T(8,128)(2,1)} %get-tuple-element.238), channel_id=1, source_target_pairs={{0,1},{1,0},{2,3},{3,2},{4,5},{5,4},{6,7},{7,6},{8,9},{9,8},{10,11... | collective-permute-start | bytes 1179656 | tf_op jit(solution)/shard_map/ppermute | solution.py:121
  221.6 11.3 %collective-permute-start.18 = (bf16[128,1536]{1,0:T(8,128)(2,1)S(1)}, bf16[128,1536]{1,0:T(8,128)(2,1)S(1)}, u32[]{:S(2)}, u32[]{:S(2)}) collective-permute-start(bf16[128,1536]{1,0:T(8,128)(2,1)S(1)} %add_convert_fusion.10), channel_id=1, source_target_pairs={{0,2},{2,4},{4,6},{6,0},{1,3},{3,5},{5,7},{7,1},{8,10},{10,12},{12... | collective-permute-start | bytes 1179656 | tf_op jit(solution)/shard_map/ppermute | solution.py:125
  222.5 14.7 %collective-permute-start.15 = (bf16[128,1536]{1,0:T(8,128)(2,1)}, bf16[128,1536]{1,0:T(8,128)(2,1)S(1)}, u32[]{:S(2)}, u32[]{:S(2)}) collective-permute-start(bf16[128,1536]{1,0:T(8,128)(2,1)} %get-tuple-element.239), channel_id=1, source_target_pairs={{0,1},{1,0},{2,3},{3,2},{4,5},{5,4},{6,7},{7,6},{8,9},{9,8},{10,11... | collective-permute-start | bytes 1179656 | tf_op jit(solution)/shard_map/ppermute | solution.py:121
  233.9 11.6 %collective-permute-start.14 = (bf16[128,1536]{1,0:T(8,128)(2,1)}, bf16[128,1536]{1,0:T(8,128)(2,1)S(1)}, u32[]{:S(2)}, u32[]{:S(2)}) collective-permute-start(bf16[128,1536]{1,0:T(8,128)(2,1)} %get-tuple-element.236), channel_id=1, source_target_pairs={{0,1},{1,0},{2,3},{3,2},{4,5},{5,4},{6,7},{7,6},{8,9},{9,8},{10,11... | collective-permute-start | bytes 1179656 | tf_op jit(solution)/shard_map/ppermute | solution.py:121
  243.6 14.2 %collective-permute-start.20 = (bf16[128,1536]{1,0:T(8,128)(2,1)S(1)}, bf16[128,1536]{1,0:T(8,128)(2,1)S(1)}, u32[]{:S(2)}, u32[]{:S(2)}) collective-permute-start(bf16[128,1536]{1,0:T(8,128)(2,1)S(1)} %add_convert_fusion.8), channel_id=1, source_target_pairs={{0,2},{2,4},{4,6},{6,0},{1,3},{3,5},{5,7},{7,1},{8,10},{10,12},{12... | collective-permute-start | bytes 1179656 | tf_op jit(solution)/shard_map/ppermute | solution.py:125
  259.8 13.8 %collective-permute-start.21 = (bf16[128,1536]{1,0:T(8,128)(2,1)S(1)}, bf16[128,1536]{1,0:T(8,128)(2,1)S(1)}, u32[]{:S(2)}, u32[]{:S(2)}) collective-permute-start(bf16[128,1536]{1,0:T(8,128)(2,1)S(1)} %multiply_convert_fusion.8), channel_id=1, source_target_pairs={{0,2},{2,4},{4,6},{6,0},{1,3},{3,5},{5,7},{7,1},{8,10},{10,12},{12... | collective-permute-start | bytes 1179656 | tf_op jit(solution)/shard_map/ppermute | solution.py:135
  259.9 21.2 %collective-permute-start.24 = (bf16[128,1536]{1,0:T(8,128)(2,1)S(1)}, bf16[128,1536]{1,0:T(8,128)(2,1)S(1)}, u32[]{:S(2)}, u32[]{:S(2)}) collective-permute-start(bf16[128,1536]{1,0:T(8,128)(2,1)S(1)} %bitcast.348), channel_id=1, source_target_pairs={{0,2},{2,4},{4,6},{6,0},{1,3},{3,5},{5,7},{7,1},{8,10},{10,12},{12... | collective-permute-start | bytes 1179656 | tf_op jit(solution)/shard_map/ppermute | solution.py:135
  273.6 11.7 %collective-permute-start.22 = (bf16[128,1536]{1,0:T(8,128)(2,1)S(1)}, bf16[128,1536]{1,0:T(8,128)(2,1)}, u32[]{:S(2)}, u32[]{:S(2)}) collective-permute-start(bf16[128,1536]{1,0:T(8,128)(2,1)S(1)} %collective-permute-done.21), channel_id=1, source_target_pairs={{0,2},{2,4},{4,6},{6,0},{1,3},{3,5},{5,7},{7,1},{8,10},{10,12},{12... | collective-permute-start | bytes 1179656 | tf_op jit(solution)/shard_map/ppermute | solution.py:135
  290.7 11.3 %collective-permute-start.26 = (bf16[128,1536]{1,0:T(8,128)(2,1)}, bf16[128,1536]{1,0:T(8,128)(2,1)}, u32[]{:S(2)}, u32[]{:S(2)}) collective-permute-start(bf16[128,1536]{1,0:T(8,128)(2,1)} %collective-permute-done.25), channel_id=1, source_target_pairs={{0,2},{2,4},{4,6},{6,0},{1,3},{3,5},{5,7},{7,1},{8,10},{10,12},{12... | collective-permute-start | bytes 1179656 | tf_op jit(solution)/shard_map/ppermute | solution.py:135
  322.2 183.6 %reduce-scatter.12.cloned.1.call-start = ((), (), s32[]{:S(2)}) async-start(), calls=%async_computation.21 | async-start | bytes 737280 | tf_op jit(solution)/shard_map/reduce_scatter | solution.py:101
  334.6 10.8 %collective-permute-start.28 = (bf16[128,1536]{1,0:T(8,128)(2,1)S(1)}, bf16[128,1536]{1,0:T(8,128)(2,1)S(1)}, u32[]{:S(2)}, u32[]{:S(2)}) collective-permute-start(bf16[128,1536]{1,0:T(8,128)(2,1)S(1)} %add_convert_fusion.7), channel_id=1, source_target_pairs={{0,2},{2,4},{4,6},{6,0},{1,3},{3,5},{5,7},{7,1},{8,10},{10,12},{12... | collective-permute-start | bytes 1179656 | tf_op jit(solution)/shard_map/ppermute | solution.py:147
  346.6 11.1 %collective-permute-start.29 = (bf16[128,1536]{1,0:T(8,128)(2,1)S(1)}, bf16[128,1536]{1,0:T(8,128)(2,1)S(1)}, u32[]{:S(2)}, u32[]{:S(2)}) collective-permute-start(bf16[128,1536]{1,0:T(8,128)(2,1)S(1)} %add_convert_fusion.6), channel_id=1, source_target_pairs={{0,2},{2,4},{4,6},{6,0},{1,3},{3,5},{5,7},{7,1},{8,10},{10,12},{12... | collective-permute-start | bytes 1179656 | tf_op jit(solution)/shard_map/ppermute | solution.py:147
  360.6 20.4 %collective-permute-start.30 = (bf16[128,1536]{1,0:T(8,128)(2,1)S(1)}, bf16[128,1536]{1,0:T(8,128)(2,1)S(1)}, u32[]{:S(2)}, u32[]{:S(2)}) collective-permute-start(bf16[128,1536]{1,0:T(8,128)(2,1)S(1)} %get-tuple-element.220), channel_id=1, source_target_pairs={{0,1},{1,0},{2,3},{3,2},{4,5},{5,4},{6,7},{7,6},{8,9},{9,8},{10,11... | collective-permute-start | bytes 1179656 | tf_op jit(solution)/shard_map/ppermute | solution.py:109
  370.1 21.1 %collective-permute-start.32 = (bf16[128,1536]{1,0:T(8,128)(2,1)S(1)}, bf16[128,1536]{1,0:T(8,128)(2,1)S(1)}, u32[]{:S(2)}, u32[]{:S(2)}) collective-permute-start(bf16[128,1536]{1,0:T(8,128)(2,1)S(1)} %collective-permute-done.31), channel_id=1, source_target_pairs={{0,1},{1,0},{2,3},{3,2},{4,5},{5,4},{6,7},{7,6},{8,9},{9,8},{10,11... | collective-permute-start | bytes 1179656 | tf_op jit(solution)/shard_map/ppermute | solution.py:109
  381.1 14.4 %collective-permute-start.34 = (bf16[128,1536]{1,0:T(8,128)(2,1)S(1)}, bf16[128,1536]{1,0:T(8,128)(2,1)S(1)}, u32[]{:S(2)}, u32[]{:S(2)}) collective-permute-start(bf16[128,1536]{1,0:T(8,128)(2,1)S(1)} %collective-permute-done.33), channel_id=1, source_target_pairs={{0,1},{1,0},{2,3},{3,2},{4,5},{5,4},{6,7},{7,6},{8,9},{9,8},{10,11... | collective-permute-start | bytes 1179656 | tf_op jit(solution)/shard_map/ppermute | solution.py:109
  391.5 15.7 %collective-permute-start.36 = (bf16[128,1536]{1,0:T(8,128)(2,1)S(1)}, bf16[128,1536]{1,0:T(8,128)(2,1)S(1)}, u32[]{:S(2)}, u32[]{:S(2)}) collective-permute-start(bf16[128,1536]{1,0:T(8,128)(2,1)S(1)} %collective-permute-done.35), channel_id=1, source_target_pairs={{0,1},{1,0},{2,3},{3,2},{4,5},{5,4},{6,7},{7,6},{8,9},{9,8},{10,11... | collective-permute-start | bytes 1179656 | tf_op jit(solution)/shard_map/ppermute | solution.py:109
  408.9 126.6 %reduce-scatter.14.cloned.1.call-start = ((), (), s32[]{:S(2)}) async-start(), calls=%async_computation.22 | async-start | bytes 3538944 | tf_op jit(solution)/shard_map/reduce_scatter | solution.py:101
  425.9 30.7 %all-to-all-start.4 = ((bf16[8,256,384]{1,2,0:T(8,128)(2,1)}), bf16[8,256,384]{1,2,0:T(8,128)(2,1)}, u32[]{:S(2)}, u32[]{:S(2)}) async-start(bf16[8,256,384]{1,2,0:T(8,128)(2,1)} %broadcast_in_dim.83), calls=%async_computation.5 | async-start | bytes 3145728 | tf_op jit(solution)/shard_map/all_to_all | solution.py:95
  430.3 171.3 %reduce-scatter.18.cloned.1.call-start = ((), (), s32[]{:S(2)}) async-start(), calls=%async_computation.24 | async-start | bytes 3932160
  445.3 31.1 %collective-permute-start.37 = (bf16[128,1536]{1,0:T(8,128)(2,1)}, bf16[128,1536]{1,0:T(8,128)(2,1)}, u32[]{:S(2)}, u32[]{:S(2)}) collective-permute-start(bf16[128,1536]{1,0:T(8,128)(2,1)} %slice.320), channel_id=1, source_target_pairs={{0,2},{2,4},{4,6},{6,0},{1,3},{3,5},{5,7},{7,1},{8,10},{10,12},{12... | collective-permute-start | bytes 1179656 | tf_op jit(solution)/shard_map/ppermute | solution.py:147
  465.5 144.2 %reduce-scatter.16.cloned.1.call-start = ((), (), s32[]{:S(2)}) async-start(), calls=%async_computation.23 | async-start | bytes 2457600 | tf_op jit(solution)/shard_map/reduce_scatter | solution.py:101
  477.5 11.6 %collective-permute-start.38 = (bf16[128,1536]{1,0:T(8,128)(2,1)S(1)}, bf16[128,1536]{1,0:T(8,128)(2,1)S(1)}, u32[]{:S(2)}, u32[]{:S(2)}) collective-permute-start(bf16[128,1536]{1,0:T(8,128)(2,1)S(1)} %add_convert_fusion.5), channel_id=1, source_target_pairs={{0,2},{2,4},{4,6},{6,0},{1,3},{3,5},{5,7},{7,1},{8,10},{10,12},{12... | collective-permute-start | bytes 1179656 | tf_op jit(solution)/shard_map/ppermute | solution.py:147
  479.0 14.9 %collective-permute-start.42 = (bf16[128,1536]{1,0:T(8,128)(2,1)S(1)}, bf16[128,1536]{1,0:T(8,128)(2,1)S(1)}, u32[]{:S(2)}, u32[]{:S(2)}) collective-permute-start(bf16[128,1536]{1,0:T(8,128)(2,1)S(1)} %get-tuple-element.234), channel_id=1, source_target_pairs={{0,1},{1,0},{2,3},{3,2},{4,5},{5,4},{6,7},{7,6},{8,9},{9,8},{10,11... | collective-permute-start | bytes 1179656 | tf_op jit(solution)/shard_map/ppermute | solution.py:121
  489.3 13.9 %collective-permute-start.41 = (bf16[128,1536]{1,0:T(8,128)(2,1)S(1)}, bf16[128,1536]{1,0:T(8,128)(2,1)S(1)}, u32[]{:S(2)}, u32[]{:S(2)}) collective-permute-start(bf16[128,1536]{1,0:T(8,128)(2,1)S(1)} %get-tuple-element.235), channel_id=1, source_target_pairs={{0,1},{1,0},{2,3},{3,2},{4,5},{5,4},{6,7},{7,6},{8,9},{9,8},{10,11... | collective-permute-start | bytes 1179656 | tf_op jit(solution)/shard_map/ppermute | solution.py:121
  505.8 29.0 %collective-permute-start.53 = (bf16[48,1536]{1,0:T(8,128)(2,1)}, bf16[48,1536]{1,0:T(8,128)(2,1)S(1)}, u32[]{:S(2)}, u32[]{:S(2)}) collective-permute-start(bf16[48,1536]{1,0:T(8,128)(2,1)} %reduce-scatter.12.cloned.1.call-done), channel_id=1, source_target_pairs={{0,0},{8,1},{16,2},{24,3},{1,4},{9,5},{17,6},{25,7},{2,8},{10,9},{... | collective-permute-start | bytes 442376 | tf_op jit(solution)/shard_map/ppermute | solution.py:391
  508.5 13.1 %collective-permute-start.51 = (f32[37,128]{1,0:T(8,128)S(1)}, f32[37,128]{1,0:T(8,128)S(1)}, u32[]{:S(2)}, u32[]{:S(2)}) collective-permute-start(f32[37,128]{1,0:T(8,128)S(1)} %fusion.189), channel_id=1, source_target_pairs={{0,2},{2,0},{4,6},{6,4},{1,3},{3,1},{5,7},{7,5},{8,10},{10,8},{12,... | collective-permute-start | bytes 56840 | tf_op jit(solution)/shard_map/ppermute | solution.py:157
  517.8 14.5 %collective-permute-start.47 = (f32[12,128]{1,0:T(8,128)S(1)}, f32[12,128]{1,0:T(8,128)S(1)}, u32[]{:S(2)}, u32[]{:S(2)}) collective-permute-start(f32[12,128]{1,0:T(8,128)S(1)} %bitcast.375), channel_id=1, source_target_pairs={{0,1},{1,0},{2,3},{3,2},{4,5},{5,4},{6,7},{7,6},{8,9},{9,8},{10,11... | collective-permute-start | bytes 18440 | tf_op jit(solution)/shard_map/ppermute | solution.py:157
  522.3 11.8 %collective-permute-start.52 = (f32[37,128]{1,0:T(8,128)S(1)}, f32[37,128]{1,0:T(8,128)S(1)}, u32[]{:S(2)}, u32[]{:S(2)}) collective-permute-start(f32[37,128]{1,0:T(8,128)S(1)} %fusion.190), channel_id=1, source_target_pairs={{0,4},{2,6},{4,0},{6,2},{1,5},{3,7},{5,1},{7,3},{8,12},{10,14},{12... | collective-permute-start | bytes 56840 | tf_op jit(solution)/shard_map/ppermute | solution.py:157
  557.7 12.1 %all-to-all-start.5 = ((f32[8,1,128]{2,1,0:T(1,128)}), f32[8,1,128]{2,1,0:T(1,128)S(1)}, u32[]{:S(2)}, u32[]{:S(2)}) async-start(f32[8,1,128]{2,1,0:T(1,128)} %reshape.710), calls=%async_computation.6 | async-start | bytes 8192 | tf_op jit(solution)/shard_map/all_to_all | solution.py:95
  575.9 11.9 %all-to-all-start.6 = ((bf16[8,32,512]{2,1,0:T(8,128)(2,1)}), bf16[8,32,512]{2,1,0:T(8,128)(2,1)S(1)}, u32[]{:S(2)}, u32[]{:S(2)}) async-start(bf16[8,32,512]{2,1,0:T(8,128)(2,1)} %bitcast.94), calls=%async_computation.7 | async-start | bytes 524288 | tf_op jit(solution)/shard_map/all_to_all | solution.py:95
  587.8 21.9 %all-to-all-start.8 = ((bf16[4,48,2048]{2,1,0:T(8,128)(2,1)}), bf16[4,48,2048]{2,1,0:T(8,128)(2,1)S(1)}, u32[]{:S(2)}, u32[]{:S(2)}) async-start(bf16[4,48,2048]{2,1,0:T(8,128)(2,1)} %bitcast.362), calls=%async_computation.10 | async-start | bytes 1572864 | tf_op jit(solution)/shard_map/all_to_all | solution.py:442
  609.7 17.7 %all-to-all-start.7 = ((bf16[8,48,576]{2,1,0:T(8,128)(2,1)}), bf16[8,48,576]{2,1,0:T(8,128)(2,1)}, u32[]{:S(2)}, u32[]{:S(2)}) async-start(bf16[8,48,576]{2,1,0:T(8,128)(2,1)} %bitcast.365), calls=%async_computation.8 | async-start | bytes 983040 | tf_op jit(solution)/shard_map/all_to_all | solution.py:95
  (165 other events, 2096.2 us)
Sparse Core Ops, SparseCore 0:
  10.2 19.7 all-gather.9
  31.6 19.6 all-gather.11
  52.8 31.8 all-gather.15
  86.7 21.8 all-gather.13
  115.1 60.1 all-gather.17
  213.3 39.5 all-gather.19
  322.3 87.1 reduce-scatter.9
  412.7 24.5 reduce-scatter.11
  441.0 51.9 reduce-scatter.13
  495.4 38.0 reduce-scatter.17
  546.6 33.2 reduce-scatter.15
